TPU v7x, 256 devices: a whole 4x4x8 slice. The times are simulated.
256 devices in a mesh: img: 32 (over y, x, core), txt: 8 (over z).
Axes of the slice: x: 4, y: 4, z: 8, core: 2. Of those that a mesh axis runs over, the one named last changes fastest.
Arguments:
- image_embed: bfloat16 [12288, 1280], P(('img', 'txt'))
- text_embed: bfloat16 [12288, 1280], P(('txt', 'img'))
- pair_col: int32 [12288], P('img'), may hold values from 0 to 12287, each once
- log_scale: float32 [], replicated, may hold values from 2.303 to 3.912
Outputs:
- row_loss: float32 [12288], P('img')
- col_loss: float32 [12288], P('txt')
- grad_image: float32 [12288, 1280], P(('img', 'txt'))
- grad_text: float32 [12288, 1280], P(('txt', 'img'))
- temp_grad: float32 [], replicated
Inputs may be any that keep to these rules, and one draw needn't show every extreme that they name: pair_col is a permutation of the 12288 text indices.
All inputs are finite; a program needn't handle non-finite values.
Results may differ from a plain program's by a relative error of at most 0.003.
Values may be sent and summed in bfloat16 or wider, within the bound.
No kernel may reach another device: no remote copies, remote signals or barrier semaphores. Data moves between devices by JAX's collectives and lax.ppermute only.
A program may use at most 64 MiB of HBM per device.

v0:
```python
import jax
import jax.numpy as jnp
from jax import lax
from jax.sharding import PartitionSpec as P


def local(image_embed, text_embed, pair_col, log_scale):
    img_all = lax.all_gather(image_embed, "txt", axis=0, tiled=True)
    txt_all = lax.all_gather(text_embed, "img", axis=0, tiled=True)
    scale = jnp.exp(log_scale)
    rows = img_all.shape[0]
    cols = txt_all.shape[0]
    batch_total = rows * lax.axis_size("img")
    col_start = lax.axis_index("txt") * cols
    col_ids = col_start + jnp.arange(cols, dtype=jnp.int32)
    hit = pair_col[:, None] == col_ids[None, :]
    logits = scale * lax.dot_general(
        img_all, txt_all, (((1,), (1,)), ((), ())), preferred_element_type=jnp.float32
    )
    paired = jnp.where(hit, logits, jnp.float32(0.0))
    row_part = jnp.sum(paired, axis=1)
    col_part = jnp.sum(paired, axis=0)
    row_max = lax.pmax(jnp.max(logits, axis=1), "txt")
    col_max = lax.pmax(jnp.max(logits, axis=0), "img")
    row_sum, row_pos = lax.psum(
        (jnp.sum(jnp.exp(logits - row_max[:, None]), axis=1), row_part), "txt"
    )
    col_sum, col_pos = lax.psum(
        (jnp.sum(jnp.exp(logits - col_max[None, :]), axis=0), col_part), "img"
    )
    row_lse = row_max + jnp.log(row_sum)
    col_lse = col_max + jnp.log(col_sum)
    row_loss = row_lse - row_pos
    col_loss = col_lse - col_pos
    grad_logits = 0.5 * (
        jnp.exp(logits - row_lse[:, None]) + jnp.exp(logits - col_lse[None, :])
    ) - hit.astype(jnp.float32)
    scaled_grad = (scale * grad_logits).astype(jnp.bfloat16)
    total = lax.psum(jnp.sum(grad_logits * logits), ("img", "txt"))
    temp_grad = total / batch_total
    image_term = jnp.dot(scaled_grad, txt_all, preferred_element_type=jnp.float32)
    grad_image = lax.psum_scatter(image_term, "txt", scatter_dimension=0, tiled=True)
    text_term = lax.dot_general(
        scaled_grad, img_all, (((0,), (0,)), ((), ())), preferred_element_type=jnp.float32
    )
    grad_text = lax.psum_scatter(text_term, "img", scatter_dimension=0, tiled=True)
    return (row_loss, col_loss, grad_image, grad_text, temp_grad)


def solution(mesh):
    in_specs = (P(("img", "txt"), None), P(("txt", "img"), None), P("img"), P())
    out_specs = (P("img"), P("txt"), P(("img", "txt"), None), P(("txt", "img"), None), P())
    return jax.shard_map(local, mesh=mesh, in_specs=in_specs, out_specs=out_specs, check_vma=False)
```

profile of v0, /device:TPU:1, one launch (start us, length us, event | category | flops | bytes accessed | tf_op | source)
XLA Modules:
  0.0 405.0 jit_solution(8623059091231567019)
XLA Ops:
  7.2 0.0 all-gather.2.cloned.1.call-start
  7.2 0.7 all-gather.2.cloned.1.call-update
  7.9 0.0 reduce-scatter.3.cloned.1.call-start
  8.6 25.7 %all_gather.6 = bf16[384,1280]{1,0:T(8,128)(2,1)S(1)} all-gather(bf16[48,1280]{1,0:T(8,128)(2,1)} %param.4), channel_id=1, replica_groups=mesh['img'=32,'txt'=8] {'txt'}, dimensions={0}, use_global_device_ids=true | all-gather | bytes 1105920 | tf_op jit(solution)/shard_map/all_gather | solution.py:8
  34.3 31.2 %all-gather.2.cloned.1.call-done = bf16[1536,1280]{1,0:T(8,128)(2,1)} async-done(((bf16[48,1280]{1,0:T(8,128)(2,1)}), bf16[1536,1280]{1,0:T(8,128)(2,1)}) %all-gather.2.cloned.1.call-update) | async-done | bytes 3932176 | tf_op jit(solution)/shard_map/all_gather | solution.py:9
  65.6 3.9 fusion.5
  69.5 0.0 copy-start
  69.5 63.3 %pmax.15 = f32[1536]{0:T(1024)S(1)} all-reduce(f32[1536]{0:T(1024)S(1)} %get-tuple-element.10), channel_id=1, replica_groups=mesh['img'=32,'txt'=8] {'img'}, use_global_device_ids=true, to_apply=%region_7.8 | all-reduce | flops 1536 | bytes 12288 | tf_op jit(solution)/shard_map/pmax | solution.py:24
  132.8 13.9 %pmax.14 = f32[384]{0:T(512)S(1)} all-reduce(f32[384]{0:T(512)S(1)} %get-tuple-element.11), channel_id=1, replica_groups=mesh['img'=32,'txt'=8] {'txt'}, use_global_device_ids=true, to_apply=%region_1.2 | all-reduce | flops 384 | bytes 3072 | tf_op jit(solution)/shard_map/pmax | solution.py:23
  146.7 0.7 exponential_reduce_fusion
  147.4 69.8 %psum.37 = f32[1536]{0:T(1024)S(1)} all-reduce(f32[1536]{0:T(1024)S(1)} %get-tuple-element.8), channel_id=1, replica_groups=mesh['img'=32,'txt'=8] {'img'}, use_global_device_ids=true, to_apply=%region_9.10 | all-reduce | flops 1536 | bytes 12288 | tf_op jit(solution)/shard_map/psum | solution.py:28
  217.2 11.3 %psum.35 = f32[384]{0:T(512)S(1)} all-reduce(f32[384]{0:T(512)S(1)} %get-tuple-element.9), channel_id=1, replica_groups=mesh['img'=32,'txt'=8] {'txt'}, use_global_device_ids=true, to_apply=%region_3.4 | all-reduce | flops 384 | bytes 3072 | tf_op jit(solution)/shard_map/psum | solution.py:25
  228.5 0.0 copy-done
  228.5 5.9 %fusion.4 = f32[384,1280]{1,0:T(8,128)} fusion(bf16[1536,1280]{1,0:T(8,128)(2,1)} %all-gather.2.cloned.1.call-done, f32[384,1536]{1,0:T(8,128)S(1)} %get-tuple-element.12, f32[1536]{0:T(1024)S(1)} %log_add_fusion, f32[384]{0:T(512)S(1)} %log_add_fusion.1, s32[1536]{0:T(1024)S(1)} %iota_add_fusion, f32[]{:T(128)S(6)} %exp.15, s32[384]{0:T(512)S(1)} %copy-done), kind=kOutput, calls=%fused_computation.14 | convolution fusion | flops 1515257856 | bytes 8272900 | tf_op jit(solution)/shard_map/dot_general | solution.py:41
  234.4 0.0 reduce-scatter.3.cloned.1.call-update
  234.4 0.0 reduce-scatter.5.cloned.1.call-start
  234.4 5.9 %fusion.3 = f32[1536,1280]{1,0:T(8,128)} fusion(bf16[384,1280]{1,0:T(8,128)(2,1)S(1)} %all_gather.6, f32[384,1536]{1,0:T(8,128)S(1)} %get-tuple-element.12, f32[1536]{0:T(1024)S(1)} %log_add_fusion, f32[384]{0:T(512)S(1)} %log_add_fusion.1, s32[1536]{0:T(1024)S(1)} %iota_add_fusion, f32[]{:T(128)S(6)} %exp.15, s32[384]{0:T(512)S(1)} %copy-done), kind=kOutput, calls=%fused_computation.13 | convolution fusion | flops 1515257856 | bytes 11222020 | tf_op jit(solution)/shard_map/dot_general | solution.py:43
  240.3 0.0 reduce-scatter.5.cloned.1.call-update
  240.3 2.2 multiply_reduce_fusion
  242.6 75.3 %psum.39 = f32[]{:T(128)} all-reduce(f32[]{:T(128)} %get-tuple-element.5), channel_id=1, replica_groups=mesh['img'=32,'txt'=8] {'img','txt'}, use_global_device_ids=true, to_apply=%region_15.16 | all-reduce | flops 1 | bytes 8 | tf_op jit(solution)/shard_map/psum | solution.py:39
  317.9 64.6 %psum.38 = f32[1536]{0:T(1024)S(1)} all-reduce(f32[1536]{0:T(1024)S(1)} %get-tuple-element.6), channel_id=1, replica_groups=mesh['img'=32,'txt'=8] {'img'}, use_global_device_ids=true, to_apply=%region_11.12 | all-reduce | flops 1536 | bytes 12288 | tf_op jit(solution)/shard_map/psum | solution.py:28
  382.4 0.6 sub.46
  383.0 13.0 %psum.36 = f32[384]{0:T(512)S(1)} all-reduce(f32[384]{0:T(512)S(1)} %get-tuple-element.7), channel_id=1, replica_groups=mesh['img'=32,'txt'=8] {'txt'}, use_global_device_ids=true, to_apply=%region_5.6 | all-reduce | flops 384 | bytes 3072 | tf_op jit(solution)/shard_map/psum | solution.py:25
  396.0 0.6 sub.43
  397.3 0.0 reduce-scatter.3.cloned.1.call-done
  397.3 0.0 reduce-scatter.5.cloned.1.call-done
  (3 shorter events, 0.0 us)
Async XLA Ops:
  7.2 58.4 %all-gather.2.cloned.1.call-start = ((), (), s32[]{:S(2)}) async-start(), calls=%async_computation.2 | async-start | bytes 4055040 | tf_op jit(solution)/shard_map/all_gather | solution.py:9
  7.9 389.4 %reduce-scatter.3.cloned.1.call-start = ((), (), s32[]{:S(2)}) async-start(), calls=%async_computation.3 | async-start | bytes 2211840 | tf_op jit(solution)/shard_map/reduce_scatter | solution.py:42
  69.5 159.0 %copy-start = (s32[384]{0:T(512)S(1)}, s32[384]{0:T(512)}, u32[]{:S(2)}) copy-start(s32[384]{0:T(512)} %param.6) | copy-start | bytes 4612
  234.4 162.9 %reduce-scatter.5.cloned.1.call-start = ((), (), s32[]{:S(2)}) async-start(), calls=%async_computation.4 | async-start | bytes 8110080 | tf_op jit(solution)/shard_map/reduce_scatter | solution.py:46
Sparse Core Ops, SparseCore 0:
  10.5 54.9 all-gather.1
  234.5 35.1 reduce-scatter.2
  274.9 99.5 reduce-scatter.4
where the time goes:
time: 409 us; the launch traced here: 405 us
  blocking collectives  337 us (82%)
  waiting for transfers between devices  32 us (8%)
  between operations  16.3 us (4%)
  matrix products  15.6 us (4%)
  other arithmetic  4.19 us (1%)
    psum x2, blocking collectives, local(): lax.psum((jnp.sum(jnp.exp(logits - col_max[None, :]), axis=0), col_part),...  134 us
    psum x1, blocking collectives, local(): total = lax.psum(jnp.sum(grad_logits * logits), ('img', 'txt'))  75.3 us
    pmax x1, blocking collectives, local(): col_max = lax.pmax(jnp.max(logits, axis=0), 'img')  63.3 us
    all_gather x1, waiting for transfers between devices, local(): txt_all = lax.all_gather(text_embed, 'img', axis=0, tiled=True)  31.2 us
    all_gather x1, blocking collectives, local(): img_all = lax.all_gather(image_embed, 'txt', axis=0, tiled=True)  25.7 us
    psum x2, blocking collectives, local(): lax.psum((jnp.sum(jnp.exp(logits - row_max[:, None]), axis=1), row_part),...  24.2 us
    pmax x1, blocking collectives, local(): row_max = lax.pmax(jnp.max(logits, axis=1), 'txt')  13.9 us
  transfers between devices with their start and end apart: 3, of which 1 were waited for; matrix products, arithmetic and copies ran while one was open for 2% of the time, Pallas kernels for 0%

commit v1 on v0

v1 whole, which is shorter than its diff:
```python
import jax
import jax.numpy as jnp
from jax import lax
from jax.sharding import Mesh, PartitionSpec as P

NY, NX, NC = 4, 4, 2
XY = ("y", "x")
CZ = ("c", "z")
SWAP = [(0, 1), (1, 0)]


def merge(lse, mean):
    top = jnp.max(lse, axis=0)
    weight = jnp.exp(lse - top)
    total = jnp.sum(weight, axis=0)
    return top + jnp.log(total), jnp.sum(weight * mean, axis=0) / total


def local(image_embed, text_embed, pair_col, log_scale):
    part, embed = image_embed.shape
    peers = NY * NX
    nz = lax.axis_size("z")
    c = lax.axis_index("c")
    z = lax.axis_index("z")
    scale = jnp.exp(log_scale)

    img = lax.all_gather(image_embed, CZ, axis=0, tiled=True)
    txt = lax.all_to_all(jnp.broadcast_to(text_embed[None], (peers, part, embed)), XY, 0, 0)
    txt = txt.reshape(peers * part, embed)
    rows, cols = img.shape[0], txt.shape[0]
    pairs = lax.all_gather(pair_col, "c", axis=0, tiled=True)
    k = jnp.arange(cols, dtype=jnp.int32)
    col_ids = z * (peers * NC * part) + (2 * (k // part) + c) * part + k % part
    hit = pairs[:, None] == col_ids[None, :]

    logits = scale * lax.dot_general(
        img, txt, (((1,), (1,)), ((), ())), preferred_element_type=jnp.float32
    )
    paired = jnp.where(hit, logits, jnp.float32(0.0))
    row_part = jnp.sum(paired, axis=1)
    col_part = jnp.sum(paired, axis=0)
    row_top = jnp.max(logits, axis=1)
    col_top = jnp.max(logits, axis=0)
    row_exp = jnp.exp(logits - row_top[:, None])
    col_exp = jnp.exp(logits - col_top[None, :])
    row_sum = jnp.sum(row_exp, axis=1)
    col_sum = jnp.sum(col_exp, axis=0)
    row_mean = jnp.sum(row_exp * logits, axis=1) / row_sum
    col_mean = jnp.sum(col_exp * logits, axis=0) / col_sum

    def exchange(axes, n, *stats):
        flat = jnp.concatenate(stats)
        size = flat.shape[0]
        pad = -size % 1024
        flat = jnp.pad(flat, (0, pad)).reshape(-1, 128)
        got = lax.all_to_all(jnp.broadcast_to(flat[None], (n,) + flat.shape), axes, 0, 0)
        return got.reshape(n, -1)

    got = exchange(CZ, NC * nz, row_top + jnp.log(row_sum), row_mean, row_part)
    row_lse, row_mean = merge(got[:, :rows], got[:, rows : 2 * rows])
    row_pos = jnp.sum(got[:, 2 * rows : 3 * rows], axis=0)
    row_total = 0.5 * jnp.sum(row_mean) - jnp.sum(row_pos)
    got = exchange(XY, peers, col_top + jnp.log(col_sum), col_mean, col_part, row_total[None])
    col_lse, col_mean = merge(got[:, :cols], got[:, cols : 2 * cols])
    col_pos = jnp.sum(got[:, 2 * cols : 3 * cols], axis=0)
    row_total = jnp.sum(got[:, 3 * cols])
    col_total = 0.5 * jnp.sum(col_mean)

    own = rows // NC
    row_loss = lax.dynamic_slice(row_lse - row_pos, (c * own,), (own,))
    col_loss = (col_lse - col_pos).reshape(peers, 1, part)
    other = lax.ppermute(col_loss, "c", SWAP)
    col_loss = jnp.where(
        c == 0, jnp.concatenate([col_loss, other], 1), jnp.concatenate([other, col_loss], 1)
    ).reshape(-1)

    grad_logits = 0.5 * (
        jnp.exp(logits - row_lse[:, None]) + jnp.exp(logits - col_lse[None, :])
    ) - hit.astype(jnp.float32)
    scaled_grad = (scale * grad_logits).astype(jnp.bfloat16)

    image_term = jnp.dot(scaled_grad, txt, preferred_element_type=jnp.float32)
    image_term = image_term.reshape(NC, nz, part, embed)
    keep = lax.dynamic_index_in_dim(image_term, c, 0, keepdims=False)
    send = lax.dynamic_index_in_dim(image_term, 1 - c, 0, keepdims=False).astype(jnp.bfloat16)
    both = keep + lax.ppermute(send, "c", SWAP).astype(jnp.float32)
    col_total = col_total + lax.ppermute(col_total[None], "c", SWAP)[0]
    extra = jnp.broadcast_to(col_total, (nz, 8, embed))
    both = jnp.concatenate([both, extra], axis=1)
    image_sum = lax.psum_scatter(both, "z", scatter_dimension=0, tiled=False)
    grad_image = image_sum[:part]

    text_term = lax.dot_general(
        scaled_grad, img, (((0,), (0,)), ((), ())), preferred_element_type=jnp.float32
    )
    text_term = text_term.astype(jnp.bfloat16).reshape(peers, part, embed)
    text_term = lax.all_to_all(text_term, XY, 0, 0)
    grad_text = jnp.sum(text_term.astype(jnp.float32), axis=0)

    temp_grad = (row_total + image_sum[part, 0]) / (rows * peers)
    return (row_loss, col_loss, grad_image, grad_text, temp_grad)


def solution(mesh):
    nz = mesh.shape["txt"]
    grid = Mesh(mesh.devices.reshape(NY, NX, NC, nz), ("y", "x", "c", "z"))
    images, texts = ("y", "x", "c", "z"), ("z", "y", "x", "c")
    in_specs = (P(images, None), P(texts, None), P(("y", "x", "c")), P())
    out_specs = (P(("y", "x", "c")), P("z"), P(images, None), P(texts, None), P())
    return jax.shard_map(local, mesh=grid, in_specs=in_specs, out_specs=out_specs, check_vma=False)
```

time: 409 us -> 157 us (0.38)
  blocking collectives: 337 us -> 15.3 us
  waiting for transfers between devices: 32 us -> 68.6 us
  starting transfers between devices: 0.12 us -> 22.2 us
  local copies, waits for them, and re-layouts: 0.01 us -> 11.7 us
  matrix products: 15.6 us -> 8.66 us
  other arithmetic: 4.19 us -> 9.56 us
    psum x5 -> x0, blocking collectives: 234 us -> none  [the longest x2 134 us: local(): lax.psum((jnp.sum(jnp.exp(logits - col_max[None, :]), axis=0), col_part),...]
    pmax x2 -> x0, blocking collectives: 77.1 us -> none  [the longest x1 63.3 us: local(): col_max = lax.pmax(jnp.max(logits, axis=0), 'img')]
    all_to_all x0 -> x3, waiting for transfers between devices: none -> 60.8 us  [the longest x1 28.2 us: local(): text_term = lax.all_to_all(text_term, XY, 0, 0)]
    all_gather x1, waiting for transfers between devices: 31.2 us -> 7.12 us  [local(): img = lax.all_gather(image_embed, CZ, axis=0, tiled=True)]
    all_gather x1, blocking collectives: 25.7 us -> 2.43 us  [local(): pairs = lax.all_gather(pair_col, 'c', axis=0, tiled=True)]
    all_to_all x0 -> x3, starting transfers between devices: none -> 17.7 us  [the longest x1 7.72 us: local(): lax.all_to_all(jnp.broadcast_to(text_embed[None], (peers, part, embed)),...]
    all_to_all x0 -> x1, blocking collectives: none -> 12.8 us  [exchange(): lax.all_to_all(jnp.broadcast_to(flat[None], (n,) + flat.shape), axes, 0, 0)]
    dot_general x3, matrix products: 15.6 us -> 8.66 us  [the longest x1 3.94 us: local(): lax.dot_general(img, txt, (((1,), (1,)), ((), ())), preferred_element_typ...]
  transfers between devices with their start and end apart: 3 -> 8, of which waited for: 1 -> 4; matrix products, arithmetic and copies ran while one was open for 2% -> 6% of each run, Pallas kernels for 0% -> 0%
where the time goes in v1:
time: 157 us; the launch traced here: 156 us
  waiting for transfers between devices  68.6 us (44%)
  starting transfers between devices  22.2 us (14%)
  between operations  20 us (13%)
  blocking collectives  15.3 us (10%)
  local copies, waits for them, and re-layouts  11.7 us (7%)
  other arithmetic  9.56 us (6%)
  matrix products  8.66 us (6%)
    all_to_all x1, waiting for transfers between devices, local(): text_term = lax.all_to_all(text_term, XY, 0, 0)  28.2 us
    all_to_all x1, waiting for transfers between devices, local(): lax.all_to_all(jnp.broadcast_to(text_embed[None], (peers, part, embed)),...  25.4 us
    all_to_all x1, blocking collectives, exchange(): lax.all_to_all(jnp.broadcast_to(flat[None], (n,) + flat.shape), axes, 0, 0)  12.8 us
    all_to_all x1, starting transfers between devices, local(): lax.all_to_all(jnp.broadcast_to(text_embed[None], (peers, part, embed)),...  7.72 us
    all_to_all x1, waiting for transfers between devices, exchange(): lax.all_to_all(jnp.broadcast_to(flat[None], (n,) + flat.shape), axes, 0, 0)  7.15 us
    all_gather x1, waiting for transfers between devices, local(): img = lax.all_gather(image_embed, CZ, axis=0, tiled=True)  7.12 us
    all_to_all x1, starting transfers between devices, exchange(): lax.all_to_all(jnp.broadcast_to(flat[None], (n,) + flat.shape), axes, 0, 0)  6.14 us
    dot_general x1, matrix products, local(): lax.dot_general(img, txt, (((1,), (1,)), ((), ())), preferred_element_typ...  3.94 us
  transfers between devices with their start and end apart: 8, of which 4 were waited for; matrix products, arithmetic and copies ran while one was open for 6% of the time, Pallas kernels for 0%

profile of v1, /device:TPU:1, one launch (start us, length us, event | category | flops | bytes accessed | tf_op | source)
XLA Modules:
  0.0 156.1 jit_solution(1482583075874628185)
XLA Ops:
  7.2 0.0 all-gather.3.cloned.1.call-start
  7.2 0.7 all-gather.3.cloned.1.call-update
  7.9 2.3 %broadcast_in_dim.18 = bf16[16,48,1280]{2,1,0:T(8,128)(2,1)} broadcast(bf16[48,1280]{1,0:T(8,128)(2,1)} %param.5), dimensions={1,2} | broadcast | bytes 2088960 | tf_op jit(solution)/shard_map/broadcast_in_dim | solution.py:28
  10.2 0.0 copy-start.5
  10.2 7.7 %all-to-all-start = ((bf16[16,48,1280]{2,1,0:T(8,128)(2,1)}), bf16[16,48,1280]{2,1,0:T(8,128)(2,1)S(1)}, u32[]{:S(2)}, u32[]{:S(2)}) async-start(bf16[16,48,1280]{2,1,0:T(8,128)(2,1)} %broadcast_in_dim.18), calls=%async_computation | async-start | bytes 3932160 | tf_op jit(solution)/shard_map/all_to_all | solution.py:28
  18.6 0.0 copy-done.5
  18.6 2.4 %all-gather = s32[2,1,384]{2,1,0:T(1,128)S(1)} all-gather(s32[1,1,384]{2,1,0:T(1,128)S(1)} %reshape.111), channel_id=1, replica_groups=mesh['y'=4,'x'=4,'c'=2,'z'=8] {'c'}, dimensions={0}, use_global_device_ids=true | all-gather | bytes 4608 | tf_op jit(solution)/shard_map/all_gather | solution.py:31
  21.1 25.4 %all-to-all-done = bf16[16,48,1280]{2,1,0:T(8,128)(2,1)S(1)} async-done(((bf16[16,48,1280]{2,1,0:T(8,128)(2,1)}), bf16[16,48,1280]{2,1,0:T(8,128)(2,1)S(1)}, u32[]{:S(2)}, u32[]{:S(2)}) %all-to-all-start) | async-done | bytes 1966112 | tf_op jit(solution)/shard_map/all_to_all | solution.py:28
  46.6 0.0 copy-start.1
  46.6 7.1 %all-gather.3.cloned.1.call-done = bf16[768,1280]{1,0:T(8,128)(2,1)} async-done(((bf16[48,1280]{1,0:T(8,128)(2,1)}), bf16[768,1280]{1,0:T(8,128)(2,1)}) %all-gather.3.cloned.1.call-update) | async-done | bytes 1966096 | tf_op jit(solution)/shard_map/all_gather | solution.py:27
  53.7 0.0 copy-done.1
  53.7 3.9 %fusion.26 = (f32[768]{0:T(1024)S(1)}, f32[768]{0:T(1024)S(1)}, f32[768,768]{1,0:T(8,128)S(1)}) fusion(bf16[768,1280]{1,0:T(8,128)(2,1)} %all-gather.3.cloned.1.call-done, bf16[768,1280]{1,0:T(8,128)(2,1)} %bitcast.36, f32[]{:T(128)S(6)} %exp.21), kind=kOutput, calls=%fused_computation.68 | convolution fusion | flops 1511717376 | bytes 6297604 | tf_op jit(solution)/shard_map/dot_general | solution.py:36
  57.6 1.9 %fusion.3 = (f32[768]{0:T(1024)S(1)}, f32[768]{0:T(1024)S(1)}, f32[768]{0:T(1024)S(1)}, f32[768]{0:T(1024)S(1)}, f32[768]{0:T(1024)S(1)}, /*index=5*/f32[768]{0:T(1024)S(1)}) fusion(f32[768,768]{1,0:T(8,128)S(1)} %get-tuple-element.34, f32[768]{0:T(1024)S(1)} %get-tuple-element.15, s32[768]{0:T(1024)S(1)} %fusion.24, s32[768]{0:T(1024)S(1)} %reshape.112, ...), kind=kLoop, calls=%fused_computation.9 | loop fusion | flops 7073280 | bytes 2390016 | tf_op jit(solution)/shard_map/reduce_sum | solution.py:47
  59.6 12.8 %all_to_all.20 = f32[16,24,128]{2,1,0:T(8,128)S(1)} all-to-all(f32[16,24,128]{2,1,0:T(8,128)S(1)} %broadcast_in_dim.21), channel_id=1, replica_groups=mesh['y'=4,'x'=4,'c'=2,'z'=8] {'c','z'}, dimensions={0} | all-to-all | bytes 393216 | tf_op jit(solution)/shard_map/all_to_all | solution.py:56
  72.5 0.6 fusion.9
  73.1 1.2 fusion.28
  75.7 0.7 broadcast_in_dim.45
  76.3 6.1 %all-to-all-start.2 = ((f32[16,24,128]{2,1,0:T(8,128)}), f32[16,24,128]{2,1,0:T(8,128)S(1)}, u32[]{:S(2)}, u32[]{:S(2)}) async-start(f32[16,24,128]{2,1,0:T(8,128)} %broadcast_in_dim.45), calls=%async_computation.2 | async-start | bytes 393216 | tf_op jit(solution)/shard_map/all_to_all | solution.py:56
  82.5 0.0 reduce-scatter.2.cloned.1.call-start
  82.5 7.2 %all-to-all-done.2 = f32[16,24,128]{2,1,0:T(8,128)S(1)} async-done(((f32[16,24,128]{2,1,0:T(8,128)}), f32[16,24,128]{2,1,0:T(8,128)S(1)}, u32[]{:S(2)}, u32[]{:S(2)}) %all-to-all-start.2) | async-done | bytes 196640 | tf_op jit(solution)/shard_map/all_to_all | solution.py:56
  89.7 0.0 copy-start.2
  89.7 0.0 copy-start.3
  89.8 0.6 fusion.27
  90.4 0.0 copy-done.3
  90.4 1.0 fusion.2
  91.5 0.0 copy-done.2
  91.5 1.7 %fusion.29 = f32[2,8,48,1280]{3,2,1,0:T(8,128)S(1)} fusion(bf16[2,8,48,768]{3,2,1,0:T(8,128)(2,1)S(1)} %bitcast.39, bf16[768,1280,1,1]{1,0,3,2:T(8,128)(2,1)S(1)} %bitcast.37), kind=kOutput, calls=%fused_computation.71 | convolution fusion | flops 1509949440 | bytes 7077888 | tf_op jit(solution)/shard_map/dot_general | solution.py:82
  93.2 0.0 copy-start
  93.2 1.9 %copy-done = f32[2,8,48,1280]{3,2,1,0:T(8,128)} copy-done((f32[2,8,48,1280]{3,2,1,0:T(8,128)}, f32[2,8,48,1280]{3,2,1,0:T(8,128)S(1)}, u32[]{:S(2)}) %copy-start) | copy-done | bytes 3932184
  95.1 0.1 fusion.7
  95.2 2.5 %collective-permute-start.1 = (bf16[8,48,1280]{2,1,0:T(8,128)(2,1)S(1)}, bf16[8,48,1280]{2,1,0:T(8,128)(2,1)S(1)}, u32[]{:S(2)}, u32[]{:S(2)}) collective-permute-start(bf16[8,48,1280]{2,1,0:T(8,128)(2,1)S(1)} %fusion.7), channel_id=1, source_target_pairs={{0,8},{8,0},{1,9},{9,1},{2,10},{10,2},{3,11},{11,3},{4,12},{12,4},... | collective-permute-start | bytes 2949128 | tf_op jit(solution)/shard_map/ppermute | solution.py:86
  98.4 1.5 collective-permute-start.2
  99.9 0.0 collective-permute-done.2
  100.6 0.0 collective-permute-done.1
  100.6 1.7 %bitcast_add_fusion = f32[8,48,1280]{2,1,0:T(8,128)S(1)} fusion(bf16[8,48,1280]{2,1,0:T(8,128)(2,1)S(1)} %collective-permute-done.1, f32[2,8,48,1280]{3,2,1,0:T(8,128)} %copy-done, s32[]{:T(128)S(6)} %select_n.53), kind=kLoop, calls=%fused_computation.15 | loop fusion | flops 983040 | bytes 4915204 | tf_op jit(solution)/shard_map/add | solution.py:86
  102.4 0.0 copy-start.6
  102.4 1.5 concatenate.19
  103.9 0.0 reduce-scatter.2.cloned.1.call-update
  103.9 0.8 copy-done.6
  104.7 3.0 %convolution_convert_fusion = bf16[768,1280]{1,0:T(8,128)(2,1)} fusion(bf16[768,768]{1,0:T(8,128)(2,1)S(1)} %fusion.2, bf16[768,1280]{1,0:T(8,128)(2,1)S(1)} %copy-done.6), kind=kOutput, calls=%fused_computation.1 | convolution fusion | flops 1510932480 | bytes 5111808 | tf_op jit(solution)/shard_map/dot_general | solution.py:93
  107.8 0.0 copy-start.4
  107.8 3.8 %all-to-all-start.3 = ((bf16[16,48,1280]{2,1,0:T(8,128)(2,1)}), bf16[16,48,1280]{2,1,0:T(8,128)(2,1)S(1)}, u32[]{:S(2)}, u32[]{:S(2)}) async-start(bf16[16,48,1280]{2,1,0:T(8,128)(2,1)} %bitcast.38), calls=%async_computation.4 | async-start | bytes 3932160 | tf_op jit(solution)/shard_map/all_to_all | solution.py:97
  111.6 0.0 copy-done.4
  111.6 0.7 dynamic_slice.10
  112.3 0.1 sub.91
  112.4 0.4 collective-permute-start
  112.8 1.3 slice_reduce_fusion.5
  114.1 0.0 collective-permute-done
  114.1 0.7 select_n.52
  114.8 28.2 %all-to-all-done.3 = bf16[16,48,1280]{2,1,0:T(8,128)(2,1)S(1)} async-done(((bf16[16,48,1280]{2,1,0:T(8,128)(2,1)}), bf16[16,48,1280]{2,1,0:T(8,128)(2,1)S(1)}, u32[]{:S(2)}, u32[]{:S(2)}) %all-to-all-start.3) | async-done | bytes 1966112 | tf_op jit(solution)/shard_map/all_to_all | solution.py:97
  143.0 1.0 convert_reduce_fusion
  144.0 0.0 reduce-scatter.2.cloned.1.call-done
  144.0 1.2 slice.48
  146.4 1.7 %slice_bitcast_fusion = f32[48,1280]{1,0:T(8,128)} fusion(f32[1,56,1280]{2,1,0:T(8,128)} %reduce-scatter.2.cloned.1.call-done), kind=kLoop, calls=%fused_computation.19 | loop fusion | bytes 491520 | tf_op jit(solution)/shard_map/slice | solution.py:91
  (14 shorter events, 0.3 us)
Async XLA Ops:
  7.2 46.5 %all-gather.3.cloned.1.call-start = ((), (), s32[]{:S(2)}) async-start(), calls=%async_computation.5 | async-start | bytes 2088960 | tf_op jit(solution)/shard_map/all_gather | solution.py:27
  10.2 8.4 %copy-start.5 = (s32[384]{0:T(512)S(1)}, s32[384]{0:T(512)}, u32[]{:S(2)}) copy-start(s32[384]{0:T(512)} %param.6) | copy-start | bytes 4612
  10.2 36.4 %all-to-all-start = ((bf16[16,48,1280]{2,1,0:T(8,128)(2,1)}), bf16[16,48,1280]{2,1,0:T(8,128)(2,1)S(1)}, u32[]{:S(2)}, u32[]{:S(2)}) async-start(bf16[16,48,1280]{2,1,0:T(8,128)(2,1)} %broadcast_in_dim.18), calls=%async_computation | async-start | bytes 3932160 | tf_op jit(solution)/shard_map/all_to_all | solution.py:28
  46.6 7.1 %copy-start.1 = (bf16[16,48,1280]{2,1,0:T(8,128)(2,1)}, bf16[16,48,1280]{2,1,0:T(8,128)(2,1)S(1)}, u32[]{:S(2)}) copy-start(bf16[16,48,1280]{2,1,0:T(8,128)(2,1)S(1)} %all-to-all-done) | copy-start | bytes 5898244
  76.3 13.4 %all-to-all-start.2 = ((f32[16,24,128]{2,1,0:T(8,128)}), f32[16,24,128]{2,1,0:T(8,128)S(1)}, u32[]{:S(2)}, u32[]{:S(2)}) async-start(f32[16,24,128]{2,1,0:T(8,128)} %broadcast_in_dim.45), calls=%async_computation.2 | async-start | bytes 393216 | tf_op jit(solution)/shard_map/all_to_all | solution.py:56
  82.5 61.5 %reduce-scatter.2.cloned.1.call-start = ((), (), s32[]{:S(2)}) async-start(), calls=%async_computation.6 | async-start | bytes 2580480 | tf_op jit(solution)/shard_map/reduce_scatter | solution.py:90
  89.7 1.8 %copy-start.2 = (bf16[16,48,1280]{2,1,0:T(8,128)(2,1)S(1)}, bf16[16,48,1280]{2,1,0:T(8,128)(2,1)}, u32[]{:S(2)}) copy-start(bf16[16,48,1280]{2,1,0:T(8,128)(2,1)} %copy-done.1) | copy-start | bytes 5898244
  89.7 0.7 copy-start.3
  93.2 1.9 %copy-start = (f32[2,8,48,1280]{3,2,1,0:T(8,128)}, f32[2,8,48,1280]{3,2,1,0:T(8,128)S(1)}, u32[]{:S(2)}) copy-start(f32[2,8,48,1280]{3,2,1,0:T(8,128)S(1)} %fusion.29) | copy-start | bytes 11796484
  95.2 5.4 %collective-permute-start.1 = (bf16[8,48,1280]{2,1,0:T(8,128)(2,1)S(1)}, bf16[8,48,1280]{2,1,0:T(8,128)(2,1)S(1)}, u32[]{:S(2)}, u32[]{:S(2)}) collective-permute-start(bf16[8,48,1280]{2,1,0:T(8,128)(2,1)S(1)} %fusion.7), channel_id=1, source_target_pairs={{0,8},{8,0},{1,9},{9,1},{2,10},{10,2},{3,11},{11,3},{4,12},{12,4},... | collective-permute-start | bytes 2949128 | tf_op jit(solution)/shard_map/ppermute | solution.py:86
  98.4 1.5 collective-permute-start.2
  102.4 2.4 %copy-start.6 = (bf16[768,1280]{1,0:T(8,128)(2,1)S(1)}, bf16[768,1280]{1,0:T(8,128)(2,1)}, u32[]{:S(2)}) copy-start(bf16[768,1280]{1,0:T(8,128)(2,1)} %all-gather.3.cloned.1.call-done) | copy-start | bytes 5898244
  107.8 3.9 %copy-start.4 = (f32[768]{0:T(1024)S(1)}, f32[768]{0:T(1024)}, u32[]{:S(2)}) copy-start(f32[768]{0:T(1024)} %get-tuple-element.26) | copy-start | bytes 9220
  107.8 35.2 %all-to-all-start.3 = ((bf16[16,48,1280]{2,1,0:T(8,128)(2,1)}), bf16[16,48,1280]{2,1,0:T(8,128)(2,1)S(1)}, u32[]{:S(2)}, u32[]{:S(2)}) async-start(bf16[16,48,1280]{2,1,0:T(8,128)(2,1)} %bitcast.38), calls=%async_computation.4 | async-start | bytes 3932160 | tf_op jit(solution)/shard_map/all_to_all | solution.py:97
  112.4 1.7 %collective-permute-start = (f32[16,1,48]{2,1,0:T(1,128)S(1)}, f32[16,1,48]{2,1,0:T(1,128)S(1)}, u32[]{:S(2)}, u32[]{:S(2)}) collective-permute-start(f32[16,1,48]{2,1,0:T(1,128)S(1)} %sub.91), channel_id=1, source_target_pairs={{0,8},{8,0},{1,9},{9,1},{2,10},{10,2},{3,11},{11,3},{4,12},{12,4},... | collective-permute-start | bytes 9224 | tf_op jit(solution)/shard_map/ppermute | solution.py:72
Sparse Core Ops, SparseCore 0:
  9.8 43.8 all-gather.2
  104.1 32.9 reduce-scatter.1

commit v2 on v0

v2 whole, which is shorter than its diff:
```python
import functools

import jax
import jax.numpy as jnp
from jax import lax
from jax.experimental import pallas as pl
from jax.experimental.pallas import tpu as pltpu
from jax.sharding import Mesh, PartitionSpec as P

NY, NX, NC = 4, 4, 2
XY = ("y", "x")
CZ = ("c", "z")
SWAP = [(0, 1), (1, 0)]
LANES = 128
F32 = jnp.float32
BF16 = jnp.bfloat16


def call(body, out_shape, *args, flops=0, smem=(), scratch=(), far=(), sent=()):
    places = {True: pl.BlockSpec(memory_space=pl.ANY), False: pl.BlockSpec(memory_space=pltpu.VMEM)}
    scalars = pl.BlockSpec(memory_space=pltpu.SMEM)
    many = isinstance(out_shape, tuple)
    outs = tuple(places[i in sent] for i in range(len(out_shape) if many else 1))
    size = sum(a.size * a.dtype.itemsize for a in args)
    return pl.pallas_call(
        body,
        out_shape=out_shape,
        in_specs=[scalars if i in smem else places[i in far] for i in range(len(args))],
        out_specs=outs if many else outs[0],
        scratch_shapes=scratch,
        cost_estimate=pl.CostEstimate(flops=flops, bytes_accessed=size, transcendentals=0),
        compiler_params=pltpu.CompilerParams(vmem_limit_bytes=16 * 1024 * 1024),
    )(*args)


def copies(sems, *pairs):
    started = [pltpu.make_async_copy(a, b, sems.at[i]) for i, (a, b) in enumerate(pairs)]
    for copy in started:
        copy.start()
    return started


def finish(started):
    for copy in started:
        copy.wait()


def dot(a, b, dims):
    return lax.dot_general(a, b, (dims, ((), ())), preferred_element_type=F32)


def spread_kernel(peers, txt, img, out, img_out, sems):
    finish(copies(sems, (img, img_out), *[(txt, out.at[p]) for p in range(peers)]))


def place_kernel(*refs):
    pieces, out, sems = refs[:-2], refs[-2], refs[-1]
    pairs, at = [], 0
    for piece in pieces:
        size = piece.shape[0]
        pairs.append((piece, out.at[at : at + size]))
        at += size
    finish(copies(sems, *pairs))


def pack(rows):
    tiles = []
    for row in rows:
        n = row.shape[1] // LANES
        tiles += [row[:, q * LANES : (q + 1) * LANES] for q in range(n)]
        tiles += [jnp.zeros((8 - n, LANES), F32)]
    return jnp.concatenate(tiles, axis=0)


def unpack(tile, n):
    return jnp.concatenate([tile[q : q + 1] for q in range(n)], axis=1)


def order_of(nz):
    first = [(who, k) for k in range(1, nz // 2) for who in (0, 1)] + [(0, nz // 2), (0, 0)]
    return first + [(1 - who, -k) for who, k in first]


def row_at(idx, block, nz, part):
    who, k = block
    c, z = idx[0], idx[1]
    core = c if who == 0 else 1 - c
    step = k * (1 - 2 * c)
    return pl.multiple_of((core * nz + lax.rem(z + step + nz, nz)) * part, 16)


def tall(rows):
    return jnp.concatenate(rows + [rows[-1]] * (8 - len(rows)), axis=0).T


def logits_kernel(peers, nz, idx, scale, own, oth, txt, pairs, logits, msg, txt_in, stat, column, packed, sems):
    half = own.shape[0]
    rows, cols = logits.shape
    part = rows // (NC * nz)
    loaded = copies(sems, *[(txt.at[n : n + 256], txt_in.at[n : n + 256]) for n in range(0, cols, 256)])
    column[...] = tall([unpack(pairs[...], rows // LANES)])
    s = scale[0]
    for i, n in enumerate(range(0, cols, 256)):
        loaded[i].wait()
        for at, images in ((0, own), (half, oth)):
            logits[at : at + half, n : n + 256] = s * dot(images[...], txt_in[n : n + 256, :], ((1,), (1,)))

    lane = lax.broadcasted_iota(jnp.int32, (part, LANES), 1)
    for i, block in enumerate(order_of(nz)):
        x = logits[i * part : (i + 1) * part, :]
        at = pl.ds(row_at(idx, block, nz, part), part)
        hit = lax.broadcasted_iota(jnp.int32, x.shape, 1) == column[at, 0:1].astype(jnp.int32)
        pos = jnp.sum(jnp.where(hit, x, 0.0), axis=1, keepdims=True)
        top = jnp.max(x, axis=1, keepdims=True)
        e = jnp.exp(x - top)
        total = jnp.sum(e, axis=1, keepdims=True)
        mean = jnp.sum(e * x, axis=1, keepdims=True) / total
        lse = top + jnp.log(total)
        stat[at, :] = jnp.where(lane == 0, lse, jnp.where(lane == 1, mean, jnp.where(lane == 2, pos, 0.0)))

    flat = stat[...].T
    packed[...] = pack([flat[0:1], flat[1:2], flat[2:3]])
    finish(copies(sems, *[(packed, msg.at[p]) for p in range(peers)]))


def columns_kernel(nz, idx, logits, pairs, out, column):
    rows, cols = logits.shape
    part = rows // (NC * nz)
    column[...] = tall([unpack(pairs[...], rows // LANES)])

    def fold(x):
        return x.reshape(part // 8, 8, cols)

    top = lax.fori_loop(
        0,
        rows // part,
        lambda i, m: jnp.maximum(m, jnp.max(fold(logits[pl.ds(pl.multiple_of(i * part, 16), part), :]), axis=0)),
        jnp.full((8, cols), -jnp.inf, F32),
    )
    top = jnp.max(top, axis=0, keepdims=True)
    total = moment = pos = jnp.zeros((8, cols), F32)
    for i, block in enumerate(order_of(nz)):
        x = logits[i * part : (i + 1) * part, :]
        at = pl.ds(row_at(idx, block, nz, part), part)
        hit = lax.broadcasted_iota(jnp.int32, x.shape, 1) == column[at, 0:1].astype(jnp.int32)
        e = jnp.exp(x - top)
        total += jnp.sum(fold(e), axis=0)
        moment += jnp.sum(fold(e * x), axis=0)
        pos += jnp.sum(fold(jnp.where(hit, x, 0.0)), axis=0)
    total = jnp.sum(total, axis=0, keepdims=True)
    moment = jnp.sum(moment, axis=0, keepdims=True)
    pos = jnp.sum(pos, axis=0, keepdims=True)
    out[...] = pack([top + jnp.log(total), moment / total, pos])


def merge(got):
    lse = got[:, 0:8, :]
    top = jnp.max(lse, axis=0)
    weight = jnp.exp(lse - top[None])
    total = jnp.sum(weight, axis=0)
    mean = jnp.sum(weight * got[:, 8:16, :], axis=0) / total
    return top + jnp.log(total), mean, jnp.sum(got[:, 16:24, :], axis=0)


def total_of(x):
    return jnp.sum(jnp.sum(x, axis=1, keepdims=True), axis=0, keepdims=True)


def rows_kernel(peers, count, got, stat, msg, lse_out, loss_out, packed, sems):
    lse, mean, pos = merge(got[...])
    row = lax.broadcasted_iota(jnp.int32, lse.shape, 0)
    used = row < count
    lse_out[...] = lse
    loss_out[...] = lse - pos
    total = total_of(jnp.where(used, 0.5 * mean - pos, 0.0))
    packed[...] = stat[...] + jnp.concatenate([jnp.where(row == count, total, 0.0), jnp.zeros((16, LANES), F32)], 0)
    finish(copies(sems, *[(packed, msg.at[p]) for p in range(peers)]))


def text_kernel(
    count, nz, idx, scale, got, logits, lse_in, pairs, own, oth, grad, text, loss_out, sums, column, blocks, sems
):
    half = own.shape[0]
    rows, cols = logits.shape
    part = rows // (NC * nz)
    s = scale[0]
    values = got[...]
    lse, mean, pos = merge(values)
    row = lax.broadcasted_iota(jnp.int32, lse.shape, 0)
    loss_out[...] = lse - pos
    col_total = total_of(jnp.where(row < count, 0.5 * mean, 0.0))
    row_total = total_of(jnp.where((row == count), jnp.sum(values[:, 0:8, :], axis=0), 0.0)) * (1.0 / LANES)
    sums[...] = jnp.where(row == 0, row_total, col_total)
    flat = unpack(lse, count)
    column[...] = tall([unpack(lse_in[...], count), unpack(pairs[...], count)])

    for i, block in enumerate(order_of(nz)):
        x = logits[i * part : (i + 1) * part, :]
        at = pl.ds(row_at(idx, block, nz, part), part)
        hit = lax.broadcasted_iota(jnp.int32, x.shape, 1) == column[at, 1:2].astype(jnp.int32)
        value = 0.5 * (jnp.exp(x - column[at, 0:1]) + jnp.exp(x - flat)) - jnp.where(hit, 1.0, 0.0)
        grad[i * part : (i + 1) * part, :] = (s * value).astype(BF16)

    started = []
    for i, n in enumerate(range(0, own.shape[1], 256)):
        block = dot(grad[:half, :], own[:, n : n + 256], ((0,), (0,)))
        block += dot(grad[half:, :], oth[:, n : n + 256], ((0,), (0,)))
        blocks[:, n : n + 256] = block.astype(BF16)
        started.append(pltpu.make_async_copy(blocks.at[:, n : n + 256], text.at[:, n : n + 256], sems.at[i]))
        started[-1].start()
    finish(started)


def image_kernel(grad, txt, keep, send, txt_in, sems):
    half, embed = keep.shape
    cuts = range(0, embed, 256)
    loaded = copies(sems, *[(txt.at[:, n : n + 256], txt_in.at[:, n : n + 256]) for n in cuts])
    for i, n in enumerate(cuts):
        loaded[i].wait()
        cut = txt_in[:, n : n + 256]
        send[:, n : n + 256] = dot(grad[half:, :], cut, ((1,), (0,))).astype(BF16)
        keep[:, n : n + 256] = dot(grad[:half, :], cut, ((1,), (0,)))


def pieces_kernel(keep, received, sums, other_sums, own, *outs):
    part, embed = own.shape
    total = sums[1:2, :] + other_sums[1:2, :]
    high = total.astype(BF16)
    rest = total - high.astype(F32)
    middle = rest.astype(BF16)
    low = (rest - middle.astype(F32)).astype(BF16)
    at = 0
    for out in outs:
        size = out.shape[0]
        out[:, :embed] = (keep[at : at + size, :] + received[at : at + size, :].astype(F32)).astype(BF16)
        lane = lax.broadcasted_iota(jnp.int32, (size, LANES), 1)
        tail = jnp.where(lane == 0, high.astype(F32), jnp.where(lane == 1, middle.astype(F32), low.astype(F32)))
        out[:, embed:] = tail.astype(BF16)
        at += size
    own[...] = keep[at:, :] + received[at:, :].astype(F32)


def tail_of(ref, embed):
    tail = ref[0:16, embed:].astype(F32)[0:8]
    lane = lax.broadcasted_iota(jnp.int32, tail.shape, 1)
    return jnp.sum(jnp.where(lane < 3, tail, 0.0), axis=1, keepdims=True)


def chip_sum_kernel(sums, other_sums, own, *refs):
    arrived, keep, send = refs[:-2], refs[-2], refs[-1]
    part, embed = own.shape
    mine = own[...]
    theirs = jnp.zeros(own.shape, F32)
    tail = jnp.zeros((8, 1), F32)
    for ref in arrived:
        mine = mine + ref[0:part, :embed].astype(F32)
        if ref.shape[0] > part:
            theirs = theirs + ref[part:, :embed].astype(F32)
            tail = tail + tail_of(ref, embed)
    keep[:, :embed] = mine
    send[:, :embed] = theirs
    send[:, embed:] = jnp.zeros((part, LANES), F32)
    send[0:8, embed:] = jnp.broadcast_to(tail, (8, LANES))
    both = tail_of(arrived[-1], embed) + sums[1:2, :] + other_sums[1:2, :]
    keep[:, embed:] = jnp.zeros((part, LANES), F32)
    keep[0:8, embed:] = tail + both + sums[0:1, :]


def image_sum_kernel(scale, keep, received, out, temp):
    embed = out.shape[1]
    out[...] = keep[:, :embed] + received[:, :embed]
    temp[...] = (keep[0:8, embed:] + received[0:8, embed:]) * scale[0]


def text_sum_kernel(got, out):
    out[...] = jnp.sum(got[...].astype(F32), axis=0)


def local(image_embed, text_embed, pair_col, log_scale):
    part, embed = image_embed.shape
    peers = NY * NX
    nz = lax.axis_size("z")
    half = nz * part
    rows, cols = NC * half, peers * part
    count = rows // LANES
    batch = peers * rows
    c = lax.axis_index("c")
    z = lax.axis_index("z")
    idx = jnp.stack([c, z])
    scale = jnp.exp(log_scale)
    scale1 = scale[None]
    sds = jax.ShapeDtypeStruct
    sems = lambda n: pltpu.SemaphoreType.DMA((n,))
    last = nz // 2

    def swap(x):
        return lax.ppermute(x, "c", SWAP)

    def ahead(x, k):
        pairs = [((i + k) % nz, i) for i in range(nz)]
        return lax.ppermute(x, CZ, pairs + [(nz + i, nz + (i + k) % nz) for i in range(nz)])

    def onward(x, k):
        pairs = [(i, (i + k) % nz) for i in range(nz)]
        return lax.ppermute(x, CZ, pairs + [(nz + (i + k) % nz, nz + i) for i in range(nz)])

    spread, image = call(
        functools.partial(spread_kernel, peers),
        (sds((peers, part, embed), BF16), sds((part, embed), BF16)),
        text_embed,
        image_embed,
        far=(0, 1),
        sent=(0, 1),
        scratch=[sems(peers + 1)],
    )
    txt = lax.all_to_all(spread, XY, 0, 0).reshape(cols, embed)
    chip = jnp.concatenate([image, swap(image)])
    got = [ahead(image, last)] + [ahead(chip, k) for k in range(last - 1, 0, -1)]
    own = call(
        place_kernel,
        sds((half, embed), BF16),
        *got[:0:-1],
        got[0],
        image,
        far=range(last + 1),
        scratch=[sems(last + 1)],
    )
    oth = swap(own)

    rem = pair_col % (cols * NC)
    block = rem // part
    ours = pair_col // (cols * NC) == z
    place = (block // NC * part + rem % part).astype(F32)
    mine = jnp.where(ours & (block % NC == c), place, -1.0)
    theirs = swap(jnp.where(ours & (block % NC == 1 - c), place, -1.0))
    pairs = jnp.where(c == 0, jnp.concatenate([mine, theirs]), jnp.concatenate([theirs, mine]))
    pairs = jnp.pad(pairs, (0, 8 * LANES - rows)).reshape(8, LANES)

    work = 2 * rows * cols * embed
    logits, msg = call(
        functools.partial(logits_kernel, NC * nz, nz),
        (sds((rows, cols), F32), sds((NC * nz, 24, LANES), F32)),
        idx,
        scale1,
        own,
        oth,
        txt,
        pairs,
        flops=work,
        smem=(0, 1),
        far=(4,),
        sent=(1,),
        scratch=[
            pltpu.VMEM((cols, embed), BF16),
            pltpu.VMEM((rows, LANES), F32),
            pltpu.VMEM((rows, 8), F32),
            pltpu.VMEM((24, LANES), F32),
            sems(NC * nz),
        ],
    )
    row_got = lax.all_to_all(msg, CZ, 0, 0)
    stat = call(
        functools.partial(columns_kernel, nz),
        sds((24, LANES), F32),
        idx,
        logits,
        pairs,
        flops=8 * rows * cols,
        smem=(0,),
        scratch=[pltpu.VMEM((rows, 8), F32)],
    )
    msg, row_lse, row_loss = call(
        functools.partial(rows_kernel, peers, count),
        (sds((peers, 24, LANES), F32), sds((8, LANES), F32), sds((8, LANES), F32)),
        row_got,
        stat,
        sent=(0,),
        scratch=[pltpu.VMEM((24, LANES), F32), sems(peers)],
    )
    col_got = lax.all_to_all(msg, XY, 0, 0)
    row_loss = lax.dynamic_slice(row_loss, (c * (count // NC), 0), (count // NC, LANES)).reshape(-1)

    grad, text_term, col_loss, sums = call(
        functools.partial(text_kernel, count, nz),
        (sds((rows, cols), BF16), sds((cols, embed), BF16), sds((8, LANES), F32), sds((8, LANES), F32)),
        idx,
        scale1,
        col_got,
        logits,
        row_lse,
        pairs,
        own,
        oth,
        flops=work,
        smem=(0, 1),
        sent=(1,),
        scratch=[pltpu.VMEM((rows, 8), F32), pltpu.VMEM((cols, embed), BF16), sems(embed // 256)],
    )
    text_got = lax.all_to_all(text_term.reshape(peers, part, embed), XY, 0, 0)
    keep, send = call(
        image_kernel,
        (sds((half, embed), F32), sds((half, embed), BF16)),
        grad,
        txt,
        flops=work,
        far=(1,),
        scratch=[pltpu.VMEM((cols, embed), BF16), sems(embed // 256)],
    )
    received = swap(send)
    other_sums = swap(sums)
    shapes = [sds((NC * part, embed + LANES), BF16)] * (last - 1) + [sds((part, embed + LANES), BF16)]
    own_sum, *outs = call(
        pieces_kernel, (sds((part, embed), F32), *shapes), keep, received, sums, other_sums
    )
    arrived = {k: onward(outs[k - 1], k) for k in range(last, 0, -1)}
    wide = sds((part, embed + LANES), F32)
    keep, send = call(
        chip_sum_kernel, (wide, wide), sums, other_sums, own_sum, *[arrived[k] for k in range(1, last + 1)]
    )
    grad_image, temp = call(
        image_sum_kernel,
        (sds((part, embed), F32), sds((8, LANES), F32)),
        jnp.full((1,), 1.0 / batch, F32),
        keep,
        swap(send),
        smem=(0,),
    )

    col_loss = col_loss[:count].reshape(peers, 1, part)
    other = swap(col_loss)
    col_loss = jnp.where(
        c == 0, jnp.concatenate([col_loss, other], 1), jnp.concatenate([other, col_loss], 1)
    ).reshape(-1)
    grad_text = call(text_sum_kernel, sds((part, embed), F32), text_got)
    return (row_loss, col_loss, grad_image, grad_text, temp[0, 0])


def solution(mesh):
    nz = mesh.shape["txt"]
    grid = Mesh(mesh.devices.reshape(NY, NX, NC, nz), ("y", "x", "c", "z"))
    images, texts = ("y", "x", "c", "z"), ("z", "y", "x", "c")
    in_specs = (P(images, None), P(texts, None), P(("y", "x", "c")), P())
    out_specs = (P(("y", "x", "c")), P("z"), P(images, None), P(texts, None), P())
    return jax.shard_map(local, mesh=grid, in_specs=in_specs, out_specs=out_specs, check_vma=False)
```

time: 409 us -> 145 us (0.35)
  blocking collectives: 337 us -> 13.9 us
  starting transfers between devices: 0.12 us -> 46.8 us
  Pallas kernels: 0 us -> 23.6 us
  matrix products: 15.6 us -> 0 us
  local copies, waits for them, and re-layouts: 0.01 us -> 15 us
  between operations: 16.3 us -> 1.55 us
  waiting for transfers between devices: 32 us -> 43.7 us
    psum x5 -> x0, blocking collectives: 234 us -> none  [the longest x2 134 us: local(): lax.psum((jnp.sum(jnp.exp(logits - col_max[None, :]), axis=0), col_part),...]
    pmax x2 -> x0, blocking collectives: 77.1 us -> none  [the longest x1 63.3 us: local(): col_max = lax.pmax(jnp.max(logits, axis=0), 'img')]
    ppermute x0 -> x15, waiting for transfers between devices: none -> 37.9 us  [the longest x4 20.4 us: ahead(): lax.ppermute(x, CZ, pairs + [(nz + i, nz + (i + k) % nz) for i in range(n...]
    all_gather x1 -> x0, waiting for transfers between devices: 31.2 us -> none  [local(): txt_all = lax.all_gather(text_embed, 'img', axis=0, tiled=True)]
    ppermute x0 -> x15, starting transfers between devices: none -> 29.4 us  [the longest x7 12.3 us: swap(): return lax.ppermute(x, 'c', SWAP)]
    all_gather x1 -> x0, blocking collectives: 25.7 us -> none  [local(): img_all = lax.all_gather(image_embed, 'txt', axis=0, tiled=True)]
    pallas_call x0 -> x11, Pallas kernels: none -> 23.6 us  [call(): pl.pallas_call(body, out_shape=out_shape, in_specs=[scalars if i in smem...]
    all_to_all x0 -> x3, starting transfers between devices: none -> 17.4 us  [the longest x1 7.58 us: local(): txt = lax.all_to_all(spread, XY, 0, 0).reshape(cols, embed)]
  transfers between devices with their start and end apart: 3 -> 18, of which waited for: 1 -> 9; matrix products, arithmetic and copies ran while one was open for 2% -> 1% of each run, Pallas kernels for 0% -> 5%
where the time goes in v2:
time: 145 us
  starting transfers between devices  46.8 us (32%)
  waiting for transfers between devices  43.7 us (30%)
  Pallas kernels  23.6 us (16%)
  local copies, waits for them, and re-layouts  15 us (10%)
  blocking collectives  13.9 us (10%)
  between operations  1.55 us (1%)
    pallas_call x11, Pallas kernels, call(): pl.pallas_call(body, out_shape=out_shape, in_specs=[scalars if i in smem...  23.6 us
    ppermute x4, waiting for transfers between devices, ahead(): lax.ppermute(x, CZ, pairs + [(nz + i, nz + (i + k) % nz) for i in range(n...  20.4 us
    all_to_all x1, blocking collectives, local(): col_got = lax.all_to_all(msg, XY, 0, 0)  13.9 us
    unnamed x33, local copies, waits for them, and re-layouts  13.1 us
    ppermute x4, waiting for transfers between devices, onward(): lax.ppermute(x, CZ, pairs + [(nz + (i + k) % nz, nz + i) for i in range(n...  12.6 us
    ppermute x7, starting transfers between devices, swap(): return lax.ppermute(x, 'c', SWAP)  12.3 us
    ppermute x4, starting transfers between devices, ahead(): lax.ppermute(x, CZ, pairs + [(nz + i, nz + (i + k) % nz) for i in range(n...  9.01 us
    ppermute x4, starting transfers between devices, onward(): lax.ppermute(x, CZ, pairs + [(nz + (i + k) % nz, nz + i) for i in range(n...  8.09 us
  transfers between devices with their start and end apart: 18, of which 9 were waited for; matrix products, arithmetic and copies ran while one was open for 1% of the time, Pallas kernels for 5%

profile of v2, /device:TPU:1, one launch (start us, length us, event | category | flops | bytes accessed | tf_op | source)
XLA Modules:
  0.0 144.7 jit_solution(17288473630042490443)
XLA Ops:
  0.6 0.9 copy-done.6
  1.5 0.9 copy-done.7
  2.4 2.8 %shard_map.83 = (bf16[16,48,1280]{2,1,0:T(8,128)(2,1)S(1)}, bf16[48,1280]{1,0:T(8,128)(2,1)S(1)}) custom-call(bf16[48,1280]{1,0:T(8,128)(2,1)S(1)} %copy-done.6, bf16[48,1280]{1,0:T(8,128)(2,1)S(1)} %copy-done.7), custom_call_target="tpu_custom_call" | custom-call | bytes 245760 | tf_op jit(solution)/shard_map/pallas_call | solution.py:25
  5.3 1.3 copy-done.4
  6.6 7.6 %all-to-all-start = ((bf16[16,48,1280]{2,1,0:T(8,128)(2,1)}), bf16[16,48,1280]{2,1,0:T(8,128)(2,1)S(1)}, u32[]{:S(2)}, u32[]{:S(2)}) async-start(bf16[16,48,1280]{2,1,0:T(8,128)(2,1)} %copy-done.4), calls=%async_computation | async-start | bytes 3932160 | tf_op jit(solution)/shard_map/all_to_all | solution.py:316
  14.2 0.0 copy-start.15
  14.2 1.0 collective-permute-start
  15.3 1.0 collective-permute-done
  16.2 4.4 %collective-permute-start.3 = (bf16[96,1280]{1,0:T(8,128)(2,1)S(1)}, bf16[96,1280]{1,0:T(8,128)(2,1)S(1)}, u32[]{:S(2)}, u32[]{:S(2)}) collective-permute-start(bf16[96,1280]{1,0:T(8,128)(2,1)S(1)} %constant_dynamic-update-slice_fusion), channel_id=1, source_target_pairs={{3,0},{4,1},{5,2},{6,3},{7,4},{0,5},{1,6},{2,7},{8,11},{9,12},{10,... | collective-permute-start | bytes 737288 | tf_op jit(solution)/shard_map/ppermute | solution.py:301
  20.7 3.3 %collective-permute-start.2 = (bf16[96,1280]{1,0:T(8,128)(2,1)S(1)}, bf16[96,1280]{1,0:T(8,128)(2,1)S(1)}, u32[]{:S(2)}, u32[]{:S(2)}) collective-permute-start(bf16[96,1280]{1,0:T(8,128)(2,1)S(1)} %constant_dynamic-update-slice_fusion), channel_id=1, source_target_pairs={{2,0},{3,1},{4,2},{5,3},{6,4},{7,5},{0,6},{1,7},{8,10},{9,11},{10,... | collective-permute-start | bytes 737288 | tf_op jit(solution)/shard_map/ppermute | solution.py:301
  24.0 0.7 collective-permute-start.1
  24.7 0.5 collective-permute-start.4
  25.2 20.4 %collective-permute-done.4.refs_3_ = bf16[48,1280]{1,0:T(8,128)(2,1)S(1)} collective-permute-done((bf16[48,1280]{1,0:T(8,128)(2,1)S(1)}, bf16[48,1280]{1,0:T(8,128)(2,1)S(1)}, u32[]{:S(2)}, u32[]{:S(2)}) %collective-permute-start.4) | collective-permute-done | bytes 122912 | tf_op jit(solution)/shard_map/ppermute | solution.py:301
  45.6 0.0 collective-permute-done.3.refs_2_
  45.6 0.0 collective-permute-done.2.refs_1_
  45.6 1.3 shard_map.84.own
  46.9 0.1 collective-permute-start.5
  47.1 0.6 collective-permute-start.6
  47.7 0.1 pad_add_fusion.idx
  48.5 1.1 collective-permute-done.6
  49.6 0.1 collective-permute-done.5.oth
  49.7 1.3 copy-done
  51.1 1.5 %copy-done.1 = bf16[16,48,1280]{2,1,0:T(8,128)(2,1)S(1)} copy-done((bf16[16,48,1280]{2,1,0:T(8,128)(2,1)S(1)}, bf16[16,48,1280]{2,1,0:T(8,128)(2,1)}, u32[]{:S(2)}) %copy-start.1) | copy-done | bytes 1966104
  52.6 5.6 %shard_map.85 = (f32[768,768]{1,0:T(8,128)S(1)}, f32[16,24,128]{2,1,0:T(8,128)S(1)}) custom-call(s32[2]{0:T(128)S(1)} %pad_add_fusion.idx, f32[1]{0:T(128)} %bitcast.2.scale, bf16[384,1280]{1,0:T(8,128)(2,1)S(1)} %shard_map.84.own, bf16[384,1280]{1,0:T(8,128)(2,1)} %collective-permute-done.5.oth, bf16[768,1280]{1,0:T(8,128)(2,1)S(1)} %bitcast.12, ...), custom_call_target="tpu_custom_call" | custom-call | flops 1509949440 | bytes 3936268 | tf_op jit(solution)/shard_map/pallas_call | solution.py:25
  58.3 0.0 copy-start.5
  58.3 0.7 copy-done.5
  58.9 6.1 %all-to-all-start.1 = ((f32[16,24,128]{2,1,0:T(8,128)}), f32[16,24,128]{2,1,0:T(8,128)S(1)}, u32[]{:S(2)}, u32[]{:S(2)}) async-start(f32[16,24,128]{2,1,0:T(8,128)} %copy-done.5), calls=%async_computation.1 | async-start | bytes 393216 | tf_op jit(solution)/shard_map/all_to_all | solution.py:361
  65.1 0.6 copy-done.11
  65.7 1.8 %shard_map.86.stat = f32[24,128]{1,0:T(8,128)S(1)} custom-call(s32[2]{0:T(128)S(1)} %copy-done.11, f32[768,768]{1,0:T(8,128)S(1)} %get-tuple-element.30.logits, f32[8,128]{1,0:T(8,128)S(1)} %pad_bitcast_fusion.pairs), custom_call_target="tpu_custom_call" | custom-call | flops 4718592 | bytes 2363400 | tf_op jit(solution)/shard_map/pallas_call | solution.py:25
  67.5 5.8 %all-to-all-done.1.got = f32[16,24,128]{2,1,0:T(8,128)S(1)} async-done(((f32[16,24,128]{2,1,0:T(8,128)}), f32[16,24,128]{2,1,0:T(8,128)S(1)}, u32[]{:S(2)}, u32[]{:S(2)}) %all-to-all-start.1) | async-done | bytes 196640 | tf_op jit(solution)/shard_map/all_to_all | solution.py:361
  73.3 0.5 shard_map.87
  73.9 0.0 copy-start.8
  73.9 13.9 %all_to_all.20.got = f32[16,24,128]{2,1,0:T(8,128)S(1)} all-to-all(f32[16,24,128]{2,1,0:T(8,128)S(1)} %get-tuple-element.32), channel_id=1, replica_groups=mesh['y'=4,'x'=4,'c'=2,'z'=8] {'y','x'}, dimensions={0} | all-to-all | bytes 393216 | tf_op jit(solution)/shard_map/all_to_all | solution.py:380
  87.8 0.7 copy-done.12
  88.4 7.0 %shard_map.88 = (bf16[768,768]{1,0:T(8,128)(2,1)S(1)}, bf16[768,1280]{1,0:T(8,128)(2,1)S(1)}, f32[8,128]{1,0:T(8,128)S(1)}, f32[8,128]{1,0:T(8,128)S(1)}) custom-call(s32[2]{0:T(128)S(1)} %copy-done.12, f32[1]{0:T(128)} %bitcast.2.scale, f32[16,24,128]{2,1,0:T(8,128)S(1)} %all_to_all.20.got, f32[768,768]{1,0:T(8,128)S(1)} %get-tuple-element.30.logits, ...), custom_call_target="tpu_custom_call" | custom-call | flops 1509949440 | bytes 4530188 | tf_op jit(solution)/shard_map/pallas_call | solution.py:25
  95.4 1.3 copy-done.3
  96.7 1.1 copy-done.13
  97.8 3.7 %all-to-all-start.3 = ((bf16[16,48,1280]{2,1,0:T(8,128)(2,1)}), bf16[16,48,1280]{2,1,0:T(8,128)(2,1)S(1)}, u32[]{:S(2)}, u32[]{:S(2)}) async-start(bf16[16,48,1280]{2,1,0:T(8,128)(2,1)} %bitcast.14), calls=%async_computation.3 | async-start | bytes 3932160 | tf_op jit(solution)/shard_map/all_to_all | solution.py:399
  101.5 1.5 %copy-done.2 = bf16[16,48,1280]{2,1,0:T(8,128)(2,1)S(1)} copy-done((bf16[16,48,1280]{2,1,0:T(8,128)(2,1)S(1)}, bf16[16,48,1280]{2,1,0:T(8,128)(2,1)}, u32[]{:S(2)}) %copy-start.2) | copy-done | bytes 1966104
  103.0 1.3 copy-done.14
  104.3 2.5 %shard_map.89 = (f32[384,1280]{1,0:T(8,128)S(1)}, bf16[384,1280]{1,0:T(8,128)(2,1)S(1)}) custom-call(bf16[768,768]{1,0:T(8,128)(2,1)S(1)} %copy-done.14, bf16[768,1280]{1,0:T(8,128)(2,1)S(1)} %bitcast.13), custom_call_target="tpu_custom_call" | custom-call | flops 1509949440 | bytes 3145728 | tf_op jit(solution)/shard_map/pallas_call | solution.py:25
  106.9 2.5 %collective-permute-start.9 = (bf16[384,1280]{1,0:T(8,128)(2,1)S(1)}, bf16[384,1280]{1,0:T(8,128)(2,1)S(1)}, u32[]{:S(2)}, u32[]{:S(2)}) collective-permute-start(bf16[384,1280]{1,0:T(8,128)(2,1)S(1)} %get-tuple-element.38), channel_id=1, source_target_pairs={{0,8},{8,0},{1,9},{9,1},{2,10},{10,2},{3,11},{11,3},{4,12},{12,4},... | collective-permute-start | bytes 2949128 | tf_op jit(solution)/shard_map/ppermute | solution.py:297
  109.3 0.1 collective-permute-start.8
  109.4 2.1 %collective-permute-done.8.other_sums = f32[8,128]{1,0:T(8,128)S(1)} collective-permute-done((f32[8,128]{1,0:T(8,128)S(1)}, f32[8,128]{1,0:T(8,128)S(1)}, u32[]{:S(2)}, u32[]{:S(2)}) %collective-permute-start.8) | collective-permute-done | bytes 4128 | tf_op jit(solution)/shard_map/ppermute | solution.py:297
  111.5 0.0 collective-permute-done.9.received
  111.5 0.2 shard_map.90
  111.7 1.9 %collective-permute-start.10 = (bf16[96,1408]{1,0:T(8,128)(2,1)S(1)}, bf16[96,1408]{1,0:T(8,128)(2,1)S(1)}, u32[]{:S(2)}, u32[]{:S(2)}) collective-permute-start(bf16[96,1408]{1,0:T(8,128)(2,1)S(1)} %get-tuple-element.40), channel_id=1, source_target_pairs={{0,1},{1,2},{2,3},{3,4},{4,5},{5,6},{6,7},{7,0},{9,8},{10,9},{11,1... | collective-permute-start | bytes 811016 | tf_op jit(solution)/shard_map/ppermute | solution.py:305
  113.6 0.6 collective-permute-start.11
  114.2 3.2 %collective-permute-start.12 = (bf16[96,1408]{1,0:T(8,128)(2,1)S(1)}, bf16[96,1408]{1,0:T(8,128)(2,1)S(1)}, u32[]{:S(2)}, u32[]{:S(2)}) collective-permute-start(bf16[96,1408]{1,0:T(8,128)(2,1)S(1)} %get-tuple-element.42), channel_id=1, source_target_pairs={{0,3},{1,4},{2,5},{3,6},{4,7},{5,0},{6,1},{7,2},{11,8},{12,9},{13,... | collective-permute-start | bytes 811016 | tf_op jit(solution)/shard_map/ppermute | solution.py:305
  117.5 2.3 %collective-permute-start.13 = (bf16[48,1408]{1,0:T(8,128)(2,1)S(1)}, bf16[48,1408]{1,0:T(8,128)(2,1)S(1)}, u32[]{:S(2)}, u32[]{:S(2)}) collective-permute-start(bf16[48,1408]{1,0:T(8,128)(2,1)S(1)} %get-tuple-element.43), channel_id=1, source_target_pairs={{0,4},{1,5},{2,6},{3,7},{4,0},{5,1},{6,2},{7,3},{12,8},{13,9},{14,... | collective-permute-start | bytes 405512 | tf_op jit(solution)/shard_map/ppermute | solution.py:305
  119.8 10.7 %collective-permute-done.13.refs_3_ = bf16[48,1408]{1,0:T(8,128)(2,1)S(1)} collective-permute-done((bf16[48,1408]{1,0:T(8,128)(2,1)S(1)}, bf16[48,1408]{1,0:T(8,128)(2,1)S(1)}, u32[]{:S(2)}, u32[]{:S(2)}) %collective-permute-start.13) | collective-permute-done | bytes 135200 | tf_op jit(solution)/shard_map/ppermute | solution.py:305
  130.6 1.9 %collective-permute-done.12.refs_2_ = bf16[96,1408]{1,0:T(8,128)(2,1)S(1)} collective-permute-done((bf16[96,1408]{1,0:T(8,128)(2,1)S(1)}, bf16[96,1408]{1,0:T(8,128)(2,1)S(1)}, u32[]{:S(2)}, u32[]{:S(2)}) %collective-permute-start.12) | collective-permute-done | bytes 270368 | tf_op jit(solution)/shard_map/ppermute | solution.py:305
  132.4 0.1 shard_map.91
  132.6 7.9 %collective-permute-start.14 = (f32[48,1408]{1,0:T(8,128)S(1)}, f32[48,1408]{1,0:T(8,128)S(1)}, u32[]{:S(2)}, u32[]{:S(2)}) collective-permute-start(f32[48,1408]{1,0:T(8,128)S(1)} %get-tuple-element.45), channel_id=1, source_target_pairs={{0,8},{8,0},{1,9},{9,1},{2,10},{10,2},{3,11},{11,3},{4,12},{12,4},... | collective-permute-start | bytes 811016 | tf_op jit(solution)/shard_map/ppermute | solution.py:297
  140.5 0.1 reshape.33
  140.6 0.0 collective-permute-start.7
  140.6 0.6 dynamic-slice_bitcast_fusion
  141.2 0.6 collective-permute-done.7
  141.8 0.7 select_n.71
  142.5 0.0 collective-permute-done.14.received
  142.5 0.7 shard_map.92
  143.2 0.5 slice.7
  143.7 0.0 all-to-all-done.3.got
  143.7 0.9 shard_map.93
  (28 shorter events, 0.2 us)
Async XLA Ops:
  0.6 0.9 copy-start.6
  1.5 0.9 copy-start.7
  5.3 1.3 copy-start.4
  6.6 43.1 %all-to-all-start = ((bf16[16,48,1280]{2,1,0:T(8,128)(2,1)}), bf16[16,48,1280]{2,1,0:T(8,128)(2,1)S(1)}, u32[]{:S(2)}, u32[]{:S(2)}) async-start(bf16[16,48,1280]{2,1,0:T(8,128)(2,1)} %copy-done.4), calls=%async_computation | async-start | bytes 3932160 | tf_op jit(solution)/shard_map/all_to_all | solution.py:316
  14.2 32.9 %copy-start.15 = (s32[384]{0:T(512)S(1)}, s32[384]{0:T(512)}, u32[]{:S(2)}) copy-start(s32[384]{0:T(512)} %param.6) | copy-start | bytes 4612
  14.2 2.0 %collective-permute-start = (bf16[48,1280]{1,0:T(8,128)(2,1)S(1)}, bf16[48,1280]{1,0:T(8,128)(2,1)S(1)}, u32[]{:S(2)}, u32[]{:S(2)}) collective-permute-start(bf16[48,1280]{1,0:T(8,128)(2,1)S(1)} %get-tuple-element.27.refs_4_), channel_id=1, source_target_pairs={{0,8},{8,0},{1,9},{9,1},{2,10},{10,2},{3,11},{11,3},{4,12},{12,4},... | collective-permute-start | bytes 368648 | tf_op jit(solution)/shard_map/ppermute | solution.py:297
  16.2 29.4 %collective-permute-start.3 = (bf16[96,1280]{1,0:T(8,128)(2,1)S(1)}, bf16[96,1280]{1,0:T(8,128)(2,1)S(1)}, u32[]{:S(2)}, u32[]{:S(2)}) collective-permute-start(bf16[96,1280]{1,0:T(8,128)(2,1)S(1)} %constant_dynamic-update-slice_fusion), channel_id=1, source_target_pairs={{3,0},{4,1},{5,2},{6,3},{7,4},{0,5},{1,6},{2,7},{8,11},{9,12},{10,... | collective-permute-start | bytes 737288 | tf_op jit(solution)/shard_map/ppermute | solution.py:301
  20.7 25.0 %collective-permute-start.2 = (bf16[96,1280]{1,0:T(8,128)(2,1)S(1)}, bf16[96,1280]{1,0:T(8,128)(2,1)S(1)}, u32[]{:S(2)}, u32[]{:S(2)}) collective-permute-start(bf16[96,1280]{1,0:T(8,128)(2,1)S(1)} %constant_dynamic-update-slice_fusion), channel_id=1, source_target_pairs={{2,0},{3,1},{4,2},{5,3},{6,4},{7,5},{0,6},{1,7},{8,10},{9,11},{10,... | collective-permute-start | bytes 737288 | tf_op jit(solution)/shard_map/ppermute | solution.py:301
  24.0 21.7 %collective-permute-start.1 = (bf16[96,1280]{1,0:T(8,128)(2,1)S(1)}, bf16[96,1280]{1,0:T(8,128)(2,1)S(1)}, u32[]{:S(2)}, u32[]{:S(2)}) collective-permute-start(bf16[96,1280]{1,0:T(8,128)(2,1)S(1)} %constant_dynamic-update-slice_fusion), channel_id=1, source_target_pairs={{1,0},{2,1},{3,2},{4,3},{5,4},{6,5},{7,6},{0,7},{8,9},{9,10},{10,1... | collective-permute-start | bytes 737288 | tf_op jit(solution)/shard_map/ppermute | solution.py:301
  24.7 20.9 %collective-permute-start.4 = (bf16[48,1280]{1,0:T(8,128)(2,1)S(1)}, bf16[48,1280]{1,0:T(8,128)(2,1)S(1)}, u32[]{:S(2)}, u32[]{:S(2)}) collective-permute-start(bf16[48,1280]{1,0:T(8,128)(2,1)S(1)} %get-tuple-element.27.refs_4_), channel_id=1, source_target_pairs={{4,0},{5,1},{6,2},{7,3},{0,4},{1,5},{2,6},{3,7},{8,12},{9,13},{10,... | collective-permute-start | bytes 368648 | tf_op jit(solution)/shard_map/ppermute | solution.py:301
  46.9 2.8 %collective-permute-start.5 = (bf16[384,1280]{1,0:T(8,128)(2,1)S(1)}, bf16[384,1280]{1,0:T(8,128)(2,1)}, u32[]{:S(2)}, u32[]{:S(2)}) collective-permute-start(bf16[384,1280]{1,0:T(8,128)(2,1)S(1)} %shard_map.84.own), channel_id=1, source_target_pairs={{0,8},{8,0},{1,9},{9,1},{2,10},{10,2},{3,11},{11,3},{4,12},{12,4},... | collective-permute-start | bytes 2949128 | tf_op jit(solution)/shard_map/ppermute | solution.py:297
  47.1 2.5 %collective-permute-start.6 = (f32[384]{0:T(512)S(1)}, f32[384]{0:T(512)S(1)}, u32[]{:S(2)}, u32[]{:S(2)}) collective-permute-start(f32[384]{0:T(512)S(1)} %and_select_fusion), channel_id=1, source_target_pairs={{0,8},{8,0},{1,9},{9,1},{2,10},{10,2},{3,11},{11,3},{4,12},{12,4},... | collective-permute-start | bytes 4616 | tf_op jit(solution)/shard_map/ppermute | solution.py:297
  47.8 10.5 %copy-start.10 = (s32[2]{0:T(128)}, s32[2]{0:T(128)S(1)}, u32[]{:S(2)}) copy-start(s32[2]{0:T(128)S(1)} %pad_add_fusion.idx) | copy-start | bytes 28
  49.7 1.3 copy-start
  51.1 1.5 %copy-start.1 = (bf16[16,48,1280]{2,1,0:T(8,128)(2,1)S(1)}, bf16[16,48,1280]{2,1,0:T(8,128)(2,1)}, u32[]{:S(2)}) copy-start(bf16[16,48,1280]{2,1,0:T(8,128)(2,1)} %copy-done) | copy-start | bytes 5898244
  58.3 0.7 copy-start.5
  58.9 14.4 %all-to-all-start.1 = ((f32[16,24,128]{2,1,0:T(8,128)}), f32[16,24,128]{2,1,0:T(8,128)S(1)}, u32[]{:S(2)}, u32[]{:S(2)}) async-start(f32[16,24,128]{2,1,0:T(8,128)} %copy-done.5), calls=%async_computation.1 | async-start | bytes 393216 | tf_op jit(solution)/shard_map/all_to_all | solution.py:361
  65.1 0.7 copy-start.11
  73.9 13.9 %copy-start.8 = (f32[8,128]{1,0:T(8,128)}, f32[8,128]{1,0:T(8,128)S(1)}, u32[]{:S(2)}) copy-start(f32[8,128]{1,0:T(8,128)S(1)} %get-tuple-element.31) | copy-start | bytes 12292
  87.8 0.7 copy-start.12
  95.4 1.3 copy-start.3
  96.7 1.1 copy-start.13
  97.8 46.0 %all-to-all-start.3 = ((bf16[16,48,1280]{2,1,0:T(8,128)(2,1)}), bf16[16,48,1280]{2,1,0:T(8,128)(2,1)S(1)}, u32[]{:S(2)}, u32[]{:S(2)}) async-start(bf16[16,48,1280]{2,1,0:T(8,128)(2,1)} %bitcast.14), calls=%async_computation.3 | async-start | bytes 3932160 | tf_op jit(solution)/shard_map/all_to_all | solution.py:399
  101.5 1.5 %copy-start.2 = (bf16[16,48,1280]{2,1,0:T(8,128)(2,1)S(1)}, bf16[16,48,1280]{2,1,0:T(8,128)(2,1)}, u32[]{:S(2)}) copy-start(bf16[16,48,1280]{2,1,0:T(8,128)(2,1)} %copy-done) | copy-start | bytes 5898244
  103.0 1.3 copy-start.14
  106.9 4.7 %collective-permute-start.9 = (bf16[384,1280]{1,0:T(8,128)(2,1)S(1)}, bf16[384,1280]{1,0:T(8,128)(2,1)S(1)}, u32[]{:S(2)}, u32[]{:S(2)}) collective-permute-start(bf16[384,1280]{1,0:T(8,128)(2,1)S(1)} %get-tuple-element.38), channel_id=1, source_target_pairs={{0,8},{8,0},{1,9},{9,1},{2,10},{10,2},{3,11},{11,3},{4,12},{12,4},... | collective-permute-start | bytes 2949128 | tf_op jit(solution)/shard_map/ppermute | solution.py:297
  109.3 2.2 %collective-permute-start.8 = (f32[8,128]{1,0:T(8,128)S(1)}, f32[8,128]{1,0:T(8,128)S(1)}, u32[]{:S(2)}, u32[]{:S(2)}) collective-permute-start(f32[8,128]{1,0:T(8,128)S(1)} %get-tuple-element.35.sums), channel_id=1, source_target_pairs={{0,8},{8,0},{1,9},{9,1},{2,10},{10,2},{3,11},{11,3},{4,12},{12,4},... | collective-permute-start | bytes 12296 | tf_op jit(solution)/shard_map/ppermute | solution.py:297
  111.5 29.1 %copy-start.9 = (f32[8,128]{1,0:T(8,128)S(1)}, f32[8,128]{1,0:T(8,128)}, u32[]{:S(2)}) copy-start(f32[8,128]{1,0:T(8,128)} %copy-done.8) | copy-start | bytes 12292
  111.7 18.8 %collective-permute-start.10 = (bf16[96,1408]{1,0:T(8,128)(2,1)S(1)}, bf16[96,1408]{1,0:T(8,128)(2,1)S(1)}, u32[]{:S(2)}, u32[]{:S(2)}) collective-permute-start(bf16[96,1408]{1,0:T(8,128)(2,1)S(1)} %get-tuple-element.40), channel_id=1, source_target_pairs={{0,1},{1,2},{2,3},{3,4},{4,5},{5,6},{6,7},{7,0},{9,8},{10,9},{11,1... | collective-permute-start | bytes 811016 | tf_op jit(solution)/shard_map/ppermute | solution.py:305
  113.6 16.9 %collective-permute-start.11 = (bf16[96,1408]{1,0:T(8,128)(2,1)S(1)}, bf16[96,1408]{1,0:T(8,128)(2,1)S(1)}, u32[]{:S(2)}, u32[]{:S(2)}) collective-permute-start(bf16[96,1408]{1,0:T(8,128)(2,1)S(1)} %get-tuple-element.41), channel_id=1, source_target_pairs={{0,2},{1,3},{2,4},{3,5},{4,6},{5,7},{6,0},{7,1},{10,8},{11,9},{12,... | collective-permute-start | bytes 811016 | tf_op jit(solution)/shard_map/ppermute | solution.py:305
  114.2 18.2 %collective-permute-start.12 = (bf16[96,1408]{1,0:T(8,128)(2,1)S(1)}, bf16[96,1408]{1,0:T(8,128)(2,1)S(1)}, u32[]{:S(2)}, u32[]{:S(2)}) collective-permute-start(bf16[96,1408]{1,0:T(8,128)(2,1)S(1)} %get-tuple-element.42), channel_id=1, source_target_pairs={{0,3},{1,4},{2,5},{3,6},{4,7},{5,0},{6,1},{7,2},{11,8},{12,9},{13,... | collective-permute-start | bytes 811016 | tf_op jit(solution)/shard_map/ppermute | solution.py:305
  117.5 13.1 %collective-permute-start.13 = (bf16[48,1408]{1,0:T(8,128)(2,1)S(1)}, bf16[48,1408]{1,0:T(8,128)(2,1)S(1)}, u32[]{:S(2)}, u32[]{:S(2)}) collective-permute-start(bf16[48,1408]{1,0:T(8,128)(2,1)S(1)} %get-tuple-element.43), channel_id=1, source_target_pairs={{0,4},{1,5},{2,6},{3,7},{4,0},{5,1},{6,2},{7,3},{12,8},{13,9},{14,... | collective-permute-start | bytes 405512 | tf_op jit(solution)/shard_map/ppermute | solution.py:305
  132.6 9.9 %collective-permute-start.14 = (f32[48,1408]{1,0:T(8,128)S(1)}, f32[48,1408]{1,0:T(8,128)S(1)}, u32[]{:S(2)}, u32[]{:S(2)}) collective-permute-start(f32[48,1408]{1,0:T(8,128)S(1)} %get-tuple-element.45), channel_id=1, source_target_pairs={{0,8},{8,0},{1,9},{9,1},{2,10},{10,2},{3,11},{11,3},{4,12},{12,4},... | collective-permute-start | bytes 811016 | tf_op jit(solution)/shard_map/ppermute | solution.py:297
  140.6 1.2 collective-permute-start.7

commit v3 on v0

v3 whole, which is shorter than its diff:
```python
import functools

import jax
import jax.numpy as jnp
from jax import lax
from jax.experimental import pallas as pl
from jax.experimental.pallas import tpu as pltpu
from jax.sharding import Mesh, PartitionSpec as P

NY, NX, NC = 4, 4, 2
XY = ("y", "x")
CZ = ("c", "z")
SWAP = [(0, 1), (1, 0)]
LANES = 128
VMEM_BYTES = 64 * 1024 * 1024
F32 = jnp.float32
BF16 = jnp.bfloat16


class Loaded:
    def __init__(self, source, ref, sems, cut):
        self.ref = ref
        self.started = []
        axis, size = cut
        for i, at in enumerate(range(0, ref.shape[axis], size)):
            window = (slice(None),) * axis + (slice(at, at + size),)
            self.started.append(pltpu.make_async_copy(source.at[window], ref.at[window], sems.at[i]))

    def start(self):
        for copy in self.started:
            copy.start()

    def part(self, i):
        self.started[i].wait()

    def get(self):
        for i in range(len(self.started)):
            self.part(i)
        return self.ref


class Joined(Loaded):
    def __init__(self, sources, ref, sems):
        self.ref = ref
        self.started = []
        at = 0
        for i, source in enumerate(sources):
            size = source.shape[0]
            self.started.append(pltpu.make_async_copy(source, ref.at[at : at + size], sems.at[i]))
            at += size


class Sender:
    def __init__(self, sems):
        self.sems = sems
        self.started = []

    def send(self, source, target):
        copy = pltpu.make_async_copy(source, target, self.sems.at[len(self.started)])
        copy.start()
        self.started.append(copy)

    def finish(self):
        for copy in self.started:
            copy.wait()


def call(body, out_shape, *args, flops=0, smem=(), scratch=(), cuts=(), joined=None, held=None, sends=16):
    many = isinstance(out_shape, tuple)
    shapes = out_shape if many else (out_shape,)
    held = [x if held is None or held[i] is None else held[i] for i, x in enumerate(shapes)]
    cuts = dict(cuts)
    joined = len(args) if joined is None else joined
    arrays = [i for i in range(joined) if i not in smem]
    plan = [cuts.get(i, (0, args[i].shape[0])) for i in arrays]
    counts = [-(-args[i].shape[axis] // size) for i, (axis, size) in zip(arrays, plan)]
    buffers_of = [pltpu.VMEM(args[i].shape, args[i].dtype) for i in arrays]
    if joined < len(args):
        counts.append(len(args) - joined)
        last = args[-1]
        buffers_of.append(pltpu.VMEM((sum(a.shape[0] for a in args[joined:]), last.shape[1]), last.dtype))

    def kernel(*refs):
        ins, refs = refs[: len(args)], refs[len(args) :]
        outs, refs = refs[: len(shapes)], refs[len(shapes) :]
        buffers, refs = refs[: len(buffers_of)], refs[len(buffers_of) :]
        spare, refs = refs[: len(held)], refs[len(held) :]
        in_sems, refs = refs[: len(counts)], refs[len(counts) :]
        out_sems, refs = refs[0], refs[1:]
        given = list(ins[:joined])
        for j, i in enumerate(arrays):
            given[i] = Loaded(ins[i], buffers[j], in_sems[j], plan[j])
            given[i].start()
        if joined < len(args):
            given.append(Joined(ins[joined:], buffers[-1], in_sems[-1]))
            given[-1].start()
        sender = Sender(out_sems)
        body(given, spare, outs, sender, *refs)
        sender.finish()

    far = pl.BlockSpec(memory_space=pltpu.HBM)
    scalars = pl.BlockSpec(memory_space=pltpu.SMEM)
    size = sum(a.size * a.dtype.itemsize for a in args)
    return pl.pallas_call(
        kernel,
        out_shape=out_shape,
        in_specs=[scalars if i in smem else far for i in range(len(args))],
        out_specs=tuple(far for _ in shapes) if many else far,
        scratch_shapes=[
            *buffers_of,
            *[pltpu.VMEM(x.shape, x.dtype) for x in held],
            *[pltpu.SemaphoreType.DMA((n,)) for n in counts],
            pltpu.SemaphoreType.DMA((sends,)),
            *scratch,
        ],
        cost_estimate=pl.CostEstimate(flops=flops, bytes_accessed=size, transcendentals=0),
        compiler_params=pltpu.CompilerParams(vmem_limit_bytes=VMEM_BYTES),
    )(*args)


def near(body, out_shape, *args, smem=(), unread=()):
    spec = lambda i: pl.BlockSpec(memory_space=pltpu.SMEM if i in smem else pltpu.HBM if i in unread else pltpu.VMEM)
    many = isinstance(out_shape, tuple)
    vmem = pl.BlockSpec(memory_space=pltpu.VMEM)
    return pl.pallas_call(
        body,
        out_shape=out_shape,
        in_specs=[spec(i) for i in range(len(args))],
        out_specs=tuple(vmem for _ in out_shape) if many else vmem,
        compiler_params=pltpu.CompilerParams(vmem_limit_bytes=8 * 1024 * 1024),
    )(*args)


def dot(a, b, dims):
    return lax.dot_general(a, b, (dims, ((), ())), preferred_element_type=F32)


def pack(rows):
    tiles = []
    for row in rows:
        n = row.shape[1] // LANES
        tiles += [row[:, q * LANES : (q + 1) * LANES] for q in range(n)]
        tiles += [jnp.zeros((8 - n, LANES), F32)]
    return jnp.concatenate(tiles, axis=0)


def unpack(tile, n):
    return jnp.concatenate([tile[q : q + 1] for q in range(n)], axis=1)


def order_of(nz):
    first = [(who, k) for k in range(1, nz // 2) for who in (0, 1)] + [(0, nz // 2), (0, 0)]
    return first + [(1 - who, -k) for who, k in first]


def row_at(idx, block, nz, part):
    who, k = block
    c, z = idx[0], idx[1]
    core = c if who == 0 else 1 - c
    step = k * (1 - 2 * c)
    return pl.multiple_of((core * nz + lax.rem(z + step + nz, nz)) * part, 16)


def tall(rows):
    return jnp.concatenate(rows + [rows[-1]] * (8 - len(rows)), axis=0).T


def logits_kernel(nz, ins, held, outs, sender, column, stat):
    idx, scale, pairs, txt, images = ins
    logits, row_out, packed = held
    rows, cols = logits.shape
    part = rows // (NC * nz)
    s = scale[0]
    column[...] = tall([unpack(pairs.get(), rows // LANES)])
    images = images.get()
    for i, n in enumerate(range(0, cols, 256)):
        txt.part(i)
        for m in range(0, rows, 384):
            block = dot(images[m : m + 384, :], txt.ref[n : n + 256, :], ((1,), (1,)))
            logits[m : m + 384, n : n + 256] = s * block
    sender.send(logits, outs[0])

    def fold(x):
        return x.reshape(part // 8, 8, cols)

    col_top = jnp.full((8, cols), -jnp.inf, F32)
    col_pos = jnp.zeros((8, cols), F32)
    lane = lax.broadcasted_iota(jnp.int32, (part, LANES), 1)
    for i, block in enumerate(order_of(nz)):
        x = logits[i * part : (i + 1) * part, :]
        col_top = jnp.maximum(col_top, jnp.max(fold(x), axis=0))
        at = pl.ds(row_at(idx, block, nz, part), part)
        hit = lax.broadcasted_iota(jnp.int32, x.shape, 1) == column[at, 0:1].astype(jnp.int32)
        paired = jnp.where(hit, x, 0.0)
        col_pos += jnp.sum(fold(paired), axis=0)
        pos = jnp.sum(paired, axis=1, keepdims=True)
        top = jnp.max(x, axis=1, keepdims=True)
        e = jnp.exp(x - top)
        total = jnp.sum(e, axis=1, keepdims=True)
        mean = jnp.sum(e * x, axis=1, keepdims=True) / total
        lse = top + jnp.log(total)
        stat[at, :] = jnp.where(lane == 0, lse, jnp.where(lane == 1, mean, jnp.where(lane == 2, pos, 0.0)))
    flat = stat[...].T
    row_out[...] = pack([flat[0:1], flat[1:2], flat[2:3]])
    sender.send(row_out, outs[1])

    top = jnp.max(col_top, axis=0, keepdims=True)
    total = moment = jnp.zeros((8, cols), F32)
    for i in range(NC * nz):
        x = logits[i * part : (i + 1) * part, :]
        e = jnp.exp(x - top)
        total += jnp.sum(fold(e), axis=0)
        moment += jnp.sum(fold(e * x), axis=0)
    total = jnp.sum(total, axis=0, keepdims=True)
    moment = jnp.sum(moment, axis=0, keepdims=True)
    pos = jnp.sum(col_pos, axis=0, keepdims=True)
    packed[...] = pack([top + jnp.log(total), moment / total, pos])
    for p in range(outs[2].shape[0]):
        sender.send(packed, outs[2].at[p])


def merge(got):
    lse = [x[0:8, :] for x in got]
    top = functools.reduce(jnp.maximum, lse)
    weight = [jnp.exp(x - top) for x in lse]
    total = sum(weight)
    mean = sum(w * x[8:16, :] for w, x in zip(weight, got)) / total
    return top + jnp.log(total), mean, sum(x[16:24, :] for x in got)


def total_of(x):
    return jnp.sum(jnp.sum(x, axis=1, keepdims=True), axis=0, keepdims=True)


def split_tail(total, size):
    high = total.astype(BF16)
    rest = total - high.astype(F32)
    middle = rest.astype(BF16)
    low = (rest - middle.astype(F32)).astype(BF16)
    lane = lax.broadcasted_iota(jnp.int32, (size, LANES), 1)
    tail = jnp.where(lane == 0, high.astype(F32), jnp.where(lane == 1, middle.astype(F32), low.astype(F32)))
    return tail.astype(BF16)


def tail_of(ref, embed):
    tail = ref[0:16, embed:].astype(F32)[0:8]
    lane = lax.broadcasted_iota(jnp.int32, tail.shape, 1)
    return jnp.sum(jnp.where(lane < 3, tail, 0.0), axis=1, keepdims=True)


def grad_kernel(count, nz, ins, held, outs, sender, column, grad, turned):
    idx, scale, col_got, chip, across, mine, theirs, pairs, logits, txt, images = ins
    text, send, first, row_loss, col_loss, sums = held
    half, embed = send.shape
    rows, cols = grad.shape
    part = rows // (NC * nz)
    s = scale[0]
    used = lax.broadcasted_iota(jnp.int32, (8, LANES), 0) < count
    row_lse, row_mean, row_pos = merge([r.get()[...] for r in (chip, across, mine, theirs)])
    row_loss[...] = row_lse - row_pos
    sender.send(row_loss, outs[3])
    row_total = total_of(jnp.where(used, 0.5 * row_mean - row_pos, 0.0))
    col_ref = col_got.get()
    col_lse, col_mean, col_pos = merge([col_ref[p] for p in range(col_ref.shape[0])])
    col_loss[...] = col_lse - col_pos
    sender.send(col_loss, outs[4])
    col_total = total_of(jnp.where(used, 0.5 * col_mean, 0.0))
    sums[...] = jnp.broadcast_to(col_total, sums.shape)
    sender.send(sums, outs[5])
    text[:, embed:] = split_tail(jnp.broadcast_to(row_total, (1, LANES)), cols)
    sender.send(text.at[:, embed:], outs[0].at[:, embed:])
    flat = unpack(col_lse, count)
    column[...] = tall([unpack(row_lse, count), unpack(pairs.get(), count)])

    for i, block in enumerate(order_of(nz)):
        logits.part(i)
        x = logits.ref[i * part : (i + 1) * part, :]
        at = pl.ds(row_at(idx, block, nz, part), part)
        hit = lax.broadcasted_iota(jnp.int32, x.shape, 1) == column[at, 1:2].astype(jnp.int32)
        value = 0.5 * (jnp.exp(x - column[at, 0:1]) + jnp.exp(x - flat)) - jnp.where(hit, 1.0, 0.0)
        grad[i * part : (i + 1) * part, :] = (s * value).astype(BF16)
    first[...] = grad[:half, :]
    sender.send(first, outs[2])

    cuts = range(0, embed, 256)
    for i, n in enumerate(cuts):
        txt.part(i)
        send[:, n : n + 256] = dot(grad[half:, :], txt.ref[:, n : n + 256], ((1,), (0,))).astype(BF16)
        sender.send(send.at[:, n : n + 256], outs[1].at[:, n : n + 256])
    turned[...] = grad[...].T
    images = images.get()
    for n in cuts:
        text[:, n : n + 256] = dot(turned[...], images[:, n : n + 256], ((1,), (0,))).astype(BF16)
        sender.send(text.at[:, n : n + 256], outs[0].at[:, n : n + 256])


def image_kernel(ins, held, outs, sender):
    sums, other_sums, first, txt, received = ins
    total = sums.get()[0:1, :] + other_sums.get()[0:1, :]
    grad = first.get()
    embed = received.ref.shape[1]
    for i, n in enumerate(range(0, embed, 256)):
        txt.part(i)
        received.part(i)
        block = dot(grad[...], txt.ref[:, n : n + 256], ((1,), (0,)))
        block += received.ref[:, n : n + 256].astype(F32)
        at = 0
        for ref in held:
            size = ref.shape[0]
            ref[:, n : n + 256] = block[at : at + size].astype(ref.dtype)
            at += size
    for ref, out in zip(held, outs):
        if ref.shape[1] > embed:
            ref[:, embed:] = split_tail(total, ref.shape[0])
        sender.send(ref, out)


def forward_kernel(idx, sums, other_sums, own, near_one, far_one, out):
    part, embed = own.shape[0] // NC, own.shape[1]
    total = own[...] + near_one[:, :embed].astype(F32)
    out[:part, :embed] = (total[:part] + far_one[:, :embed].astype(F32)).astype(BF16)
    out[part:, :embed] = total[part:].astype(BF16)
    across = jnp.where(idx[0] == 0, 1.0, 0.0) * tail_of(far_one, embed)
    tail = sums[0:1, :] + other_sums[0:1, :] + tail_of(near_one, embed)[0:1] + across[0:1]
    out[:, embed:] = split_tail(tail, NC * part)


def chip_sum_kernel(sums, other_sums, own, one, two, row_total, *refs):
    keep, send = refs[-2], refs[-1]
    part, embed = own.shape
    total = one[:, :embed].astype(F32) + two[:, :embed].astype(F32)
    tail = tail_of(one, embed) + tail_of(two, embed)
    send[:, :embed] = total[part:]
    send[:, embed:] = jnp.zeros((part, LANES), F32)
    send[0:8, embed:] = jnp.broadcast_to(tail, (8, LANES))
    keep[:, :embed] = own[...] + total[:part]
    keep[:, embed:] = jnp.zeros((part, LANES), F32)
    keep[0:8, embed:] = tail + sums[...] + other_sums[...] + row_total[...]


def text_sum_kernel(got, out, total):
    embed = out.shape[1]
    out[...] = jnp.sum(got[:, :, :embed].astype(F32), axis=0)
    tail = sum(tail_of(got.at[p], embed) for p in range(got.shape[0]))
    total[...] = jnp.broadcast_to(tail, total.shape)


def image_sum_kernel(scale, keep, received, out, temp):
    embed = out.shape[1]
    out[...] = keep[:, :embed] + received[:, :embed]
    temp[...] = (keep[0:1, embed : embed + 1] + received[0:1, embed : embed + 1]) * scale[0]


def local(image_embed, text_embed, pair_col, log_scale):
    part, embed = image_embed.shape
    peers = NY * NX
    nz = lax.axis_size("z")
    half = nz * part
    rows, cols = NC * half, peers * part
    count = rows // LANES
    batch = peers * rows
    c = lax.axis_index("c")
    z = lax.axis_index("z")
    idx = jnp.stack([c, z])
    scale = jnp.exp(log_scale)
    scale1 = scale[None]
    sds = jax.ShapeDtypeStruct
    vmem = pltpu.VMEM
    last = nz // 2

    def swap(x):
        return lax.ppermute(x, "c", SWAP)

    def ahead(x, k):
        pairs = [((i + k) % nz, i) for i in range(nz)]
        return lax.ppermute(x, CZ, pairs + [(nz + i, nz + (i + k) % nz) for i in range(nz)])

    def onward(x, k):
        pairs = [(i, (i + k) % nz) for i in range(nz)]
        return lax.ppermute(x, CZ, pairs + [(nz + (i + k) % nz, nz + i) for i in range(nz)])

    spread = jnp.broadcast_to(text_embed[None], (peers, part, embed))
    txt = lax.all_to_all(spread, XY, 0, 0).reshape(cols, embed)
    partner = swap(image_embed)
    chip = jnp.concatenate([image_embed, partner])
    got = [ahead(chip, 1), ahead(chip, 2)]
    got += [ahead(got[1], 1), ahead(got[1][:part], 2)]
    images = got + [image_embed] + [swap(x) for x in got] + [partner]

    rem = pair_col % (cols * NC)
    block = rem // part
    ours = pair_col // (cols * NC) == z
    place = (block // NC * part + rem % part).astype(F32)
    mine = jnp.where(ours & (block % NC == c), place, -1.0)
    theirs = swap(jnp.where(ours & (block % NC == 1 - c), place, -1.0))
    pairs = jnp.where(c == 0, jnp.concatenate([mine, theirs]), jnp.concatenate([theirs, mine]))
    pairs = jnp.pad(pairs, (0, 8 * LANES - rows)).reshape(8, LANES)

    work = 2 * rows * cols * embed
    tile, pad = sds((24, LANES), F32), sds((8, LANES), F32)
    logits, stat, msg = call(
        functools.partial(logits_kernel, nz),
        (sds((rows, cols), F32), tile, sds((peers, 24, LANES), F32)),
        idx,
        scale1,
        pairs,
        txt,
        *images,
        flops=work,
        smem=(0, 1),
        cuts={3: (0, 256)},
        joined=4,
        held=(None, None, tile),
        sends=2 + peers,
        scratch=[vmem((rows, 8), F32), vmem((rows, LANES), F32)],
    )
    col_got = lax.all_to_all(msg, XY, 0, 0)
    chip_stat = jnp.concatenate(merge([stat, swap(stat)]))
    stats = [ahead(chip_stat, k) for k in range(last, 0, -1)]
    merged = jnp.concatenate(merge(stats[1:]))

    wide = embed + LANES
    text_term, send, first, row_loss, col_loss, sums = call(
        functools.partial(grad_kernel, count, nz),
        (sds((cols, wide), BF16), sds((half, embed), BF16), sds((half, cols), BF16), pad, pad, pad),
        idx,
        scale1,
        col_got,
        chip_stat,
        stats[0],
        merged,
        swap(merged),
        pairs,
        logits,
        txt,
        *images,
        flops=2 * work,
        smem=(0, 1),
        cuts={8: (0, part), 9: (1, 256)},
        joined=10,
        sends=5 + 2 * (embed // 256),
        scratch=[vmem((rows, 8), F32), vmem((rows, cols), BF16), vmem((cols, rows), BF16)],
    )
    received = swap(send)
    other_sums = swap(sums)
    text_got = lax.all_to_all(text_term.reshape(peers, part, wide), XY, 0, 0)
    one, two, three, four, own = call(
        image_kernel,
        (
            sds((NC * part, wide), BF16),
            sds((NC * part, embed), F32),
            sds((NC * part, wide), BF16),
            sds((part, wide), BF16),
            sds((part, embed), F32),
        ),
        sums,
        other_sums,
        first,
        txt,
        received,
        flops=work // 2,
        cuts={3: (1, 256), 4: (1, 256)},
    )
    two = near(
        forward_kernel,
        sds((NC * part, wide), BF16),
        idx,
        sums,
        other_sums,
        two,
        onward(three, 1),
        onward(four, 2),
        smem=(0,),
    )
    row_loss = lax.dynamic_slice(row_loss, (c * (count // NC), 0), (count // NC, LANES)).reshape(-1)
    col_loss = col_loss[:count].reshape(peers, 1, part)
    other = swap(col_loss)
    col_loss = jnp.where(
        c == 0, jnp.concatenate([col_loss, other], 1), jnp.concatenate([other, col_loss], 1)
    ).reshape(-1)
    grad_text, row_total = near(text_sum_kernel, (sds((part, embed), F32), pad), text_got)
    keep, send = near(
        chip_sum_kernel,
        (sds((part, wide), F32), sds((part, wide), F32)),
        sums,
        other_sums,
        own,
        onward(one, 1),
        onward(two, 2),
        row_total,
        row_loss,
        col_loss,
        unread=(6, 7),
    )
    grad_image, temp = near(
        image_sum_kernel,
        (sds((part, embed), F32), sds((1, 1), F32)),
        jnp.full((1,), 1.0 / batch, F32),
        keep,
        swap(send),
        smem=(0,),
    )
    return (row_loss, col_loss, grad_image, grad_text, temp[0, 0])


def solution(mesh):
    nz = mesh.shape["txt"]
    grid = Mesh(mesh.devices.reshape(NY, NX, NC, nz), ("y", "x", "c", "z"))
    images, texts = ("y", "x", "c", "z"), ("z", "y", "x", "c")
    in_specs = (P(images, None), P(texts, None), P(("y", "x", "c")), P())
    out_specs = (P(("y", "x", "c")), P("z"), P(images, None), P(texts, None), P())
    return jax.shard_map(local, mesh=grid, in_specs=in_specs, out_specs=out_specs, check_vma=False)
```

time: 409 us -> 127 us (0.31)
  blocking collectives: 337 us -> 0 us
  starting transfers between devices: 0.12 us -> 60.8 us
  Pallas kernels: 0 us -> 28.4 us
  matrix products: 15.6 us -> 0 us
  between operations: 16.3 us -> 1.61 us
  local copies, waits for them, and re-layouts: 0.01 us -> 11.1 us
  waiting for transfers between devices: 32 us -> 23 us
    psum x5 -> x0, blocking collectives: 234 us -> none  [the longest x2 134 us: local(): lax.psum((jnp.sum(jnp.exp(logits - col_max[None, :]), axis=0), col_part),...]
    pmax x2 -> x0, blocking collectives: 77.1 us -> none  [the longest x1 63.3 us: local(): col_max = lax.pmax(jnp.max(logits, axis=0), 'img')]
    ppermute x0 -> x24, starting transfers between devices: none -> 43.2 us  [the longest x12 19 us: swap(): return lax.ppermute(x, 'c', SWAP)]
    all_gather x1 -> x0, waiting for transfers between devices: 31.2 us -> none  [local(): txt_all = lax.all_gather(text_embed, 'img', axis=0, tiled=True)]
    pallas_call x0 -> x7, Pallas kernels: none -> 28.4 us  [the longest x3 24.2 us: call(): pl.pallas_call(kernel, out_shape=out_shape, in_specs=[scalars if i in sme...]
    all_gather x1 -> x0, blocking collectives: 25.7 us -> none  [local(): img_all = lax.all_gather(image_embed, 'txt', axis=0, tiled=True)]
    ppermute x0 -> x24, waiting for transfers between devices: none -> 20.2 us  [the longest x8 8.26 us: ahead(): lax.ppermute(x, CZ, pairs + [(nz + i, nz + (i + k) % nz) for i in range(n...]
    all_to_all x0 -> x3, starting transfers between devices: none -> 17.7 us  [the longest x1 7.76 us: local(): txt = lax.all_to_all(spread, XY, 0, 0).reshape(cols, embed)]
  transfers between devices with their start and end apart: 3 -> 27, of which waited for: 1 -> 14; matrix products, arithmetic and copies ran while one was open for 2% -> 2% of each run, Pallas kernels for 0% -> 7%
where the time goes in v3:
time: 127 us; the launch traced here: 126 us
  starting transfers between devices  60.8 us (48%)
  Pallas kernels  28.4 us (22%)
  waiting for transfers between devices  23 us (18%)
  local copies, waits for them, and re-layouts  11.1 us (9%)
  between operations  1.61 us (1%)
  other arithmetic  1.43 us (1%)
    pallas_call x3, Pallas kernels, call(): pl.pallas_call(kernel, out_shape=out_shape, in_specs=[scalars if i in sme...  24.2 us
    ppermute x12, starting transfers between devices, swap(): return lax.ppermute(x, 'c', SWAP)  19 us
    ppermute x8, starting transfers between devices, ahead(): lax.ppermute(x, CZ, pairs + [(nz + i, nz + (i + k) % nz) for i in range(n...  16.6 us
    ppermute x8, waiting for transfers between devices, ahead(): lax.ppermute(x, CZ, pairs + [(nz + i, nz + (i + k) % nz) for i in range(n...  8.26 us
    all_to_all x1, starting transfers between devices, local(): txt = lax.all_to_all(spread, XY, 0, 0).reshape(cols, embed)  7.76 us
    ppermute x4, starting transfers between devices, onward(): lax.ppermute(x, CZ, pairs + [(nz + (i + k) % nz, nz + i) for i in range(n...  7.54 us
    unnamed x55, local copies, waits for them, and re-layouts  6.59 us
    ppermute x12, waiting for transfers between devices, swap(): return lax.ppermute(x, 'c', SWAP)  6.11 us
  transfers between devices with their start and end apart: 27, of which 14 were waited for; matrix products, arithmetic and copies ran while one was open for 2% of the time, Pallas kernels for 7%

profile of v3, /device:TPU:1, one launch (start us, length us, event | category | flops | bytes accessed | tf_op | source)
XLA Modules:
  0.0 126.4 jit_solution(14796318279122646494)
XLA Ops:
  0.6 2.3 %broadcast_in_dim.16 = bf16[16,48,1280]{2,1,0:T(8,128)(2,1)} broadcast(bf16[48,1280]{1,0:T(8,128)(2,1)} %param.5), dimensions={1,2} | broadcast | bytes 2088960 | tf_op jit(solution)/shard_map/broadcast_in_dim | solution.py:382
  3.0 7.8 %all-to-all-start = ((bf16[16,48,1280]{2,1,0:T(8,128)(2,1)}), bf16[16,48,1280]{2,1,0:T(8,128)(2,1)}, u32[]{:S(2)}, u32[]{:S(2)}) async-start(bf16[16,48,1280]{2,1,0:T(8,128)(2,1)} %broadcast_in_dim.16), calls=%async_computation | async-start | bytes 3932160 | tf_op jit(solution)/shard_map/all_to_all | solution.py:383
  10.7 1.0 collective-permute-start.1
  11.8 1.0 collective-permute-done.1.refs_13_.refs_19_
  12.8 0.6 copy-done.13
  13.4 3.1 %collective-permute-start.3 = (bf16[96,1280]{1,0:T(8,128)(2,1)S(1)}, bf16[96,1280]{1,0:T(8,128)(2,1)S(1)}, u32[]{:S(2)}, u32[]{:S(2)}) collective-permute-start(bf16[96,1280]{1,0:T(8,128)(2,1)S(1)} %constant_dynamic-update-slice_fusion), channel_id=1, source_target_pairs={{2,0},{3,1},{4,2},{5,3},{6,4},{7,5},{0,6},{1,7},{8,10},{9,11},{10,... | collective-permute-start | bytes 737288 | tf_op jit(solution)/shard_map/ppermute | solution.py:376
  16.5 1.6 %collective-permute-start.2 = (bf16[96,1280]{1,0:T(8,128)(2,1)S(1)}, bf16[96,1280]{1,0:T(8,128)(2,1)S(1)}, u32[]{:S(2)}, u32[]{:S(2)}) collective-permute-start(bf16[96,1280]{1,0:T(8,128)(2,1)S(1)} %constant_dynamic-update-slice_fusion), channel_id=1, source_target_pairs={{1,0},{2,1},{3,2},{4,3},{5,4},{6,5},{7,6},{0,7},{8,9},{9,10},{10,1... | collective-permute-start | bytes 737288 | tf_op jit(solution)/shard_map/ppermute | solution.py:376
  18.1 6.0 %collective-permute-done.3.refs_5_.refs_11_ = bf16[96,1280]{1,0:T(8,128)(2,1)S(1)} collective-permute-done((bf16[96,1280]{1,0:T(8,128)(2,1)S(1)}, bf16[96,1280]{1,0:T(8,128)(2,1)S(1)}, u32[]{:S(2)}, u32[]{:S(2)}) %collective-permute-start.3) | collective-permute-done | bytes 245792 | tf_op jit(solution)/shard_map/ppermute | solution.py:376
  24.1 2.8 %collective-permute-start.4 = (bf16[96,1280]{1,0:T(8,128)(2,1)S(1)}, bf16[96,1280]{1,0:T(8,128)(2,1)S(1)}, u32[]{:S(2)}, u32[]{:S(2)}) collective-permute-start(bf16[96,1280]{1,0:T(8,128)(2,1)S(1)} %collective-permute-done.3.refs_5_.refs_11_), channel_id=1, source_target_pairs={{1,0},{2,1},{3,2},{4,3},{5,4},{6,5},{7,6},{0,7},{8,9},{9,10},{10,1... | collective-permute-start | bytes 737288 | tf_op jit(solution)/shard_map/ppermute | solution.py:376
  26.9 0.1 collective-permute-start.5
  27.1 4.4 %collective-permute-start = (f32[384]{0:T(512)S(1)}, f32[384]{0:T(512)S(1)}, u32[]{:S(2)}, u32[]{:S(2)}) collective-permute-start(f32[384]{0:T(512)S(1)} %and_select_fusion), channel_id=1, source_target_pairs={{0,8},{8,0},{1,9},{9,1},{2,10},{10,2},{3,11},{11,3},{4,12},{12,4},... | collective-permute-start | bytes 4616 | tf_op jit(solution)/shard_map/ppermute | solution.py:372
  31.5 0.1 collective-permute-start.7
  31.6 0.4 collective-permute-start.6
  32.0 1.0 collective-permute-start.8
  33.0 0.6 pad_add_fusion.refs_0_.idx
  34.3 0.3 collective-permute-done.5.refs_7_.refs_13_
  34.7 1.7 %collective-permute-start.9 = (bf16[48,1280]{1,0:T(8,128)(2,1)S(1)}, bf16[48,1280]{1,0:T(8,128)(2,1)S(1)}, u32[]{:S(2)}, u32[]{:S(2)}) collective-permute-start(bf16[48,1280]{1,0:T(8,128)(2,1)S(1)} %collective-permute-done.5.refs_7_.refs_13_), channel_id=1, source_target_pairs={{0,8},{8,0},{1,9},{9,1},{2,10},{10,2},{3,11},{11,3},{4,12},{12,4},... | collective-permute-start | bytes 368648 | tf_op jit(solution)/shard_map/ppermute | solution.py:372
  36.4 0.6 pad_bitcast_fusion.refs_2_.refs_7_
  36.9 0.4 collective-permute-done.9.refs_12_.refs_18_
  37.4 0.7 copy-done.21
  38.1 1.4 %all-to-all-done = bf16[16,48,1280]{2,1,0:T(8,128)(2,1)} async-done(((bf16[16,48,1280]{2,1,0:T(8,128)(2,1)}), bf16[16,48,1280]{2,1,0:T(8,128)(2,1)}, u32[]{:S(2)}, u32[]{:S(2)}) %all-to-all-start) | async-done | bytes 1966112 | tf_op jit(solution)/shard_map/all_to_all | solution.py:383
  39.5 7.8 %shard_map.83 = (f32[768,768]{1,0:T(8,128)}, f32[24,128]{1,0:T(8,128)}, f32[16,24,128]{2,1,0:T(8,128)}) custom-call(s32[2]{0:T(128)} %pad_add_fusion.refs_0_.idx, f32[1]{0:T(128)} %bitcast.2.refs_1_, f32[8,128]{1,0:T(8,128)} %pad_bitcast_fusion.refs_2_.refs_7_, bf16[768,1280]{1,0:T(8,128)(2,1)} %bitcast.4.refs_3_.refs_9_, bf16[96,1280]{1,0:T(8,128)(2,1)} %copy-done.19, ...), custom_call_target="tpu_custom_call" | custom-call | flops 1509949440 | bytes 3936268 | tf_op jit(solution)/shard_map/pallas_call | solution.py:104
  47.3 2.2 %collective-permute-start.10 = (f32[24,128]{1,0:T(8,128)}, f32[24,128]{1,0:T(8,128)S(1)}, u32[]{:S(2)}, u32[]{:S(2)}) collective-permute-start(f32[24,128]{1,0:T(8,128)} %get-tuple-element.26), channel_id=1, source_target_pairs={{0,8},{8,0},{1,9},{9,1},{2,10},{10,2},{3,11},{11,3},{4,12},{12,4},... | collective-permute-start | bytes 36872 | tf_op jit(solution)/shard_map/ppermute | solution.py:372
  49.5 1.0 collective-permute-done.10
  50.6 0.7 log_add_fusion.1
  51.3 1.7 %collective-permute-start.14 = (f32[24,128]{1,0:T(8,128)S(1)}, f32[24,128]{1,0:T(8,128)S(1)}, u32[]{:S(2)}, u32[]{:S(2)}) collective-permute-start(f32[24,128]{1,0:T(8,128)S(1)} %pad_maximum_fusion.refs_3_), channel_id=1, source_target_pairs={{1,0},{2,1},{3,2},{4,3},{5,4},{6,5},{7,6},{0,7},{8,9},{9,10},{10,1... | collective-permute-start | bytes 36872 | tf_op jit(solution)/shard_map/ppermute | solution.py:376
  53.0 3.0 %collective-permute-start.13 = (f32[24,128]{1,0:T(8,128)S(1)}, f32[24,128]{1,0:T(8,128)S(1)}, u32[]{:S(2)}, u32[]{:S(2)}) collective-permute-start(f32[24,128]{1,0:T(8,128)S(1)} %pad_maximum_fusion.refs_3_), channel_id=1, source_target_pairs={{2,0},{3,1},{4,2},{5,3},{6,4},{7,5},{0,6},{1,7},{8,10},{9,11},{10,... | collective-permute-start | bytes 36872 | tf_op jit(solution)/shard_map/ppermute | solution.py:376
  56.0 3.7 %collective-permute-start.12 = (f32[24,128]{1,0:T(8,128)S(1)}, f32[24,128]{1,0:T(8,128)S(1)}, u32[]{:S(2)}, u32[]{:S(2)}) collective-permute-start(f32[24,128]{1,0:T(8,128)S(1)} %pad_maximum_fusion.refs_3_), channel_id=1, source_target_pairs={{3,0},{4,1},{5,2},{6,3},{7,4},{0,5},{1,6},{2,7},{8,11},{9,12},{10,... | collective-permute-start | bytes 36872 | tf_op jit(solution)/shard_map/ppermute | solution.py:376
  59.7 4.2 %all-to-all-start.1 = ((f32[16,24,128]{2,1,0:T(8,128)}), f32[16,24,128]{2,1,0:T(8,128)}, u32[]{:S(2)}, u32[]{:S(2)}) async-start(f32[16,24,128]{2,1,0:T(8,128)} %get-tuple-element.25), calls=%async_computation.1 | async-start | bytes 393216 | tf_op jit(solution)/shard_map/all_to_all | solution.py:417
  63.9 0.7 collective-permute-start.11
  64.6 4.3 %collective-permute-start.15 = (f32[24,128]{1,0:T(8,128)S(1)}, f32[24,128]{1,0:T(8,128)}, u32[]{:S(2)}, u32[]{:S(2)}) collective-permute-start(f32[24,128]{1,0:T(8,128)S(1)} %pad_maximum_fusion.1.refs_5_), channel_id=1, source_target_pairs={{0,8},{8,0},{1,9},{9,1},{2,10},{10,2},{3,11},{11,3},{4,12},{12,4},... | collective-permute-start | bytes 36872 | tf_op jit(solution)/shard_map/ppermute | solution.py:372
  68.9 1.9 %collective-permute-done.11.refs_4_ = f32[24,128]{1,0:T(8,128)S(1)} collective-permute-done((f32[24,128]{1,0:T(8,128)S(1)}, f32[24,128]{1,0:T(8,128)S(1)}, u32[]{:S(2)}, u32[]{:S(2)}) %collective-permute-start.11) | collective-permute-done | bytes 12320 | tf_op jit(solution)/shard_map/ppermute | solution.py:376
  70.8 0.6 copy-done.26
  71.4 0.5 all-to-all-done.1.refs_2_
  72.0 11.2 %shard_map.84 = (bf16[768,1408]{1,0:T(8,128)(2,1)}, bf16[384,1280]{1,0:T(8,128)(2,1)}, bf16[384,768]{1,0:T(8,128)(2,1)}, f32[8,128]{1,0:T(8,128)}, f32[8,128]{1,0:T(8,128)}, /*index=5*/f32[8,128]{1,0:T(8,128)}) custom-call(s32[2]{0:T(128)} %pad_add_fusion.refs_0_.idx, f32[1]{0:T(128)} %bitcast.2.refs_1_, f32[16,24,128]{2,1,0:T(8,128)} %all-to-all-done.1.refs_2_, ...), custom_call_target="tpu_custom_call" | custom-call | flops 3019898880 | bytes 6541324 | tf_op jit(solution)/shard_map/pallas_call | solution.py:104
  83.2 5.7 %all-to-all-start.2 = ((bf16[16,48,1408]{2,1,0:T(8,128)(2,1)}), bf16[16,48,1408]{2,1,0:T(8,128)(2,1)}, u32[]{:S(2)}, u32[]{:S(2)}) async-start(bf16[16,48,1408]{2,1,0:T(8,128)(2,1)} %bitcast.12), calls=%async_computation.2 | async-start | bytes 4325376 | tf_op jit(solution)/shard_map/all_to_all | solution.py:446
  88.9 1.6 %collective-permute-start.18 = (bf16[384,1280]{1,0:T(8,128)(2,1)S(1)}, bf16[384,1280]{1,0:T(8,128)(2,1)S(1)}, u32[]{:S(2)}, u32[]{:S(2)}) collective-permute-start(bf16[384,1280]{1,0:T(8,128)(2,1)S(1)} %copy-done.18), channel_id=1, source_target_pairs={{0,8},{8,0},{1,9},{9,1},{2,10},{10,2},{3,11},{11,3},{4,12},{12,4},... | collective-permute-start | bytes 2949128 | tf_op jit(solution)/shard_map/ppermute | solution.py:372
  90.6 0.1 collective-permute-start.17
  90.7 2.1 %collective-permute-done.17.refs_1_.other_sums = f32[8,128]{1,0:T(8,128)S(1)} collective-permute-done((f32[8,128]{1,0:T(8,128)S(1)}, f32[8,128]{1,0:T(8,128)S(1)}, u32[]{:S(2)}, u32[]{:S(2)}) %collective-permute-start.17) | collective-permute-done | bytes 4128 | tf_op jit(solution)/shard_map/ppermute | solution.py:372
  92.8 0.6 copy-done.5
  93.4 1.0 copy-done.11
  94.3 5.3 %shard_map.85 = (bf16[96,1408]{1,0:T(8,128)(2,1)}, f32[96,1280]{1,0:T(8,128)}, bf16[96,1408]{1,0:T(8,128)(2,1)}, bf16[48,1408]{1,0:T(8,128)(2,1)}, f32[48,1280]{1,0:T(8,128)}) custom-call(f32[8,128]{1,0:T(8,128)} %get-tuple-element.30.refs_0_.sums, f32[8,128]{1,0:T(8,128)} %copy-done.5, bf16[384,768]{1,0:T(8,128)(2,1)} %get-tuple-element.31.refs_2_, ...), custom_call_target="tpu_custom_call" | custom-call | flops 754974720 | bytes 3547136 | tf_op jit(solution)/shard_map/pallas_call | solution.py:104
  99.6 0.9 collective-permute-start.20
  100.5 3.7 %collective-permute-start.21 = (bf16[48,1408]{1,0:T(8,128)(2,1)}, bf16[48,1408]{1,0:T(8,128)(2,1)S(1)}, u32[]{:S(2)}, u32[]{:S(2)}) collective-permute-start(bf16[48,1408]{1,0:T(8,128)(2,1)} %get-tuple-element.37), channel_id=1, source_target_pairs={{0,2},{1,3},{2,4},{3,5},{4,6},{5,7},{6,0},{7,1},{10,8},{11,9},{12,... | collective-permute-start | bytes 405512 | tf_op jit(solution)/shard_map/ppermute | solution.py:380
  104.2 0.7 collective-permute-start.19
  104.9 4.7 %collective-permute-done.21.far_one = bf16[48,1408]{1,0:T(8,128)(2,1)S(1)} collective-permute-done((bf16[48,1408]{1,0:T(8,128)(2,1)}, bf16[48,1408]{1,0:T(8,128)(2,1)S(1)}, u32[]{:S(2)}, u32[]{:S(2)}) %collective-permute-start.21) | collective-permute-done | bytes 135200 | tf_op jit(solution)/shard_map/ppermute | solution.py:380
  109.6 1.0 copy-done
  110.6 0.7 copy-done.3
  111.3 0.7 copy-done.6
  112.0 0.6 copy-done.10
  112.6 0.7 shard_map.86
  113.3 2.3 %collective-permute-start.22 = (bf16[96,1408]{1,0:T(8,128)(2,1)S(1)}, bf16[96,1408]{1,0:T(8,128)(2,1)S(1)}, u32[]{:S(2)}, u32[]{:S(2)}) collective-permute-start(bf16[96,1408]{1,0:T(8,128)(2,1)S(1)} %shard_map.86), channel_id=1, source_target_pairs={{0,2},{1,3},{2,4},{3,5},{4,6},{5,7},{6,0},{7,1},{10,8},{11,9},{12,... | collective-permute-start | bytes 811016 | tf_op jit(solution)/shard_map/ppermute | solution.py:380
  115.6 0.8 reshape.34
  116.3 0.0 collective-permute-start.16
  116.4 0.7 dynamic-slice_bitcast_fusion.refs_0_
  117.1 0.5 collective-permute-done.16
  117.6 0.1 select_n.71.refs_1_
  117.6 0.9 all-to-all-done.2.got
  118.6 2.7 %shard_map.87 = (f32[48,1280]{1,0:T(8,128)}, f32[8,128]{1,0:T(8,128)S(1)}) custom-call(bf16[16,48,1408]{2,1,0:T(8,128)(2,1)} %all-to-all-done.2.got), custom_call_target="tpu_custom_call" | custom-call | tf_op jit(solution)/shard_map/pallas_call | solution.py:125
  121.2 1.1 collective-permute-done.22.two
  122.3 0.1 shard_map.88
  122.4 2.0 %collective-permute-start.23 = (f32[48,1408]{1,0:T(8,128)S(1)}, f32[48,1408]{1,0:T(8,128)S(1)}, u32[]{:S(2)}, u32[]{:S(2)}) collective-permute-start(f32[48,1408]{1,0:T(8,128)S(1)} %get-tuple-element.41), channel_id=1, source_target_pairs={{0,8},{8,0},{1,9},{9,1},{2,10},{10,2},{3,11},{11,3},{4,12},{12,4},... | collective-permute-start | bytes 811016 | tf_op jit(solution)/shard_map/ppermute | solution.py:372
  124.5 1.2 collective-permute-done.23.received
  125.6 0.7 shard_map.89
  (68 shorter events, 0.3 us)
Async XLA Ops:
  3.0 7.8 %copy-start.12 = (bf16[48,1280]{1,0:T(8,128)(2,1)S(1)}, bf16[48,1280]{1,0:T(8,128)(2,1)}, u32[]{:S(2)}) copy-start(bf16[48,1280]{1,0:T(8,128)(2,1)} %refs_14_.1) | copy-start | bytes 368644
  3.0 23.9 %copy-start.17 = (s32[384]{0:T(512)S(1)}, s32[384]{0:T(512)}, u32[]{:S(2)}) copy-start(s32[384]{0:T(512)} %param.6) | copy-start | bytes 4612
  3.0 36.5 %all-to-all-start = ((bf16[16,48,1280]{2,1,0:T(8,128)(2,1)}), bf16[16,48,1280]{2,1,0:T(8,128)(2,1)}, u32[]{:S(2)}, u32[]{:S(2)}) async-start(bf16[16,48,1280]{2,1,0:T(8,128)(2,1)} %broadcast_in_dim.16), calls=%async_computation | async-start | bytes 3932160 | tf_op jit(solution)/shard_map/all_to_all | solution.py:383
  10.7 2.0 %collective-permute-start.1 = (bf16[48,1280]{1,0:T(8,128)(2,1)S(1)}, bf16[48,1280]{1,0:T(8,128)(2,1)S(1)}, u32[]{:S(2)}, u32[]{:S(2)}) collective-permute-start(bf16[48,1280]{1,0:T(8,128)(2,1)S(1)} %copy-done.12), channel_id=1, source_target_pairs={{0,8},{8,0},{1,9},{9,1},{2,10},{10,2},{3,11},{11,3},{4,12},{12,4},... | collective-permute-start | bytes 368648 | tf_op jit(solution)/shard_map/ppermute | solution.py:372
  12.8 0.7 copy-start.13
  13.4 10.7 %collective-permute-start.3 = (bf16[96,1280]{1,0:T(8,128)(2,1)S(1)}, bf16[96,1280]{1,0:T(8,128)(2,1)S(1)}, u32[]{:S(2)}, u32[]{:S(2)}) collective-permute-start(bf16[96,1280]{1,0:T(8,128)(2,1)S(1)} %constant_dynamic-update-slice_fusion), channel_id=1, source_target_pairs={{2,0},{3,1},{4,2},{5,3},{6,4},{7,5},{0,6},{1,7},{8,10},{9,11},{10,... | collective-permute-start | bytes 737288 | tf_op jit(solution)/shard_map/ppermute | solution.py:376
  16.5 15.1 %collective-permute-start.2 = (bf16[96,1280]{1,0:T(8,128)(2,1)S(1)}, bf16[96,1280]{1,0:T(8,128)(2,1)S(1)}, u32[]{:S(2)}, u32[]{:S(2)}) collective-permute-start(bf16[96,1280]{1,0:T(8,128)(2,1)S(1)} %constant_dynamic-update-slice_fusion), channel_id=1, source_target_pairs={{1,0},{2,1},{3,2},{4,3},{5,4},{6,5},{7,6},{0,7},{8,9},{9,10},{10,1... | collective-permute-start | bytes 737288 | tf_op jit(solution)/shard_map/ppermute | solution.py:376
  24.1 10.5 %copy-start.14 = (bf16[96,1280]{1,0:T(8,128)(2,1)}, bf16[96,1280]{1,0:T(8,128)(2,1)S(1)}, u32[]{:S(2)}) copy-start(bf16[96,1280]{1,0:T(8,128)(2,1)S(1)} %collective-permute-done.3.refs_5_.refs_11_) | copy-start | bytes 737284
  24.1 7.9 %collective-permute-start.4 = (bf16[96,1280]{1,0:T(8,128)(2,1)S(1)}, bf16[96,1280]{1,0:T(8,128)(2,1)S(1)}, u32[]{:S(2)}, u32[]{:S(2)}) collective-permute-start(bf16[96,1280]{1,0:T(8,128)(2,1)S(1)} %collective-permute-done.3.refs_5_.refs_11_), channel_id=1, source_target_pairs={{1,0},{2,1},{3,2},{4,3},{5,4},{6,5},{7,6},{0,7},{8,9},{9,10},{10,1... | collective-permute-start | bytes 737288 | tf_op jit(solution)/shard_map/ppermute | solution.py:376
  26.9 7.7 %collective-permute-start.5 = (bf16[48,1280]{1,0:T(8,128)(2,1)S(1)}, bf16[48,1280]{1,0:T(8,128)(2,1)S(1)}, u32[]{:S(2)}, u32[]{:S(2)}) collective-permute-start(bf16[48,1280]{1,0:T(8,128)(2,1)S(1)} %slice.68), channel_id=1, source_target_pairs={{2,0},{3,1},{4,2},{5,3},{6,4},{7,5},{0,6},{1,7},{8,10},{9,11},{10,... | collective-permute-start | bytes 368648 | tf_op jit(solution)/shard_map/ppermute | solution.py:376
  27.1 9.3 %collective-permute-start = (f32[384]{0:T(512)S(1)}, f32[384]{0:T(512)S(1)}, u32[]{:S(2)}, u32[]{:S(2)}) collective-permute-start(f32[384]{0:T(512)S(1)} %and_select_fusion), channel_id=1, source_target_pairs={{0,8},{8,0},{1,9},{9,1},{2,10},{10,2},{3,11},{11,3},{4,12},{12,4},... | collective-permute-start | bytes 4616 | tf_op jit(solution)/shard_map/ppermute | solution.py:372
  31.5 5.9 %collective-permute-start.7 = (bf16[96,1280]{1,0:T(8,128)(2,1)S(1)}, bf16[96,1280]{1,0:T(8,128)(2,1)S(1)}, u32[]{:S(2)}, u32[]{:S(2)}) collective-permute-start(bf16[96,1280]{1,0:T(8,128)(2,1)S(1)} %collective-permute-done.3.refs_5_.refs_11_), channel_id=1, source_target_pairs={{0,8},{8,0},{1,9},{9,1},{2,10},{10,2},{3,11},{11,3},{4,12},{12,4},... | collective-permute-start | bytes 737288 | tf_op jit(solution)/shard_map/ppermute | solution.py:372
  31.6 5.8 %copy-start.19 = (bf16[96,1280]{1,0:T(8,128)(2,1)}, bf16[96,1280]{1,0:T(8,128)(2,1)S(1)}, u32[]{:S(2)}) copy-start(bf16[96,1280]{1,0:T(8,128)(2,1)S(1)} %collective-permute-done.2.refs_4_.refs_10_) | copy-start | bytes 737284
  31.6 5.8 %collective-permute-start.6 = (bf16[96,1280]{1,0:T(8,128)(2,1)S(1)}, bf16[96,1280]{1,0:T(8,128)(2,1)S(1)}, u32[]{:S(2)}, u32[]{:S(2)}) collective-permute-start(bf16[96,1280]{1,0:T(8,128)(2,1)S(1)} %collective-permute-done.2.refs_4_.refs_10_), channel_id=1, source_target_pairs={{0,8},{8,0},{1,9},{9,1},{2,10},{10,2},{3,11},{11,3},{4,12},{12,4},... | collective-permute-start | bytes 737288 | tf_op jit(solution)/shard_map/ppermute | solution.py:372
  32.0 5.4 %copy-start.20 = (bf16[96,1280]{1,0:T(8,128)(2,1)}, bf16[96,1280]{1,0:T(8,128)(2,1)S(1)}, u32[]{:S(2)}) copy-start(bf16[96,1280]{1,0:T(8,128)(2,1)S(1)} %collective-permute-done.4.refs_6_.refs_12_) | copy-start | bytes 737284
  32.0 5.4 %collective-permute-start.8 = (bf16[96,1280]{1,0:T(8,128)(2,1)S(1)}, bf16[96,1280]{1,0:T(8,128)(2,1)S(1)}, u32[]{:S(2)}, u32[]{:S(2)}) collective-permute-start(bf16[96,1280]{1,0:T(8,128)(2,1)S(1)} %collective-permute-done.4.refs_6_.refs_12_), channel_id=1, source_target_pairs={{0,8},{8,0},{1,9},{9,1},{2,10},{10,2},{3,11},{11,3},{4,12},{12,4},... | collective-permute-start | bytes 737288 | tf_op jit(solution)/shard_map/ppermute | solution.py:372
  34.7 4.8 %copy-start.24 = (bf16[48,1280]{1,0:T(8,128)(2,1)}, bf16[48,1280]{1,0:T(8,128)(2,1)S(1)}, u32[]{:S(2)}) copy-start(bf16[48,1280]{1,0:T(8,128)(2,1)S(1)} %collective-permute-done.5.refs_7_.refs_13_) | copy-start | bytes 368644
  34.7 2.7 %collective-permute-start.9 = (bf16[48,1280]{1,0:T(8,128)(2,1)S(1)}, bf16[48,1280]{1,0:T(8,128)(2,1)S(1)}, u32[]{:S(2)}, u32[]{:S(2)}) collective-permute-start(bf16[48,1280]{1,0:T(8,128)(2,1)S(1)} %collective-permute-done.5.refs_7_.refs_13_), channel_id=1, source_target_pairs={{0,8},{8,0},{1,9},{9,1},{2,10},{10,2},{3,11},{11,3},{4,12},{12,4},... | collective-permute-start | bytes 368648 | tf_op jit(solution)/shard_map/ppermute | solution.py:372
  37.3 2.1 %copy-start.25 = (bf16[48,1280]{1,0:T(8,128)(2,1)}, bf16[48,1280]{1,0:T(8,128)(2,1)S(1)}, u32[]{:S(2)}) copy-start(bf16[48,1280]{1,0:T(8,128)(2,1)S(1)} %collective-permute-done.9.refs_12_.refs_18_) | copy-start | bytes 368644
  37.3 0.7 copy-start.21
  37.3 2.1 %copy-start.22 = (bf16[96,1280]{1,0:T(8,128)(2,1)}, bf16[96,1280]{1,0:T(8,128)(2,1)S(1)}, u32[]{:S(2)}) copy-start(bf16[96,1280]{1,0:T(8,128)(2,1)S(1)} %collective-permute-done.6.refs_9_.refs_15_) | copy-start | bytes 737284
  38.1 1.4 %copy-start.23 = (bf16[96,1280]{1,0:T(8,128)(2,1)}, bf16[96,1280]{1,0:T(8,128)(2,1)S(1)}, u32[]{:S(2)}) copy-start(bf16[96,1280]{1,0:T(8,128)(2,1)S(1)} %collective-permute-done.8.refs_11_.refs_17_) | copy-start | bytes 737284
  47.3 3.3 %collective-permute-start.10 = (f32[24,128]{1,0:T(8,128)}, f32[24,128]{1,0:T(8,128)S(1)}, u32[]{:S(2)}, u32[]{:S(2)}) collective-permute-start(f32[24,128]{1,0:T(8,128)} %get-tuple-element.26), channel_id=1, source_target_pairs={{0,8},{8,0},{1,9},{9,1},{2,10},{10,2},{3,11},{11,3},{4,12},{12,4},... | collective-permute-start | bytes 36872 | tf_op jit(solution)/shard_map/ppermute | solution.py:372
  51.3 13.3 %copy-start.15 = (f32[24,128]{1,0:T(8,128)}, f32[24,128]{1,0:T(8,128)S(1)}, u32[]{:S(2)}) copy-start(f32[24,128]{1,0:T(8,128)S(1)} %pad_maximum_fusion.refs_3_) | copy-start | bytes 36868
  51.3 13.3 %collective-permute-start.14 = (f32[24,128]{1,0:T(8,128)S(1)}, f32[24,128]{1,0:T(8,128)S(1)}, u32[]{:S(2)}, u32[]{:S(2)}) collective-permute-start(f32[24,128]{1,0:T(8,128)S(1)} %pad_maximum_fusion.refs_3_), channel_id=1, source_target_pairs={{1,0},{2,1},{3,2},{4,3},{5,4},{6,5},{7,6},{0,7},{8,9},{9,10},{10,1... | collective-permute-start | bytes 36872 | tf_op jit(solution)/shard_map/ppermute | solution.py:376
  53.0 11.6 %collective-permute-start.13 = (f32[24,128]{1,0:T(8,128)S(1)}, f32[24,128]{1,0:T(8,128)S(1)}, u32[]{:S(2)}, u32[]{:S(2)}) collective-permute-start(f32[24,128]{1,0:T(8,128)S(1)} %pad_maximum_fusion.refs_3_), channel_id=1, source_target_pairs={{2,0},{3,1},{4,2},{5,3},{6,4},{7,5},{0,6},{1,7},{8,10},{9,11},{10,... | collective-permute-start | bytes 36872 | tf_op jit(solution)/shard_map/ppermute | solution.py:376
  56.0 8.6 %collective-permute-start.12 = (f32[24,128]{1,0:T(8,128)S(1)}, f32[24,128]{1,0:T(8,128)S(1)}, u32[]{:S(2)}, u32[]{:S(2)}) collective-permute-start(f32[24,128]{1,0:T(8,128)S(1)} %pad_maximum_fusion.refs_3_), channel_id=1, source_target_pairs={{3,0},{4,1},{5,2},{6,3},{7,4},{0,5},{1,6},{2,7},{8,11},{9,12},{10,... | collective-permute-start | bytes 36872 | tf_op jit(solution)/shard_map/ppermute | solution.py:376
  59.7 12.2 %all-to-all-start.1 = ((f32[16,24,128]{2,1,0:T(8,128)}), f32[16,24,128]{2,1,0:T(8,128)}, u32[]{:S(2)}, u32[]{:S(2)}) async-start(f32[16,24,128]{2,1,0:T(8,128)} %get-tuple-element.25), calls=%async_computation.1 | async-start | bytes 393216 | tf_op jit(solution)/shard_map/all_to_all | solution.py:417
  63.9 6.9 %collective-permute-start.11 = (f32[24,128]{1,0:T(8,128)S(1)}, f32[24,128]{1,0:T(8,128)S(1)}, u32[]{:S(2)}, u32[]{:S(2)}) collective-permute-start(f32[24,128]{1,0:T(8,128)S(1)} %pad_maximum_fusion.refs_3_), channel_id=1, source_target_pairs={{4,0},{5,1},{6,2},{7,3},{0,4},{1,5},{2,6},{3,7},{8,12},{9,13},{10,... | collective-permute-start | bytes 36872 | tf_op jit(solution)/shard_map/ppermute | solution.py:376
  64.6 6.2 %copy-start.16 = (f32[24,128]{1,0:T(8,128)}, f32[24,128]{1,0:T(8,128)S(1)}, u32[]{:S(2)}) copy-start(f32[24,128]{1,0:T(8,128)S(1)} %pad_maximum_fusion.1.refs_5_) | copy-start | bytes 36868
  64.6 6.8 %collective-permute-start.15 = (f32[24,128]{1,0:T(8,128)S(1)}, f32[24,128]{1,0:T(8,128)}, u32[]{:S(2)}, u32[]{:S(2)}) collective-permute-start(f32[24,128]{1,0:T(8,128)S(1)} %pad_maximum_fusion.1.refs_5_), channel_id=1, source_target_pairs={{0,8},{8,0},{1,9},{9,1},{2,10},{10,2},{3,11},{11,3},{4,12},{12,4},... | collective-permute-start | bytes 36872 | tf_op jit(solution)/shard_map/ppermute | solution.py:372
  70.8 0.6 copy-start.26
  83.1 5.8 %copy-start.18 = (bf16[384,1280]{1,0:T(8,128)(2,1)S(1)}, bf16[384,1280]{1,0:T(8,128)(2,1)}, u32[]{:S(2)}) copy-start(bf16[384,1280]{1,0:T(8,128)(2,1)} %get-tuple-element.32) | copy-start | bytes 2949124
  83.2 7.4 %copy-start.2 = (f32[8,128]{1,0:T(8,128)S(1)}, f32[8,128]{1,0:T(8,128)}, u32[]{:S(2)}) copy-start(f32[8,128]{1,0:T(8,128)} %get-tuple-element.30.refs_0_.sums) | copy-start | bytes 12292
  83.2 35.4 %all-to-all-start.2 = ((bf16[16,48,1408]{2,1,0:T(8,128)(2,1)}), bf16[16,48,1408]{2,1,0:T(8,128)(2,1)}, u32[]{:S(2)}, u32[]{:S(2)}) async-start(bf16[16,48,1408]{2,1,0:T(8,128)(2,1)} %bitcast.12), calls=%async_computation.2 | async-start | bytes 4325376 | tf_op jit(solution)/shard_map/all_to_all | solution.py:446
  88.9 4.4 %collective-permute-start.18 = (bf16[384,1280]{1,0:T(8,128)(2,1)S(1)}, bf16[384,1280]{1,0:T(8,128)(2,1)S(1)}, u32[]{:S(2)}, u32[]{:S(2)}) collective-permute-start(bf16[384,1280]{1,0:T(8,128)(2,1)S(1)} %copy-done.18), channel_id=1, source_target_pairs={{0,8},{8,0},{1,9},{9,1},{2,10},{10,2},{3,11},{11,3},{4,12},{12,4},... | collective-permute-start | bytes 2949128 | tf_op jit(solution)/shard_map/ppermute | solution.py:372
  90.6 2.2 %collective-permute-start.17 = (f32[8,128]{1,0:T(8,128)S(1)}, f32[8,128]{1,0:T(8,128)S(1)}, u32[]{:S(2)}, u32[]{:S(2)}) collective-permute-start(f32[8,128]{1,0:T(8,128)S(1)} %copy-done.2), channel_id=1, source_target_pairs={{0,8},{8,0},{1,9},{9,1},{2,10},{10,2},{3,11},{11,3},{4,12},{12,4},... | collective-permute-start | bytes 12296 | tf_op jit(solution)/shard_map/ppermute | solution.py:372
  92.8 0.6 copy-start.5
  93.3 1.0 copy-start.11
  99.6 22.7 %copy-start.4 = (f32[8,128]{1,0:T(8,128)S(1)}, f32[8,128]{1,0:T(8,128)}, u32[]{:S(2)}) copy-start(f32[8,128]{1,0:T(8,128)} %get-tuple-element.30.refs_0_.sums) | copy-start | bytes 12292
  99.6 10.0 %collective-permute-start.20 = (bf16[96,1408]{1,0:T(8,128)(2,1)}, bf16[96,1408]{1,0:T(8,128)(2,1)S(1)}, u32[]{:S(2)}, u32[]{:S(2)}) collective-permute-start(bf16[96,1408]{1,0:T(8,128)(2,1)} %get-tuple-element.36), channel_id=1, source_target_pairs={{0,1},{1,2},{2,3},{3,4},{4,5},{5,6},{6,7},{7,0},{9,8},{10,9},{11,1... | collective-permute-start | bytes 811016 | tf_op jit(solution)/shard_map/ppermute | solution.py:380
  100.5 9.1 %collective-permute-start.21 = (bf16[48,1408]{1,0:T(8,128)(2,1)}, bf16[48,1408]{1,0:T(8,128)(2,1)S(1)}, u32[]{:S(2)}, u32[]{:S(2)}) collective-permute-start(bf16[48,1408]{1,0:T(8,128)(2,1)} %get-tuple-element.37), channel_id=1, source_target_pairs={{0,2},{1,3},{2,4},{3,5},{4,6},{5,7},{6,0},{7,1},{10,8},{11,9},{12,... | collective-permute-start | bytes 405512 | tf_op jit(solution)/shard_map/ppermute | solution.py:380
  104.2 17.0 %collective-permute-start.19 = (bf16[96,1408]{1,0:T(8,128)(2,1)}, bf16[96,1408]{1,0:T(8,128)(2,1)S(1)}, u32[]{:S(2)}, u32[]{:S(2)}) collective-permute-start(bf16[96,1408]{1,0:T(8,128)(2,1)} %get-tuple-element.34), channel_id=1, source_target_pairs={{0,1},{1,2},{2,3},{3,4},{4,5},{5,6},{6,7},{7,0},{9,8},{10,9},{11,1... | collective-permute-start | bytes 811016 | tf_op jit(solution)/shard_map/ppermute | solution.py:380
  109.6 1.0 copy-start
  110.6 0.7 copy-start.3
  111.3 0.7 copy-start.6
  112.0 0.6 copy-start.10
  112.6 9.7 %copy-start.1 = (f32[48,1280]{1,0:T(8,128)S(1)}, f32[48,1280]{1,0:T(8,128)}, u32[]{:S(2)}) copy-start(f32[48,1280]{1,0:T(8,128)} %get-tuple-element.33.own) | copy-start | bytes 737284
  112.6 9.7 %copy-start.7 = (f32[8,128]{1,0:T(8,128)S(1)}, f32[8,128]{1,0:T(8,128)}, u32[]{:S(2)}) copy-start(f32[8,128]{1,0:T(8,128)} %copy-done.5) | copy-start | bytes 12292
  113.3 9.0 %collective-permute-start.22 = (bf16[96,1408]{1,0:T(8,128)(2,1)S(1)}, bf16[96,1408]{1,0:T(8,128)(2,1)S(1)}, u32[]{:S(2)}, u32[]{:S(2)}) collective-permute-start(bf16[96,1408]{1,0:T(8,128)(2,1)S(1)} %shard_map.86), channel_id=1, source_target_pairs={{0,2},{1,3},{2,4},{3,5},{4,6},{5,7},{6,0},{7,1},{10,8},{11,9},{12,... | collective-permute-start | bytes 811016 | tf_op jit(solution)/shard_map/ppermute | solution.py:380
  116.3 1.2 collective-permute-start.16
  117.1 9.3 %copy-start.9 = (f32[384]{0:T(512)}, f32[384]{0:T(512)S(1)}, u32[]{:S(2)}) copy-start(f32[384]{0:T(512)S(1)} %dynamic-slice_bitcast_fusion.refs_0_) | copy-start | bytes 4612
  117.6 8.7 %copy-start.8 = (f32[1536]{0:T(1024)}, f32[1536]{0:T(1024)S(1)}, u32[]{:S(2)}) copy-start(f32[1536]{0:T(1024)S(1)} %select_n.71.refs_1_) | copy-start | bytes 18436
  122.4 3.2 %collective-permute-start.23 = (f32[48,1408]{1,0:T(8,128)S(1)}, f32[48,1408]{1,0:T(8,128)S(1)}, u32[]{:S(2)}, u32[]{:S(2)}) collective-permute-start(f32[48,1408]{1,0:T(8,128)S(1)} %get-tuple-element.41), channel_id=1, source_target_pairs={{0,8},{8,0},{1,9},{9,1},{2,10},{10,2},{3,11},{11,3},{4,12},{12,4},... | collective-permute-start | bytes 811016 | tf_op jit(solution)/shard_map/ppermute | solution.py:372

commit v4 on v3

--- a/solution.py
+++ b/solution.py
@@ -13,6 +13,7 @@
 SWAP = [(0, 1), (1, 0)]
 LANES = 128
 VMEM_BYTES = 64 * 1024 * 1024
+MESSAGE = 48
 F32 = jnp.float32
 BF16 = jnp.bfloat16
 
@@ -29,6 +30,9 @@
     def start(self):
         for copy in self.started:
             copy.start()
+
+    def start_part(self, i):
+        self.started[i].start()
 
     def part(self, i):
         self.started[i].wait()
@@ -65,7 +69,7 @@
             copy.wait()
 
 
-def call(body, out_shape, *args, flops=0, smem=(), scratch=(), cuts=(), joined=None, held=None, sends=16):
+def call(body, out_shape, *args, flops=0, smem=(), scratch=(), cuts=(), joined=None, held=None, sends=16, spare=0, later=()):
     many = isinstance(out_shape, tuple)
     shapes = out_shape if many else (out_shape,)
     held = [x if held is None or held[i] is None else held[i] for i, x in enumerate(shapes)]
@@ -84,21 +88,23 @@
         ins, refs = refs[: len(args)], refs[len(args) :]
         outs, refs = refs[: len(shapes)], refs[len(shapes) :]
         buffers, refs = refs[: len(buffers_of)], refs[len(buffers_of) :]
-        spare, refs = refs[: len(held)], refs[len(held) :]
+        kept, refs = refs[: len(held)], refs[len(held) :]
         in_sems, refs = refs[: len(counts)], refs[len(counts) :]
         out_sems, refs = refs[0], refs[1:]
         given = list(ins[:joined])
         for j, i in enumerate(arrays):
             given[i] = Loaded(ins[i], buffers[j], in_sems[j], plan[j])
-            given[i].start()
+            if i not in later:
+                given[i].start()
         if joined < len(args):
             given.append(Joined(ins[joined:], buffers[-1], in_sems[-1]))
-            given[-1].start()
+            if joined not in later:
+                given[-1].start()
         sender = Sender(out_sems)
-        body(given, spare, outs, sender, *refs)
+        body(given, kept, outs, sender, *refs)
         sender.finish()
 
-    far = pl.BlockSpec(memory_space=pltpu.HBM)
+    far = pl.BlockSpec(memory_space=pl.ANY if spare else pltpu.HBM)
     scalars = pl.BlockSpec(memory_space=pltpu.SMEM)
     size = sum(a.size * a.dtype.itemsize for a in args)
     return pl.pallas_call(
@@ -114,11 +120,11 @@
             *scratch,
         ],
         cost_estimate=pl.CostEstimate(flops=flops, bytes_accessed=size, transcendentals=0),
-        compiler_params=pltpu.CompilerParams(vmem_limit_bytes=VMEM_BYTES),
+        compiler_params=pltpu.CompilerParams(vmem_limit_bytes=VMEM_BYTES - spare),
     )(*args)
 
 
-def near(body, out_shape, *args, smem=(), unread=()):
+def small(body, out_shape, *args, smem=(), unread=()):
     spec = lambda i: pl.BlockSpec(memory_space=pltpu.SMEM if i in smem else pltpu.HBM if i in unread else pltpu.VMEM)
     many = isinstance(out_shape, tuple)
     vmem = pl.BlockSpec(memory_space=pltpu.VMEM)
@@ -153,9 +159,9 @@
     return first + [(1 - who, -k) for who, k in first]
 
 
-def row_at(idx, block, nz, part):
+def row_at(block, nz, part):
     who, k = block
-    c, z = idx[0], idx[1]
+    c, z = lax.axis_index("c"), lax.axis_index("z")
     core = c if who == 0 else 1 - c
     step = k * (1 - 2 * c)
     return pl.multiple_of((core * nz + lax.rem(z + step + nz, nz)) * part, 16)
@@ -166,19 +172,27 @@
 
 
 def logits_kernel(nz, ins, held, outs, sender, column, stat):
-    idx, scale, pairs, txt, images = ins
+    scale, pairs, txt, images = ins
     logits, row_out, packed = held
     rows, cols = logits.shape
     part = rows // (NC * nz)
     s = scale[0]
+    count = len(images.started)
+    txt.start_part(0)
+    for i in range(count):
+        images.start_part(i)
+    for i in range(1, len(txt.started)):
+        txt.start_part(i)
     column[...] = tall([unpack(pairs.get(), rows // LANES)])
-    images = images.get()
     for i, n in enumerate(range(0, cols, 256)):
         txt.part(i)
-        for m in range(0, rows, 384):
-            block = dot(images[m : m + 384, :], txt.ref[n : n + 256, :], ((1,), (1,)))
-            logits[m : m + 384, n : n + 256] = s * block
-    sender.send(logits, outs[0])
+        for j, m in enumerate((0, rows // 2)):
+            if i == 0:
+                for k in range(j * count // 2, (j + 1) * count // 2):
+                    images.part(k)
+            block = dot(images.ref[m : m + rows // 2, :], txt.ref[n : n + 256, :], ((1,), (1,)))
+            logits[m : m + rows // 2, n : n + 256] = s * block
+        sender.send(logits.at[:, n : n + 256], outs[0].at[:, n : n + 256])
 
     def fold(x):
         return x.reshape(part // 8, 8, cols)
@@ -189,7 +203,7 @@
     for i, block in enumerate(order_of(nz)):
         x = logits[i * part : (i + 1) * part, :]
         col_top = jnp.maximum(col_top, jnp.max(fold(x), axis=0))
-        at = pl.ds(row_at(idx, block, nz, part), part)
+        at = pl.ds(row_at(block, nz, part), part)
         hit = lax.broadcasted_iota(jnp.int32, x.shape, 1) == column[at, 0:1].astype(jnp.int32)
         paired = jnp.where(hit, x, 0.0)
         col_pos += jnp.sum(fold(paired), axis=0)
@@ -214,7 +228,8 @@
     total = jnp.sum(total, axis=0, keepdims=True)
     moment = jnp.sum(moment, axis=0, keepdims=True)
     pos = jnp.sum(col_pos, axis=0, keepdims=True)
-    packed[...] = pack([top + jnp.log(total), moment / total, pos])
+    packed[:24, :] = pack([top + jnp.log(total), moment / total, pos])
+    packed[24:, :] = jnp.zeros((packed.shape[0] - 24, LANES), F32)
     for p in range(outs[2].shape[0]):
         sender.send(packed, outs[2].at[p])
 
@@ -249,57 +264,70 @@
 
 
 def grad_kernel(count, nz, ins, held, outs, sender, column, grad, turned):
-    idx, scale, col_got, chip, across, mine, theirs, pairs, logits, txt, images = ins
-    text, send, first, row_loss, col_loss, sums = held
-    half, embed = send.shape
+    scale, col_got, chip, across, mine, theirs, pairs, logits, txt, images = ins
+    text, first, row_loss, col_loss, sums, send = held
     rows, cols = grad.shape
+    half = rows // 2
+    peers, embed = text.shape[0], images.ref.shape[1]
     part = rows // (NC * nz)
     s = scale[0]
     used = lax.broadcasted_iota(jnp.int32, (8, LANES), 0) < count
     row_lse, row_mean, row_pos = merge([r.get()[...] for r in (chip, across, mine, theirs)])
     row_loss[...] = row_lse - row_pos
-    sender.send(row_loss, outs[3])
+    sender.send(row_loss, outs[2])
     row_total = total_of(jnp.where(used, 0.5 * row_mean - row_pos, 0.0))
     col_ref = col_got.get()
     col_lse, col_mean, col_pos = merge([col_ref[p] for p in range(col_ref.shape[0])])
     col_loss[...] = col_lse - col_pos
-    sender.send(col_loss, outs[4])
+    sender.send(col_loss, outs[3])
     col_total = total_of(jnp.where(used, 0.5 * col_mean, 0.0))
     sums[...] = jnp.broadcast_to(col_total, sums.shape)
-    sender.send(sums, outs[5])
-    text[:, embed:] = split_tail(jnp.broadcast_to(row_total, (1, LANES)), cols)
-    sender.send(text.at[:, embed:], outs[0].at[:, embed:])
+    sender.send(sums, outs[4])
+    send[:, embed:] = split_tail(jnp.broadcast_to(col_total, (1, LANES)), half)
+    sender.send(send.at[:, embed:], outs[5].at[:, embed:])
+    last = embed // LANES * part
+    text[:, last:, :] = jnp.broadcast_to(
+        split_tail(jnp.broadcast_to(row_total, (1, LANES)), text.shape[1] - last)[None],
+        (peers, text.shape[1] - last, LANES),
+    )
+    sender.send(text.at[:, last:], outs[0].at[:, last:])
     flat = unpack(col_lse, count)
     column[...] = tall([unpack(row_lse, count), unpack(pairs.get(), count)])
 
     for i, block in enumerate(order_of(nz)):
         logits.part(i)
+        if i == nz // 2:
+            txt.start()
+        if i == nz:
+            images.start()
         x = logits.ref[i * part : (i + 1) * part, :]
-        at = pl.ds(row_at(idx, block, nz, part), part)
+        at = pl.ds(row_at(block, nz, part), part)
         hit = lax.broadcasted_iota(jnp.int32, x.shape, 1) == column[at, 1:2].astype(jnp.int32)
         value = 0.5 * (jnp.exp(x - column[at, 0:1]) + jnp.exp(x - flat)) - jnp.where(hit, 1.0, 0.0)
         grad[i * part : (i + 1) * part, :] = (s * value).astype(BF16)
     first[...] = grad[:half, :]
-    sender.send(first, outs[2])
-
-    cuts = range(0, embed, 256)
-    for i, n in enumerate(cuts):
+    sender.send(first, outs[1])
+
+    for i, n in enumerate(range(0, embed, 256)):
         txt.part(i)
         send[:, n : n + 256] = dot(grad[half:, :], txt.ref[:, n : n + 256], ((1,), (0,))).astype(BF16)
-        sender.send(send.at[:, n : n + 256], outs[1].at[:, n : n + 256])
+        sender.send(send.at[:, n : n + 256], outs[5].at[:, n : n + 256])
     turned[...] = grad[...].T
     images = images.get()
-    for n in cuts:
-        text[:, n : n + 256] = dot(turned[...], images[:, n : n + 256], ((1,), (0,))).astype(BF16)
-        sender.send(text.at[:, n : n + 256], outs[0].at[:, n : n + 256])
+    for n in range(0, embed, 256):
+        block = dot(turned[...], images[:, n : n + 256], ((1,), (0,))).reshape(peers, part, 256)
+        at = n // LANES * part
+        text[:, at : at + part, :] = block[:, :, :LANES].astype(BF16)
+        text[:, at + part : at + 2 * part, :] = block[:, :, LANES:].astype(BF16)
+        sender.send(text.at[:, at : at + 2 * part], outs[0].at[:, at : at + 2 * part])
 
 
 def image_kernel(ins, held, outs, sender):
-    sums, other_sums, first, txt, received = ins
-    total = sums.get()[0:1, :] + other_sums.get()[0:1, :]
-    grad = first.get()
-    embed = received.ref.shape[1]
-    for i, n in enumerate(range(0, embed, 256)):
+    sums, grad, txt, received = ins
+    embed = txt.ref.shape[1]
+    cuts = range(0, embed, 256)
+    grad = grad.get()
+    for i, n in enumerate(cuts):
         txt.part(i)
         received.part(i)
         block = dot(grad[...], txt.ref[:, n : n + 256], ((1,), (0,)))
@@ -309,46 +337,59 @@
             size = ref.shape[0]
             ref[:, n : n + 256] = block[at : at + size].astype(ref.dtype)
             at += size
+    received.part(len(cuts))
+    total = sums.get()[0:1, :] + tail_of(received.ref, embed)[0:1]
     for ref, out in zip(held, outs):
-        if ref.shape[1] > embed:
-            ref[:, embed:] = split_tail(total, ref.shape[0])
+        size = ref.shape[0]
+        ref[:, embed:] = split_tail(total, size) if ref.dtype == BF16 else jnp.broadcast_to(total, (size, LANES))
         sender.send(ref, out)
 
 
-def forward_kernel(idx, sums, other_sums, own, near_one, far_one, out):
-    part, embed = own.shape[0] // NC, own.shape[1]
-    total = own[...] + near_one[:, :embed].astype(F32)
+def forward_kernel(ins, held, outs, sender):
+    own, near_one, far_one = ins
+    (out,) = held
+    own, near_one, far_one = own.get(), near_one.get(), far_one.get()
+    part, embed = own.shape[0] // NC, own.shape[1] - LANES
+    total = own[:, :embed] + near_one[:, :embed].astype(F32)
     out[:part, :embed] = (total[:part] + far_one[:, :embed].astype(F32)).astype(BF16)
     out[part:, :embed] = total[part:].astype(BF16)
-    across = jnp.where(idx[0] == 0, 1.0, 0.0) * tail_of(far_one, embed)
-    tail = sums[0:1, :] + other_sums[0:1, :] + tail_of(near_one, embed)[0:1] + across[0:1]
+    across = jnp.where(lax.axis_index("c") == 0, 1.0, 0.0) * tail_of(far_one, embed)
+    tail = own[0:1, embed:] + tail_of(near_one, embed)[0:1] + across[0:1]
     out[:, embed:] = split_tail(tail, NC * part)
-
-
-def chip_sum_kernel(sums, other_sums, own, one, two, row_total, *refs):
+    sender.send(out, outs[0])
+
+
+def chip_sum_kernel(own, one, two, *refs):
     keep, send = refs[-2], refs[-1]
-    part, embed = own.shape
+    part, embed = own.shape[0], own.shape[1] - LANES
     total = one[:, :embed].astype(F32) + two[:, :embed].astype(F32)
     tail = tail_of(one, embed) + tail_of(two, embed)
     send[:, :embed] = total[part:]
     send[:, embed:] = jnp.zeros((part, LANES), F32)
     send[0:8, embed:] = jnp.broadcast_to(tail, (8, LANES))
-    keep[:, :embed] = own[...] + total[:part]
-    keep[:, embed:] = jnp.zeros((part, LANES), F32)
-    keep[0:8, embed:] = tail + sums[...] + other_sums[...] + row_total[...]
-
-
-def text_sum_kernel(got, out, total):
-    embed = out.shape[1]
-    out[...] = jnp.sum(got[:, :, :embed].astype(F32), axis=0)
-    tail = sum(tail_of(got.at[p], embed) for p in range(got.shape[0]))
-    total[...] = jnp.broadcast_to(tail, total.shape)
-
-
-def image_sum_kernel(scale, keep, received, out, temp):
+    keep[:, :embed] = own[:, :embed] + total[:part]
+    keep[:, embed:] = own[:, embed:]
+    keep[0:8, embed:] = tail + own[0:8, embed:]
+
+
+def image_sum_kernel(scale, keep, received, others, out, temp):
     embed = out.shape[1]
     out[...] = keep[:, :embed] + received[:, :embed]
-    temp[...] = (keep[0:1, embed : embed + 1] + received[0:1, embed : embed + 1]) * scale[0]
+    total = keep[0:8, embed:] + received[0:8, embed:] + others[...]
+    temp[...] = total[0:1, 0:1] * scale[0]
+
+
+def text_sum_kernel(got, unread, out, rows_total):
+    part = out.shape[0]
+    total = got[0].astype(F32)
+    for p in range(1, got.shape[0]):
+        total = total + got[p].astype(F32)
+    for i in range(out.shape[1] // LANES):
+        out[:, i * LANES : (i + 1) * LANES] = total[i * part : (i + 1) * part]
+    tail = total[out.shape[1] // LANES * part :][0:8]
+    lane = lax.broadcasted_iota(jnp.int32, tail.shape, 1)
+    tail = jnp.sum(jnp.where(lane < 3, tail, 0.0), axis=1, keepdims=True)
+    rows_total[...] = jnp.broadcast_to(tail, rows_total.shape)
 
 
 def local(image_embed, text_embed, pair_col, log_scale):
@@ -361,7 +402,6 @@
     batch = peers * rows
     c = lax.axis_index("c")
     z = lax.axis_index("z")
-    idx = jnp.stack([c, z])
     scale = jnp.exp(log_scale)
     scale1 = scale[None]
     sds = jax.ShapeDtypeStruct
@@ -398,20 +438,21 @@
 
     work = 2 * rows * cols * embed
     tile, pad = sds((24, LANES), F32), sds((8, LANES), F32)
+    message = sds((MESSAGE, LANES), F32)
     logits, stat, msg = call(
         functools.partial(logits_kernel, nz),
-        (sds((rows, cols), F32), tile, sds((peers, 24, LANES), F32)),
-        idx,
+        (sds((rows, cols), F32), tile, sds((peers, MESSAGE, LANES), F32)),
         scale1,
         pairs,
         txt,
         *images,
         flops=work,
-        smem=(0, 1),
-        cuts={3: (0, 256)},
-        joined=4,
-        held=(None, None, tile),
-        sends=2 + peers,
+        smem=(0,),
+        cuts={2: (0, 256)},
+        joined=3,
+        later=(2, 3),
+        held=(None, None, message),
+        sends=1 + cols // 256 + peers,
         scratch=[vmem((rows, 8), F32), vmem((rows, LANES), F32)],
     )
     col_got = lax.all_to_all(msg, XY, 0, 0)
@@ -420,10 +461,10 @@
     merged = jnp.concatenate(merge(stats[1:]))
 
     wide = embed + LANES
-    text_term, send, first, row_loss, col_loss, sums = call(
+    high = embed // LANES * part + 16
+    text_term, first, row_loss, col_loss, sums, send = call(
         functools.partial(grad_kernel, count, nz),
-        (sds((cols, wide), BF16), sds((half, embed), BF16), sds((half, cols), BF16), pad, pad, pad),
-        idx,
+        (sds((peers, high, LANES), BF16), sds((half, cols), BF16), pad, pad, pad, sds((half, wide), BF16)),
         scale1,
         col_got,
         chip_stat,
@@ -435,69 +476,51 @@
         txt,
         *images,
         flops=2 * work,
-        smem=(0, 1),
-        cuts={8: (0, part), 9: (1, 256)},
-        joined=10,
-        sends=5 + 2 * (embed // 256),
+        smem=(0,),
+        cuts={7: (0, part), 8: (1, 256)},
+        joined=9,
+        later=(8, 9),
         scratch=[vmem((rows, 8), F32), vmem((rows, cols), BF16), vmem((cols, rows), BF16)],
     )
     received = swap(send)
-    other_sums = swap(sums)
-    text_got = lax.all_to_all(text_term.reshape(peers, part, wide), XY, 0, 0)
+    text_got = lax.all_to_all(text_term, XY, 0, 0)
+    chip_rows = sds((NC * part, wide), BF16)
     one, two, three, four, own = call(
         image_kernel,
-        (
-            sds((NC * part, wide), BF16),
-            sds((NC * part, embed), F32),
-            sds((NC * part, wide), BF16),
-            sds((part, wide), BF16),
-            sds((part, embed), F32),
-        ),
+        (chip_rows, sds((NC * part, wide), F32), chip_rows, sds((part, wide), BF16), sds((part, wide), F32)),
         sums,
-        other_sums,
         first,
         txt,
         received,
         flops=work // 2,
-        cuts={3: (1, 256), 4: (1, 256)},
+        cuts={2: (1, 256), 3: (1, 256)},
+        spare=6 << 20,
     )
-    two = near(
-        forward_kernel,
-        sds((NC * part, wide), BF16),
-        idx,
-        sums,
-        other_sums,
-        two,
-        onward(three, 1),
-        onward(four, 2),
-        smem=(0,),
-    )
+    two = call(forward_kernel, chip_rows, two, onward(three, 1), onward(four, 2), spare=VMEM_BYTES // 2)
     row_loss = lax.dynamic_slice(row_loss, (c * (count // NC), 0), (count // NC, LANES)).reshape(-1)
     col_loss = col_loss[:count].reshape(peers, 1, part)
     other = swap(col_loss)
     col_loss = jnp.where(
         c == 0, jnp.concatenate([col_loss, other], 1), jnp.concatenate([other, col_loss], 1)
     ).reshape(-1)
-    grad_text, row_total = near(text_sum_kernel, (sds((part, embed), F32), pad), text_got)
-    keep, send = near(
+    keep, send = small(
         chip_sum_kernel,
         (sds((part, wide), F32), sds((part, wide), F32)),
-        sums,
-        other_sums,
         own,
         onward(one, 1),
         onward(two, 2),
-        row_total,
         row_loss,
         col_loss,
-        unread=(6, 7),
+        unread=(3, 4),
     )
-    grad_image, temp = near(
+    grad_text, row_total = small(text_sum_kernel, (sds((part, embed), F32), pad), text_got, send, unread=(1,))
+    grad_image, temp = small(
         image_sum_kernel,
         (sds((part, embed), F32), sds((1, 1), F32)),
         jnp.full((1,), 1.0 / batch, F32),
         keep,
         swap(send),
+        row_total,
         smem=(0,),
     )
     return (row_loss, col_loss, grad_image, grad_text, temp[0, 0])

time: 127 us -> 121 us (0.953)
  waiting for transfers between devices: 23 us -> 27.4 us
  Pallas kernels: 28.4 us -> 24.9 us
  local copies, waits for them, and re-layouts: 11.1 us -> 8.14 us
  starting transfers between devices: 60.8 us -> 58 us
    ppermute x4, waiting for transfers between devices: 5.82 us -> 10.2 us  [onward(): lax.ppermute(x, CZ, pairs + [(nz + (i + k) % nz, nz + i) for i in range(n...]
    ppermute x12 -> x11, starting transfers between devices: 19 us -> 15.1 us  [swap(): return lax.ppermute(x, 'c', SWAP)]
    ppermute x12 -> x11, waiting for transfers between devices: 6.11 us -> 2.47 us  [swap(): return lax.ppermute(x, 'c', SWAP)]
    pallas_call x4 -> x3, Pallas kernels: 4.16 us -> 1.86 us  [small(): pl.pallas_call(body, out_shape=out_shape, in_specs=[spec(i) for i in rang...]
    ppermute x8, waiting for transfers between devices: 8.26 us -> 10.4 us  [ahead(): lax.ppermute(x, CZ, pairs + [(nz + i, nz + (i + k) % nz) for i in range(n...]
    all_to_all x1, waiting for transfers between devices: 0.92 us -> 2.96 us  [local(): text_got = lax.all_to_all(text_term, XY, 0, 0)]
    unnamed x55 -> x43, local copies, waits for them, and re-layouts: 6.59 us -> 5.02 us
    pallas_call x3 -> x4, Pallas kernels: 24.2 us -> 23.1 us  [call(): pl.pallas_call(kernel, out_shape=out_shape, in_specs=[scalars if i in sme...]
  transfers between devices with their start and end apart: 27 -> 26, of which waited for: 14 -> 12; matrix products, arithmetic and copies ran while one was open for 2% -> 1% of each run, Pallas kernels for 7% -> 6%
where the time goes in v4:
time: 121 us
  starting transfers between devices  58 us (48%)
  waiting for transfers between devices  27.4 us (23%)
  Pallas kernels  24.9 us (21%)
  local copies, waits for them, and re-layouts  8.14 us (7%)
  between operations  1.62 us (1%)
    pallas_call x4, Pallas kernels, call(): pl.pallas_call(kernel, out_shape=out_shape, in_specs=[scalars if i in sme...  23.1 us
    ppermute x8, starting transfers between devices, ahead(): lax.ppermute(x, CZ, pairs + [(nz + i, nz + (i + k) % nz) for i in range(n...  16.3 us
    ppermute x11, starting transfers between devices, swap(): return lax.ppermute(x, 'c', SWAP)  15.1 us
    ppermute x8, waiting for transfers between devices, ahead(): lax.ppermute(x, CZ, pairs + [(nz + i, nz + (i + k) % nz) for i in range(n...  10.4 us
    ppermute x4, waiting for transfers between devices, onward(): lax.ppermute(x, CZ, pairs + [(nz + (i + k) % nz, nz + i) for i in range(n...  10.2 us
    all_to_all x1, starting transfers between devices, local(): txt = lax.all_to_all(spread, XY, 0, 0).reshape(cols, embed)  7.76 us
    ppermute x4, starting transfers between devices, onward(): lax.ppermute(x, CZ, pairs + [(nz + (i + k) % nz, nz + i) for i in range(n...  7.56 us
    all_to_all x1, starting transfers between devices, local(): text_got = lax.all_to_all(text_term, XY, 0, 0)  6.82 us
  transfers between devices with their start and end apart: 26, of which 12 were waited for; matrix products, arithmetic and copies ran while one was open for 1% of the time, Pallas kernels for 6%

profile of v4, /device:TPU:1, one launch (start us, length us, event | category | flops | bytes accessed | tf_op | source)
XLA Modules:
  0.0 120.9 jit_solution(14714698700995057310)
XLA Ops:
  0.6 2.3 %broadcast_in_dim.16 = bf16[16,48,1280]{2,1,0:T(8,128)(2,1)} broadcast(bf16[48,1280]{1,0:T(8,128)(2,1)} %param.5), dimensions={1,2} | broadcast | bytes 2088960 | tf_op jit(solution)/shard_map/broadcast_in_dim | solution.py:422
  3.0 7.8 %all-to-all-start = ((bf16[16,48,1280]{2,1,0:T(8,128)(2,1)}), bf16[16,48,1280]{2,1,0:T(8,128)(2,1)}, u32[]{:S(2)}, u32[]{:S(2)}) async-start(bf16[16,48,1280]{2,1,0:T(8,128)(2,1)} %broadcast_in_dim.16), calls=%async_computation | async-start | bytes 3932160 | tf_op jit(solution)/shard_map/all_to_all | solution.py:423
  10.8 1.0 collective-permute-start.1
  11.8 1.0 collective-permute-done.1.refs_12_.refs_18_
  12.8 0.6 copy-done.6
  13.4 3.1 %collective-permute-start.3 = (bf16[96,1280]{1,0:T(8,128)(2,1)S(1)}, bf16[96,1280]{1,0:T(8,128)(2,1)S(1)}, u32[]{:S(2)}, u32[]{:S(2)}) collective-permute-start(bf16[96,1280]{1,0:T(8,128)(2,1)S(1)} %constant_dynamic-update-slice_fusion), channel_id=1, source_target_pairs={{2,0},{3,1},{4,2},{5,3},{6,4},{7,5},{0,6},{1,7},{8,10},{9,11},{10,... | collective-permute-start | bytes 737288 | tf_op jit(solution)/shard_map/ppermute | solution.py:416
  16.5 1.6 %collective-permute-start.2 = (bf16[96,1280]{1,0:T(8,128)(2,1)S(1)}, bf16[96,1280]{1,0:T(8,128)(2,1)S(1)}, u32[]{:S(2)}, u32[]{:S(2)}) collective-permute-start(bf16[96,1280]{1,0:T(8,128)(2,1)S(1)} %constant_dynamic-update-slice_fusion), channel_id=1, source_target_pairs={{1,0},{2,1},{3,2},{4,3},{5,4},{6,5},{7,6},{0,7},{8,9},{9,10},{10,1... | collective-permute-start | bytes 737288 | tf_op jit(solution)/shard_map/ppermute | solution.py:416
  18.1 6.0 %collective-permute-done.3.refs_4_.refs_10_ = bf16[96,1280]{1,0:T(8,128)(2,1)S(1)} collective-permute-done((bf16[96,1280]{1,0:T(8,128)(2,1)S(1)}, bf16[96,1280]{1,0:T(8,128)(2,1)S(1)}, u32[]{:S(2)}, u32[]{:S(2)}) %collective-permute-start.3) | collective-permute-done | bytes 245792 | tf_op jit(solution)/shard_map/ppermute | solution.py:416
  24.1 2.8 %collective-permute-start.4 = (bf16[96,1280]{1,0:T(8,128)(2,1)S(1)}, bf16[96,1280]{1,0:T(8,128)(2,1)S(1)}, u32[]{:S(2)}, u32[]{:S(2)}) collective-permute-start(bf16[96,1280]{1,0:T(8,128)(2,1)S(1)} %collective-permute-done.3.refs_4_.refs_10_), channel_id=1, source_target_pairs={{1,0},{2,1},{3,2},{4,3},{5,4},{6,5},{7,6},{0,7},{8,9},{9,10},{10,1... | collective-permute-start | bytes 737288 | tf_op jit(solution)/shard_map/ppermute | solution.py:416
  26.9 0.1 collective-permute-start.5
  27.0 4.3 %collective-permute-start.7 = (bf16[96,1280]{1,0:T(8,128)(2,1)S(1)}, bf16[96,1280]{1,0:T(8,128)(2,1)S(1)}, u32[]{:S(2)}, u32[]{:S(2)}) collective-permute-start(bf16[96,1280]{1,0:T(8,128)(2,1)S(1)} %collective-permute-done.3.refs_4_.refs_10_), channel_id=1, source_target_pairs={{0,8},{8,0},{1,9},{9,1},{2,10},{10,2},{3,11},{11,3},{4,12},{12,4},... | collective-permute-start | bytes 737288 | tf_op jit(solution)/shard_map/ppermute | solution.py:412
  31.4 0.1 collective-permute-start.6
  31.4 0.2 collective-permute-done.4.refs_5_.refs_11_
  31.6 1.4 %collective-permute-start.8 = (bf16[96,1280]{1,0:T(8,128)(2,1)S(1)}, bf16[96,1280]{1,0:T(8,128)(2,1)S(1)}, u32[]{:S(2)}, u32[]{:S(2)}) collective-permute-start(bf16[96,1280]{1,0:T(8,128)(2,1)S(1)} %collective-permute-done.4.refs_5_.refs_11_), channel_id=1, source_target_pairs={{0,8},{8,0},{1,9},{9,1},{2,10},{10,2},{3,11},{11,3},{4,12},{12,4},... | collective-permute-start | bytes 737288 | tf_op jit(solution)/shard_map/ppermute | solution.py:412
  33.0 0.1 collective-permute-start
  33.8 0.8 collective-permute-done.5.refs_6_.refs_12_
  34.7 1.7 %collective-permute-start.9 = (bf16[48,1280]{1,0:T(8,128)(2,1)S(1)}, bf16[48,1280]{1,0:T(8,128)(2,1)S(1)}, u32[]{:S(2)}, u32[]{:S(2)}) collective-permute-start(bf16[48,1280]{1,0:T(8,128)(2,1)S(1)} %collective-permute-done.5.refs_6_.refs_12_), channel_id=1, source_target_pairs={{0,8},{8,0},{1,9},{9,1},{2,10},{10,2},{3,11},{11,3},{4,12},{12,4},... | collective-permute-start | bytes 368648 | tf_op jit(solution)/shard_map/ppermute | solution.py:412
  36.3 0.0 collective-permute-done
  36.3 0.6 pad_bitcast_fusion.refs_1_.refs_6_
  36.9 0.4 collective-permute-done.9.refs_11_.refs_17_
  37.3 0.0 collective-permute-done.7.refs_9_.refs_15_
  37.3 0.0 collective-permute-done.8.refs_10_.refs_16_
  37.4 0.7 copy-done.15
  38.1 1.4 %all-to-all-done = bf16[16,48,1280]{2,1,0:T(8,128)(2,1)} async-done(((bf16[16,48,1280]{2,1,0:T(8,128)(2,1)}), bf16[16,48,1280]{2,1,0:T(8,128)(2,1)}, u32[]{:S(2)}, u32[]{:S(2)}) %all-to-all-start) | async-done | bytes 1966112 | tf_op jit(solution)/shard_map/all_to_all | solution.py:423
  39.5 7.4 %shard_map.83 = (f32[768,768]{1,0:T(8,128)}, f32[24,128]{1,0:T(8,128)}, f32[16,48,128]{2,1,0:T(8,128)}) custom-call(f32[1]{0:T(128)} %bitcast.refs_0_, f32[8,128]{1,0:T(8,128)} %pad_bitcast_fusion.refs_1_.refs_6_, bf16[768,1280]{1,0:T(8,128)(2,1)} %bitcast.2.refs_2_.refs_8_, bf16[96,1280]{1,0:T(8,128)(2,1)} %copy-done.13, bf16[96,1280]{1,0:T(8,128)(2,1)} %copy-done.7, ...), custom_call_target="tpu_custom_call" | custom-call | flops 1509949440 | bytes 3936260 | tf_op jit(solution)/shard_map/pallas_call | solution.py:110
  46.9 2.2 %collective-permute-start.10 = (f32[24,128]{1,0:T(8,128)}, f32[24,128]{1,0:T(8,128)S(1)}, u32[]{:S(2)}, u32[]{:S(2)}) collective-permute-start(f32[24,128]{1,0:T(8,128)} %get-tuple-element.26), channel_id=1, source_target_pairs={{0,8},{8,0},{1,9},{9,1},{2,10},{10,2},{3,11},{11,3},{4,12},{12,4},... | collective-permute-start | bytes 36872 | tf_op jit(solution)/shard_map/ppermute | solution.py:412
  49.1 4.5 %all-to-all-start.1 = ((f32[16,48,128]{2,1,0:T(8,128)}), f32[16,48,128]{2,1,0:T(8,128)}, u32[]{:S(2)}, u32[]{:S(2)}) async-start(f32[16,48,128]{2,1,0:T(8,128)} %get-tuple-element.25), calls=%async_computation.1 | async-start | bytes 786432 | tf_op jit(solution)/shard_map/all_to_all | solution.py:458
  53.6 0.0 collective-permute-done.10
  53.6 0.7 log_add_fusion.1
  54.3 1.5 %collective-permute-start.14 = (f32[24,128]{1,0:T(8,128)S(1)}, f32[24,128]{1,0:T(8,128)S(1)}, u32[]{:S(2)}, u32[]{:S(2)}) collective-permute-start(f32[24,128]{1,0:T(8,128)S(1)} %pad_maximum_fusion.refs_2_), channel_id=1, source_target_pairs={{1,0},{2,1},{3,2},{4,3},{5,4},{6,5},{7,6},{0,7},{8,9},{9,10},{10,1... | collective-permute-start | bytes 36872 | tf_op jit(solution)/shard_map/ppermute | solution.py:416
  55.8 3.0 %collective-permute-start.13 = (f32[24,128]{1,0:T(8,128)S(1)}, f32[24,128]{1,0:T(8,128)S(1)}, u32[]{:S(2)}, u32[]{:S(2)}) collective-permute-start(f32[24,128]{1,0:T(8,128)S(1)} %pad_maximum_fusion.refs_2_), channel_id=1, source_target_pairs={{2,0},{3,1},{4,2},{5,3},{6,4},{7,5},{0,6},{1,7},{8,10},{9,11},{10,... | collective-permute-start | bytes 36872 | tf_op jit(solution)/shard_map/ppermute | solution.py:416
  58.8 3.8 %collective-permute-start.12 = (f32[24,128]{1,0:T(8,128)S(1)}, f32[24,128]{1,0:T(8,128)S(1)}, u32[]{:S(2)}, u32[]{:S(2)}) collective-permute-start(f32[24,128]{1,0:T(8,128)S(1)} %pad_maximum_fusion.refs_2_), channel_id=1, source_target_pairs={{3,0},{4,1},{5,2},{6,3},{7,4},{0,5},{1,6},{2,7},{8,11},{9,12},{10,... | collective-permute-start | bytes 36872 | tf_op jit(solution)/shard_map/ppermute | solution.py:416
  62.6 0.5 collective-permute-start.11
  63.1 0.0 collective-permute-done.14
  63.1 0.0 collective-permute-done.13
  63.1 1.3 %collective-permute-done.12 = f32[24,128]{1,0:T(8,128)S(1)} collective-permute-done((f32[24,128]{1,0:T(8,128)S(1)}, f32[24,128]{1,0:T(8,128)S(1)}, u32[]{:S(2)}, u32[]{:S(2)}) %collective-permute-start.12) | collective-permute-done | bytes 12320 | tf_op jit(solution)/shard_map/ppermute | solution.py:416
  64.4 2.8 %collective-permute-start.15 = (f32[24,128]{1,0:T(8,128)S(1)}, f32[24,128]{1,0:T(8,128)}, u32[]{:S(2)}, u32[]{:S(2)}) collective-permute-start(f32[24,128]{1,0:T(8,128)S(1)} %pad_maximum_fusion.1.refs_4_), channel_id=1, source_target_pairs={{0,8},{8,0},{1,9},{9,1},{2,10},{10,2},{3,11},{11,3},{4,12},{12,4},... | collective-permute-start | bytes 36872 | tf_op jit(solution)/shard_map/ppermute | solution.py:412
  67.1 2.1 %collective-permute-done.11.refs_3_ = f32[24,128]{1,0:T(8,128)S(1)} collective-permute-done((f32[24,128]{1,0:T(8,128)S(1)}, f32[24,128]{1,0:T(8,128)S(1)}, u32[]{:S(2)}, u32[]{:S(2)}) %collective-permute-start.11) | collective-permute-done | bytes 12320 | tf_op jit(solution)/shard_map/ppermute | solution.py:416
  69.3 0.6 copy-done.20
  69.9 9.5 %shard_map.84 = (bf16[16,496,128]{2,1,0:T(8,128)(2,1)}, bf16[384,768]{1,0:T(8,128)(2,1)}, f32[8,128]{1,0:T(8,128)}, f32[8,128]{1,0:T(8,128)}, f32[8,128]{1,0:T(8,128)}, /*index=5*/bf16[384,1408]{1,0:T(8,128)(2,1)}) custom-call(f32[1]{0:T(128)} %bitcast.refs_0_, f32[16,48,128]{2,1,0:T(8,128)} %all-to-all-done.1.refs_1_, f32[24,128]{1,0:T(8,128)} %copy-done.8, ...), custom_call_target="tpu_custom_call" | custom-call | flops 3019898880 | bytes 6737924 | tf_op jit(solution)/shard_map/pallas_call | solution.py:110
  79.4 0.5 collective-permute-start.17
  79.9 6.8 %all-to-all-start.2 = ((bf16[16,496,128]{2,1,0:T(8,128)(2,1)}), bf16[16,496,128]{2,1,0:T(8,128)(2,1)S(1)}, u32[]{:S(2)}, u32[]{:S(2)}) async-start(bf16[16,496,128]{2,1,0:T(8,128)(2,1)} %get-tuple-element.40), calls=%async_computation.2 | async-start | bytes 4063232 | tf_op jit(solution)/shard_map/all_to_all | solution.py:486
  86.8 1.0 copy-done.4
  87.8 5.6 %shard_map.85 = (bf16[96,1408]{1,0:T(8,128)(2,1)}, f32[96,1408]{1,0:T(8,128)}, bf16[96,1408]{1,0:T(8,128)(2,1)}, bf16[48,1408]{1,0:T(8,128)(2,1)}, f32[48,1408]{1,0:T(8,128)}) custom-call(f32[8,128]{1,0:T(8,128)} %get-tuple-element.30.refs_0_, bf16[384,768]{1,0:T(8,128)(2,1)} %get-tuple-element.31.refs_1_, bf16[768,1280]{1,0:T(8,128)(2,1)} %bitcast.2.refs_2_.refs_8_, ...), custom_call_target="tpu_custom_call" | custom-call | flops 754974720 | bytes 3641344 | tf_op jit(solution)/shard_map/pallas_call | solution.py:110
  93.3 1.1 collective-permute-start.19
  94.4 3.4 %collective-permute-start.20 = (bf16[48,1408]{1,0:T(8,128)(2,1)}, bf16[48,1408]{1,0:T(8,128)(2,1)S(1)}, u32[]{:S(2)}, u32[]{:S(2)}) collective-permute-start(bf16[48,1408]{1,0:T(8,128)(2,1)} %get-tuple-element.37), channel_id=1, source_target_pairs={{0,2},{1,3},{2,4},{3,5},{4,6},{5,7},{6,0},{7,1},{10,8},{11,9},{12,... | collective-permute-start | bytes 405512 | tf_op jit(solution)/shard_map/ppermute | solution.py:420
  97.9 0.8 collective-permute-start.18
  98.6 4.6 %collective-permute-done.20.refs_2_ = bf16[48,1408]{1,0:T(8,128)(2,1)S(1)} collective-permute-done((bf16[48,1408]{1,0:T(8,128)(2,1)}, bf16[48,1408]{1,0:T(8,128)(2,1)S(1)}, u32[]{:S(2)}, u32[]{:S(2)}) %collective-permute-start.20) | collective-permute-done | bytes 135200 | tf_op jit(solution)/shard_map/ppermute | solution.py:420
  103.2 1.0 copy-done
  104.3 0.6 shard_map.86
  104.9 2.3 %collective-permute-start.21 = (bf16[96,1408]{1,0:T(8,128)(2,1)S(1)}, bf16[96,1408]{1,0:T(8,128)(2,1)S(1)}, u32[]{:S(2)}, u32[]{:S(2)}) collective-permute-start(bf16[96,1408]{1,0:T(8,128)(2,1)S(1)} %shard_map.86), channel_id=1, source_target_pairs={{0,2},{1,3},{2,4},{3,5},{4,6},{5,7},{6,0},{7,1},{10,8},{11,9},{12,... | collective-permute-start | bytes 811016 | tf_op jit(solution)/shard_map/ppermute | solution.py:420
  107.1 0.1 reshape.31
  107.2 0.0 collective-permute-start.16
  107.3 0.0 copy-start.3
  107.3 1.1 collective-permute-done.16
  108.5 0.1 select_n.71.refs_1_
  108.5 0.0 collective-permute-done.18.one
  108.6 5.6 %collective-permute-done.21.two = bf16[96,1408]{1,0:T(8,128)(2,1)S(1)} collective-permute-done((bf16[96,1408]{1,0:T(8,128)(2,1)S(1)}, bf16[96,1408]{1,0:T(8,128)(2,1)S(1)}, u32[]{:S(2)}, u32[]{:S(2)}) %collective-permute-start.21) | collective-permute-done | bytes 270368 | tf_op jit(solution)/shard_map/ppermute | solution.py:420
  114.2 1.0 copy-done.1
  115.1 0.1 shard_map.87
  115.2 1.0 collective-permute-start.22
  116.2 3.0 %all-to-all-done.2.got = bf16[16,496,128]{2,1,0:T(8,128)(2,1)S(1)} async-done(((bf16[16,496,128]{2,1,0:T(8,128)(2,1)}), bf16[16,496,128]{2,1,0:T(8,128)(2,1)S(1)}, u32[]{:S(2)}, u32[]{:S(2)}) %all-to-all-start.2) | async-done | bytes 2031648 | tf_op jit(solution)/shard_map/all_to_all | solution.py:486
  119.1 1.0 shard_map.88
  120.2 0.7 shard_map.89
  (53 shorter events, 0.2 us)
Async XLA Ops:
  3.0 7.8 %copy-start.5 = (bf16[48,1280]{1,0:T(8,128)(2,1)S(1)}, bf16[48,1280]{1,0:T(8,128)(2,1)}, u32[]{:S(2)}) copy-start(bf16[48,1280]{1,0:T(8,128)(2,1)} %refs_13_.1) | copy-start | bytes 368644
  3.0 23.9 %copy-start.10 = (s32[384]{0:T(512)S(1)}, s32[384]{0:T(512)}, u32[]{:S(2)}) copy-start(s32[384]{0:T(512)} %param.6) | copy-start | bytes 4612
  3.0 36.5 %all-to-all-start = ((bf16[16,48,1280]{2,1,0:T(8,128)(2,1)}), bf16[16,48,1280]{2,1,0:T(8,128)(2,1)}, u32[]{:S(2)}, u32[]{:S(2)}) async-start(bf16[16,48,1280]{2,1,0:T(8,128)(2,1)} %broadcast_in_dim.16), calls=%async_computation | async-start | bytes 3932160 | tf_op jit(solution)/shard_map/all_to_all | solution.py:423
  10.8 2.0 %collective-permute-start.1 = (bf16[48,1280]{1,0:T(8,128)(2,1)S(1)}, bf16[48,1280]{1,0:T(8,128)(2,1)S(1)}, u32[]{:S(2)}, u32[]{:S(2)}) collective-permute-start(bf16[48,1280]{1,0:T(8,128)(2,1)S(1)} %copy-done.5), channel_id=1, source_target_pairs={{0,8},{8,0},{1,9},{9,1},{2,10},{10,2},{3,11},{11,3},{4,12},{12,4},... | collective-permute-start | bytes 368648 | tf_op jit(solution)/shard_map/ppermute | solution.py:412
  12.8 0.6 copy-start.6
  13.4 10.7 %collective-permute-start.3 = (bf16[96,1280]{1,0:T(8,128)(2,1)S(1)}, bf16[96,1280]{1,0:T(8,128)(2,1)S(1)}, u32[]{:S(2)}, u32[]{:S(2)}) collective-permute-start(bf16[96,1280]{1,0:T(8,128)(2,1)S(1)} %constant_dynamic-update-slice_fusion), channel_id=1, source_target_pairs={{2,0},{3,1},{4,2},{5,3},{6,4},{7,5},{0,6},{1,7},{8,10},{9,11},{10,... | collective-permute-start | bytes 737288 | tf_op jit(solution)/shard_map/ppermute | solution.py:416
  16.5 14.9 %collective-permute-start.2 = (bf16[96,1280]{1,0:T(8,128)(2,1)S(1)}, bf16[96,1280]{1,0:T(8,128)(2,1)S(1)}, u32[]{:S(2)}, u32[]{:S(2)}) collective-permute-start(bf16[96,1280]{1,0:T(8,128)(2,1)S(1)} %constant_dynamic-update-slice_fusion), channel_id=1, source_target_pairs={{1,0},{2,1},{3,2},{4,3},{5,4},{6,5},{7,6},{0,7},{8,9},{9,10},{10,1... | collective-permute-start | bytes 737288 | tf_op jit(solution)/shard_map/ppermute | solution.py:416
  24.1 10.5 %copy-start.7 = (bf16[96,1280]{1,0:T(8,128)(2,1)}, bf16[96,1280]{1,0:T(8,128)(2,1)S(1)}, u32[]{:S(2)}) copy-start(bf16[96,1280]{1,0:T(8,128)(2,1)S(1)} %collective-permute-done.3.refs_4_.refs_10_) | copy-start | bytes 737284
  24.1 7.5 %collective-permute-start.4 = (bf16[96,1280]{1,0:T(8,128)(2,1)S(1)}, bf16[96,1280]{1,0:T(8,128)(2,1)S(1)}, u32[]{:S(2)}, u32[]{:S(2)}) collective-permute-start(bf16[96,1280]{1,0:T(8,128)(2,1)S(1)} %collective-permute-done.3.refs_4_.refs_10_), channel_id=1, source_target_pairs={{1,0},{2,1},{3,2},{4,3},{5,4},{6,5},{7,6},{0,7},{8,9},{9,10},{10,1... | collective-permute-start | bytes 737288 | tf_op jit(solution)/shard_map/ppermute | solution.py:416
  26.9 7.7 %collective-permute-start.5 = (bf16[48,1280]{1,0:T(8,128)(2,1)S(1)}, bf16[48,1280]{1,0:T(8,128)(2,1)S(1)}, u32[]{:S(2)}, u32[]{:S(2)}) collective-permute-start(bf16[48,1280]{1,0:T(8,128)(2,1)S(1)} %slice.68), channel_id=1, source_target_pairs={{2,0},{3,1},{4,2},{5,3},{6,4},{7,5},{0,6},{1,7},{8,10},{9,11},{10,... | collective-permute-start | bytes 368648 | tf_op jit(solution)/shard_map/ppermute | solution.py:416
  27.0 10.3 %collective-permute-start.7 = (bf16[96,1280]{1,0:T(8,128)(2,1)S(1)}, bf16[96,1280]{1,0:T(8,128)(2,1)S(1)}, u32[]{:S(2)}, u32[]{:S(2)}) collective-permute-start(bf16[96,1280]{1,0:T(8,128)(2,1)S(1)} %collective-permute-done.3.refs_4_.refs_10_), channel_id=1, source_target_pairs={{0,8},{8,0},{1,9},{9,1},{2,10},{10,2},{3,11},{11,3},{4,12},{12,4},... | collective-permute-start | bytes 737288 | tf_op jit(solution)/shard_map/ppermute | solution.py:412
  31.4 6.0 %copy-start.13 = (bf16[96,1280]{1,0:T(8,128)(2,1)}, bf16[96,1280]{1,0:T(8,128)(2,1)S(1)}, u32[]{:S(2)}) copy-start(bf16[96,1280]{1,0:T(8,128)(2,1)S(1)} %collective-permute-done.2.refs_3_.refs_9_) | copy-start | bytes 737284
  31.4 6.0 %collective-permute-start.6 = (bf16[96,1280]{1,0:T(8,128)(2,1)S(1)}, bf16[96,1280]{1,0:T(8,128)(2,1)S(1)}, u32[]{:S(2)}, u32[]{:S(2)}) collective-permute-start(bf16[96,1280]{1,0:T(8,128)(2,1)S(1)} %collective-permute-done.2.refs_3_.refs_9_), channel_id=1, source_target_pairs={{0,8},{8,0},{1,9},{9,1},{2,10},{10,2},{3,11},{11,3},{4,12},{12,4},... | collective-permute-start | bytes 737288 | tf_op jit(solution)/shard_map/ppermute | solution.py:412
  31.6 5.7 %copy-start.14 = (bf16[96,1280]{1,0:T(8,128)(2,1)}, bf16[96,1280]{1,0:T(8,128)(2,1)S(1)}, u32[]{:S(2)}) copy-start(bf16[96,1280]{1,0:T(8,128)(2,1)S(1)} %collective-permute-done.4.refs_5_.refs_11_) | copy-start | bytes 737284
  31.6 5.7 %collective-permute-start.8 = (bf16[96,1280]{1,0:T(8,128)(2,1)S(1)}, bf16[96,1280]{1,0:T(8,128)(2,1)S(1)}, u32[]{:S(2)}, u32[]{:S(2)}) collective-permute-start(bf16[96,1280]{1,0:T(8,128)(2,1)S(1)} %collective-permute-done.4.refs_5_.refs_11_), channel_id=1, source_target_pairs={{0,8},{8,0},{1,9},{9,1},{2,10},{10,2},{3,11},{11,3},{4,12},{12,4},... | collective-permute-start | bytes 737288 | tf_op jit(solution)/shard_map/ppermute | solution.py:412
  33.0 3.3 %collective-permute-start = (f32[384]{0:T(512)S(1)}, f32[384]{0:T(512)S(1)}, u32[]{:S(2)}, u32[]{:S(2)}) collective-permute-start(f32[384]{0:T(512)S(1)} %and_select_fusion), channel_id=1, source_target_pairs={{0,8},{8,0},{1,9},{9,1},{2,10},{10,2},{3,11},{11,3},{4,12},{12,4},... | collective-permute-start | bytes 4616 | tf_op jit(solution)/shard_map/ppermute | solution.py:412
  34.7 4.8 %copy-start.18 = (bf16[48,1280]{1,0:T(8,128)(2,1)}, bf16[48,1280]{1,0:T(8,128)(2,1)S(1)}, u32[]{:S(2)}) copy-start(bf16[48,1280]{1,0:T(8,128)(2,1)S(1)} %collective-permute-done.5.refs_6_.refs_12_) | copy-start | bytes 368644
  34.7 2.7 %collective-permute-start.9 = (bf16[48,1280]{1,0:T(8,128)(2,1)S(1)}, bf16[48,1280]{1,0:T(8,128)(2,1)S(1)}, u32[]{:S(2)}, u32[]{:S(2)}) collective-permute-start(bf16[48,1280]{1,0:T(8,128)(2,1)S(1)} %collective-permute-done.5.refs_6_.refs_12_), channel_id=1, source_target_pairs={{0,8},{8,0},{1,9},{9,1},{2,10},{10,2},{3,11},{11,3},{4,12},{12,4},... | collective-permute-start | bytes 368648 | tf_op jit(solution)/shard_map/ppermute | solution.py:412
  37.3 2.1 %copy-start.19 = (bf16[48,1280]{1,0:T(8,128)(2,1)}, bf16[48,1280]{1,0:T(8,128)(2,1)S(1)}, u32[]{:S(2)}) copy-start(bf16[48,1280]{1,0:T(8,128)(2,1)S(1)} %collective-permute-done.9.refs_11_.refs_17_) | copy-start | bytes 368644
  37.3 0.7 copy-start.15
  37.3 2.1 %copy-start.16 = (bf16[96,1280]{1,0:T(8,128)(2,1)}, bf16[96,1280]{1,0:T(8,128)(2,1)S(1)}, u32[]{:S(2)}) copy-start(bf16[96,1280]{1,0:T(8,128)(2,1)S(1)} %collective-permute-done.6.refs_8_.refs_14_) | copy-start | bytes 737284
  38.0 1.4 %copy-start.17 = (bf16[96,1280]{1,0:T(8,128)(2,1)}, bf16[96,1280]{1,0:T(8,128)(2,1)S(1)}, u32[]{:S(2)}) copy-start(bf16[96,1280]{1,0:T(8,128)(2,1)S(1)} %collective-permute-done.8.refs_10_.refs_16_) | copy-start | bytes 737284
  46.9 6.7 %collective-permute-start.10 = (f32[24,128]{1,0:T(8,128)}, f32[24,128]{1,0:T(8,128)S(1)}, u32[]{:S(2)}, u32[]{:S(2)}) collective-permute-start(f32[24,128]{1,0:T(8,128)} %get-tuple-element.26), channel_id=1, source_target_pairs={{0,8},{8,0},{1,9},{9,1},{2,10},{10,2},{3,11},{11,3},{4,12},{12,4},... | collective-permute-start | bytes 36872 | tf_op jit(solution)/shard_map/ppermute | solution.py:412
  49.1 20.8 %all-to-all-start.1 = ((f32[16,48,128]{2,1,0:T(8,128)}), f32[16,48,128]{2,1,0:T(8,128)}, u32[]{:S(2)}, u32[]{:S(2)}) async-start(f32[16,48,128]{2,1,0:T(8,128)} %get-tuple-element.25), calls=%async_computation.1 | async-start | bytes 786432 | tf_op jit(solution)/shard_map/all_to_all | solution.py:458
  54.3 10.0 %copy-start.8 = (f32[24,128]{1,0:T(8,128)}, f32[24,128]{1,0:T(8,128)S(1)}, u32[]{:S(2)}) copy-start(f32[24,128]{1,0:T(8,128)S(1)} %pad_maximum_fusion.refs_2_) | copy-start | bytes 36868
  54.3 8.7 %collective-permute-start.14 = (f32[24,128]{1,0:T(8,128)S(1)}, f32[24,128]{1,0:T(8,128)S(1)}, u32[]{:S(2)}, u32[]{:S(2)}) collective-permute-start(f32[24,128]{1,0:T(8,128)S(1)} %pad_maximum_fusion.refs_2_), channel_id=1, source_target_pairs={{1,0},{2,1},{3,2},{4,3},{5,4},{6,5},{7,6},{0,7},{8,9},{9,10},{10,1... | collective-permute-start | bytes 36872 | tf_op jit(solution)/shard_map/ppermute | solution.py:416
  55.8 7.3 %collective-permute-start.13 = (f32[24,128]{1,0:T(8,128)S(1)}, f32[24,128]{1,0:T(8,128)S(1)}, u32[]{:S(2)}, u32[]{:S(2)}) collective-permute-start(f32[24,128]{1,0:T(8,128)S(1)} %pad_maximum_fusion.refs_2_), channel_id=1, source_target_pairs={{2,0},{3,1},{4,2},{5,3},{6,4},{7,5},{0,6},{1,7},{8,10},{9,11},{10,... | collective-permute-start | bytes 36872 | tf_op jit(solution)/shard_map/ppermute | solution.py:416
  58.8 5.6 %collective-permute-start.12 = (f32[24,128]{1,0:T(8,128)S(1)}, f32[24,128]{1,0:T(8,128)S(1)}, u32[]{:S(2)}, u32[]{:S(2)}) collective-permute-start(f32[24,128]{1,0:T(8,128)S(1)} %pad_maximum_fusion.refs_2_), channel_id=1, source_target_pairs={{3,0},{4,1},{5,2},{6,3},{7,4},{0,5},{1,6},{2,7},{8,11},{9,12},{10,... | collective-permute-start | bytes 36872 | tf_op jit(solution)/shard_map/ppermute | solution.py:416
  62.6 6.7 %collective-permute-start.11 = (f32[24,128]{1,0:T(8,128)S(1)}, f32[24,128]{1,0:T(8,128)S(1)}, u32[]{:S(2)}, u32[]{:S(2)}) collective-permute-start(f32[24,128]{1,0:T(8,128)S(1)} %pad_maximum_fusion.refs_2_), channel_id=1, source_target_pairs={{4,0},{5,1},{6,2},{7,3},{0,4},{1,5},{2,6},{3,7},{8,12},{9,13},{10,... | collective-permute-start | bytes 36872 | tf_op jit(solution)/shard_map/ppermute | solution.py:416
  64.4 4.9 %copy-start.9 = (f32[24,128]{1,0:T(8,128)}, f32[24,128]{1,0:T(8,128)S(1)}, u32[]{:S(2)}) copy-start(f32[24,128]{1,0:T(8,128)S(1)} %pad_maximum_fusion.1.refs_4_) | copy-start | bytes 36868
  64.4 5.5 %collective-permute-start.15 = (f32[24,128]{1,0:T(8,128)S(1)}, f32[24,128]{1,0:T(8,128)}, u32[]{:S(2)}, u32[]{:S(2)}) collective-permute-start(f32[24,128]{1,0:T(8,128)S(1)} %pad_maximum_fusion.1.refs_4_), channel_id=1, source_target_pairs={{0,8},{8,0},{1,9},{9,1},{2,10},{10,2},{3,11},{11,3},{4,12},{12,4},... | collective-permute-start | bytes 36872 | tf_op jit(solution)/shard_map/ppermute | solution.py:412
  69.3 0.6 copy-start.20
  79.4 7.3 %collective-permute-start.17 = (bf16[384,1408]{1,0:T(8,128)(2,1)}, bf16[384,1408]{1,0:T(8,128)(2,1)S(1)}, u32[]{:S(2)}, u32[]{:S(2)}) collective-permute-start(bf16[384,1408]{1,0:T(8,128)(2,1)} %get-tuple-element.32), channel_id=1, source_target_pairs={{0,8},{8,0},{1,9},{9,1},{2,10},{10,2},{3,11},{11,3},{4,12},{12,4},... | collective-permute-start | bytes 3244040 | tf_op jit(solution)/shard_map/ppermute | solution.py:412
  79.9 39.2 %all-to-all-start.2 = ((bf16[16,496,128]{2,1,0:T(8,128)(2,1)}), bf16[16,496,128]{2,1,0:T(8,128)(2,1)S(1)}, u32[]{:S(2)}, u32[]{:S(2)}) async-start(bf16[16,496,128]{2,1,0:T(8,128)(2,1)} %get-tuple-element.40), calls=%async_computation.2 | async-start | bytes 4063232 | tf_op jit(solution)/shard_map/all_to_all | solution.py:486
  86.7 1.0 copy-start.4
  87.8 19.4 %copy-start.11 = (f32[8,128]{1,0:T(8,128)S(1)}, f32[8,128]{1,0:T(8,128)}, u32[]{:S(2)}) copy-start(f32[8,128]{1,0:T(8,128)} %get-tuple-element.29) | copy-start | bytes 12292
  87.8 19.5 %copy-start.12 = (f32[8,128]{1,0:T(8,128)S(1)}, f32[8,128]{1,0:T(8,128)}, u32[]{:S(2)}) copy-start(f32[8,128]{1,0:T(8,128)} %get-tuple-element.28) | copy-start | bytes 12292
  93.3 9.9 %collective-permute-start.19 = (bf16[96,1408]{1,0:T(8,128)(2,1)}, bf16[96,1408]{1,0:T(8,128)(2,1)S(1)}, u32[]{:S(2)}, u32[]{:S(2)}) collective-permute-start(bf16[96,1408]{1,0:T(8,128)(2,1)} %get-tuple-element.36), channel_id=1, source_target_pairs={{0,1},{1,2},{2,3},{3,4},{4,5},{5,6},{6,7},{7,0},{9,8},{10,9},{11,1... | collective-permute-start | bytes 811016 | tf_op jit(solution)/shard_map/ppermute | solution.py:420
  94.4 8.8 %collective-permute-start.20 = (bf16[48,1408]{1,0:T(8,128)(2,1)}, bf16[48,1408]{1,0:T(8,128)(2,1)S(1)}, u32[]{:S(2)}, u32[]{:S(2)}) collective-permute-start(bf16[48,1408]{1,0:T(8,128)(2,1)} %get-tuple-element.37), channel_id=1, source_target_pairs={{0,2},{1,3},{2,4},{3,5},{4,6},{5,7},{6,0},{7,1},{10,8},{11,9},{12,... | collective-permute-start | bytes 405512 | tf_op jit(solution)/shard_map/ppermute | solution.py:420
  97.9 10.7 %collective-permute-start.18 = (bf16[96,1408]{1,0:T(8,128)(2,1)}, bf16[96,1408]{1,0:T(8,128)(2,1)S(1)}, u32[]{:S(2)}, u32[]{:S(2)}) collective-permute-start(bf16[96,1408]{1,0:T(8,128)(2,1)} %get-tuple-element.34), channel_id=1, source_target_pairs={{0,1},{1,2},{2,3},{3,4},{4,5},{5,6},{6,7},{7,0},{9,8},{10,9},{11,1... | collective-permute-start | bytes 811016 | tf_op jit(solution)/shard_map/ppermute | solution.py:420
  103.2 1.0 copy-start
  104.9 9.3 %collective-permute-start.21 = (bf16[96,1408]{1,0:T(8,128)(2,1)S(1)}, bf16[96,1408]{1,0:T(8,128)(2,1)S(1)}, u32[]{:S(2)}, u32[]{:S(2)}) collective-permute-start(bf16[96,1408]{1,0:T(8,128)(2,1)S(1)} %shard_map.86), channel_id=1, source_target_pairs={{0,2},{1,3},{2,4},{3,5},{4,6},{5,7},{6,0},{7,1},{10,8},{11,9},{12,... | collective-permute-start | bytes 811016 | tf_op jit(solution)/shard_map/ppermute | solution.py:420
  107.2 1.2 collective-permute-start.16
  107.3 13.6 %copy-start.3 = (f32[384]{0:T(512)}, f32[384]{0:T(512)S(1)}, u32[]{:S(2)}) copy-start(f32[384]{0:T(512)S(1)} %dynamic-slice_bitcast_fusion.refs_0_) | copy-start | bytes 4612
  108.5 12.4 %copy-start.2 = (f32[1536]{0:T(1024)}, f32[1536]{0:T(1024)S(1)}, u32[]{:S(2)}) copy-start(f32[1536]{0:T(1024)S(1)} %select_n.71.refs_1_) | copy-start | bytes 18436
  114.2 1.0 copy-start.1
  115.2 5.0 %collective-permute-start.22 = (f32[48,1408]{1,0:T(8,128)S(1)}, f32[48,1408]{1,0:T(8,128)S(1)}, u32[]{:S(2)}, u32[]{:S(2)}) collective-permute-start(f32[48,1408]{1,0:T(8,128)S(1)} %get-tuple-element.39.unread), channel_id=1, source_target_pairs={{0,8},{8,0},{1,9},{9,1},{2,10},{10,2},{3,11},{11,3},{4,12},{12,4},... | collective-permute-start | bytes 811016 | tf_op jit(solution)/shard_map/ppermute | solution.py:412

commit v5 on v4

--- a/solution.py
+++ b/solution.py
@@ -8,12 +8,13 @@
 from jax.sharding import Mesh, PartitionSpec as P
 
 NY, NX, NC = 4, 4, 2
-XY = ("y", "x")
+XY = ("x", "y")
 CZ = ("c", "z")
 SWAP = [(0, 1), (1, 0)]
 LANES = 128
 VMEM_BYTES = 64 * 1024 * 1024
 MESSAGE = 48
+SPARE = 1048576
 F32 = jnp.float32
 BF16 = jnp.bfloat16
 
@@ -169,6 +170,13 @@
 
 def tall(rows):
     return jnp.concatenate(rows + [rows[-1]] * (8 - len(rows)), axis=0).T
+
+
+def spread_kernel(ins, held, outs, sender):
+    for p in range(outs[0].shape[0]):
+        if p == 0:
+            ins[0].get()
+        sender.send(ins[0].ref, outs[0].at[p])
 
 
 def logits_kernel(nz, ins, held, outs, sender, column, stat):
@@ -419,7 +427,7 @@
         pairs = [(i, (i + k) % nz) for i in range(nz)]
         return lax.ppermute(x, CZ, pairs + [(nz + (i + k) % nz, nz + i) for i in range(nz)])
 
-    spread = jnp.broadcast_to(text_embed[None], (peers, part, embed))
+    spread = call(spread_kernel, sds((peers, part, embed), BF16), text_embed, flops=1 << 34, held=(sds((8, LANES), BF16),))
     txt = lax.all_to_all(spread, XY, 0, 0).reshape(cols, embed)
     partner = swap(image_embed)
     chip = jnp.concatenate([image_embed, partner])
@@ -430,7 +438,8 @@
     rem = pair_col % (cols * NC)
     block = rem // part
     ours = pair_col // (cols * NC) == z
-    place = (block // NC * part + rem % part).astype(F32)
+    chip = block // NC
+    place = ((chip % NX * NY + chip // NX) * part + rem % part).astype(F32)
     mine = jnp.where(ours & (block % NC == c), place, -1.0)
     theirs = swap(jnp.where(ours & (block % NC == 1 - c), place, -1.0))
     pairs = jnp.where(c == 0, jnp.concatenate([mine, theirs]), jnp.concatenate([theirs, mine]))
@@ -452,6 +461,7 @@
         joined=3,
         later=(2, 3),
         held=(None, None, message),
+        spare=SPARE,
         sends=1 + cols // 256 + peers,
         scratch=[vmem((rows, 8), F32), vmem((rows, LANES), F32)],
     )
@@ -480,6 +490,7 @@
         cuts={7: (0, part), 8: (1, 256)},
         joined=9,
         later=(8, 9),
+        spare=SPARE,
         scratch=[vmem((rows, 8), F32), vmem((rows, cols), BF16), vmem((cols, rows), BF16)],
     )
     received = swap(send)
@@ -494,11 +505,11 @@
         received,
         flops=work // 2,
         cuts={2: (1, 256), 3: (1, 256)},
-        spare=6 << 20,
+        spare=VMEM_BYTES // 2,
     )
     two = call(forward_kernel, chip_rows, two, onward(three, 1), onward(four, 2), spare=VMEM_BYTES // 2)
     row_loss = lax.dynamic_slice(row_loss, (c * (count // NC), 0), (count // NC, LANES)).reshape(-1)
-    col_loss = col_loss[:count].reshape(peers, 1, part)
+    col_loss = jnp.swapaxes(col_loss[:count].reshape(NX, NY, part), 0, 1).reshape(peers, 1, part)
     other = swap(col_loss)
     col_loss = jnp.where(
         c == 0, jnp.concatenate([col_loss, other], 1), jnp.concatenate([other, col_loss], 1)

time: 121 us -> 116 us (0.959)
  local copies, waits for them, and re-layouts: 8.14 us -> 4.1 us
  waiting for transfers between devices: 27.4 us -> 25.8 us
    broadcast_in_dim x1 -> x0, local copies, waits for them, and re-layouts: 2.34 us -> none  [local(): spread = jnp.broadcast_to(text_embed[None], (peers, part, embed))]
    unnamed x43 -> x45, local copies, waits for them, and re-layouts: 5.02 us -> 3.3 us
    all_to_all x1, waiting for transfers between devices: 1.39 us -> 0.01 us  [local(): txt = lax.all_to_all(spread, XY, 0, 0).reshape(cols, embed)]
    pallas_call x4 -> x5, Pallas kernels: 23.1 us -> 24.2 us  [call(): pl.pallas_call(kernel, out_shape=out_shape, in_specs=[scalars if i in sme...]
  transfers between devices with their start and end apart: 26 -> 26, of which waited for: 12 -> 10; matrix products, arithmetic and copies ran while one was open for 1% -> 1% of each run, Pallas kernels for 6% -> 5%
where the time goes in v5:
time: 116 us
  starting transfers between devices  57.6 us (50%)
  Pallas kernels  26 us (22%)
  waiting for transfers between devices  25.8 us (22%)
  local copies, waits for them, and re-layouts  4.1 us (4%)
  between operations  1.64 us (1%)
    pallas_call x5, Pallas kernels, call(): pl.pallas_call(kernel, out_shape=out_shape, in_specs=[scalars if i in sme...  24.2 us
    ppermute x11, starting transfers between devices, swap(): return lax.ppermute(x, 'c', SWAP)  15.3 us
    ppermute x8, starting transfers between devices, ahead(): lax.ppermute(x, CZ, pairs + [(nz + i, nz + (i + k) % nz) for i in range(n...  15.3 us
    ppermute x8, waiting for transfers between devices, ahead(): lax.ppermute(x, CZ, pairs + [(nz + i, nz + (i + k) % nz) for i in range(n...  10.5 us
    ppermute x4, waiting for transfers between devices, onward(): lax.ppermute(x, CZ, pairs + [(nz + (i + k) % nz, nz + i) for i in range(n...  10.1 us
    all_to_all x1, starting transfers between devices, local(): txt = lax.all_to_all(spread, XY, 0, 0).reshape(cols, embed)  7.77 us
    ppermute x4, starting transfers between devices, onward(): lax.ppermute(x, CZ, pairs + [(nz + (i + k) % nz, nz + i) for i in range(n...  7.41 us
    all_to_all x1, starting transfers between devices, local(): text_got = lax.all_to_all(text_term, XY, 0, 0)  7.07 us
  transfers between devices with their start and end apart: 26, of which 10 were waited for; matrix products, arithmetic and copies ran while one was open for 1% of the time, Pallas kernels for 5%

profile of v5, /device:TPU:1, one launch (start us, length us, event | category | flops | bytes accessed | tf_op | source)
XLA Modules:
  0.0 115.9 jit_solution(13452416663654915233)
XLA Ops:
  0.6 2.4 %shard_map.83 = bf16[16,48,1280]{2,1,0:T(8,128)(2,1)} custom-call(bf16[48,1280]{1,0:T(8,128)(2,1)} %refs_0_.1), custom_call_target="tpu_custom_call" | custom-call | flops 17179869184 | bytes 122880 | tf_op jit(solution)/shard_map/pallas_call | solution.py:111
  3.0 0.0 copy-start.5
  3.0 0.0 copy-start.10
  3.0 7.8 %all-to-all-start = ((bf16[16,48,1280]{2,1,0:T(8,128)(2,1)}), bf16[16,48,1280]{2,1,0:T(8,128)(2,1)}, u32[]{:S(2)}, u32[]{:S(2)}) async-start(bf16[16,48,1280]{2,1,0:T(8,128)(2,1)} %shard_map.83), calls=%async_computation | async-start | bytes 3932160 | tf_op jit(solution)/shard_map/all_to_all | solution.py:431
  10.8 1.0 collective-permute-start.1
  11.9 1.0 collective-permute-done.1.refs_12_.refs_18_
  12.8 3.1 %collective-permute-start.3 = (bf16[96,1280]{1,0:T(8,128)(2,1)S(1)}, bf16[96,1280]{1,0:T(8,128)(2,1)S(1)}, u32[]{:S(2)}, u32[]{:S(2)}) collective-permute-start(bf16[96,1280]{1,0:T(8,128)(2,1)S(1)} %constant_dynamic-update-slice_fusion), channel_id=1, source_target_pairs={{2,0},{3,1},{4,2},{5,3},{6,4},{7,5},{0,6},{1,7},{8,10},{9,11},{10,... | collective-permute-start | bytes 737288 | tf_op jit(solution)/shard_map/ppermute | solution.py:424
  15.9 1.6 %collective-permute-start.2 = (bf16[96,1280]{1,0:T(8,128)(2,1)S(1)}, bf16[96,1280]{1,0:T(8,128)(2,1)S(1)}, u32[]{:S(2)}, u32[]{:S(2)}) collective-permute-start(bf16[96,1280]{1,0:T(8,128)(2,1)S(1)} %constant_dynamic-update-slice_fusion), channel_id=1, source_target_pairs={{1,0},{2,1},{3,2},{4,3},{5,4},{6,5},{7,6},{0,7},{8,9},{9,10},{10,1... | collective-permute-start | bytes 737288 | tf_op jit(solution)/shard_map/ppermute | solution.py:424
  17.5 6.0 %collective-permute-done.3.refs_4_.refs_10_ = bf16[96,1280]{1,0:T(8,128)(2,1)S(1)} collective-permute-done((bf16[96,1280]{1,0:T(8,128)(2,1)S(1)}, bf16[96,1280]{1,0:T(8,128)(2,1)S(1)}, u32[]{:S(2)}, u32[]{:S(2)}) %collective-permute-start.3) | collective-permute-done | bytes 245792 | tf_op jit(solution)/shard_map/ppermute | solution.py:424
  23.5 2.8 %collective-permute-start.4 = (bf16[96,1280]{1,0:T(8,128)(2,1)S(1)}, bf16[96,1280]{1,0:T(8,128)(2,1)S(1)}, u32[]{:S(2)}, u32[]{:S(2)}) collective-permute-start(bf16[96,1280]{1,0:T(8,128)(2,1)S(1)} %collective-permute-done.3.refs_4_.refs_10_), channel_id=1, source_target_pairs={{1,0},{2,1},{3,2},{4,3},{5,4},{6,5},{7,6},{0,7},{8,9},{9,10},{10,1... | collective-permute-start | bytes 737288 | tf_op jit(solution)/shard_map/ppermute | solution.py:424
  26.4 0.1 collective-permute-start.5
  26.5 4.3 %collective-permute-start.7 = (bf16[96,1280]{1,0:T(8,128)(2,1)S(1)}, bf16[96,1280]{1,0:T(8,128)(2,1)S(1)}, u32[]{:S(2)}, u32[]{:S(2)}) collective-permute-start(bf16[96,1280]{1,0:T(8,128)(2,1)S(1)} %collective-permute-done.3.refs_4_.refs_10_), channel_id=1, source_target_pairs={{0,8},{8,0},{1,9},{9,1},{2,10},{10,2},{3,11},{11,3},{4,12},{12,4},... | collective-permute-start | bytes 737288 | tf_op jit(solution)/shard_map/ppermute | solution.py:420
  30.8 0.0 collective-permute-done.2.refs_3_.refs_9_
  30.8 0.1 collective-permute-start.6
  30.9 0.0 collective-permute-done.4.refs_5_.refs_11_
  30.9 1.6 %collective-permute-start.8 = (bf16[96,1280]{1,0:T(8,128)(2,1)S(1)}, bf16[96,1280]{1,0:T(8,128)(2,1)S(1)}, u32[]{:S(2)}, u32[]{:S(2)}) collective-permute-start(bf16[96,1280]{1,0:T(8,128)(2,1)S(1)} %collective-permute-done.4.refs_5_.refs_11_), channel_id=1, source_target_pairs={{0,8},{8,0},{1,9},{9,1},{2,10},{10,2},{3,11},{11,3},{4,12},{12,4},... | collective-permute-start | bytes 737288 | tf_op jit(solution)/shard_map/ppermute | solution.py:420
  32.5 0.1 collective-permute-start
  33.2 1.2 %collective-permute-done.5.refs_6_.refs_12_ = bf16[48,1280]{1,0:T(8,128)(2,1)S(1)} collective-permute-done((bf16[48,1280]{1,0:T(8,128)(2,1)S(1)}, bf16[48,1280]{1,0:T(8,128)(2,1)S(1)}, u32[]{:S(2)}, u32[]{:S(2)}) %collective-permute-start.5) | collective-permute-done | bytes 122912 | tf_op jit(solution)/shard_map/ppermute | solution.py:424
  34.5 1.3 %collective-permute-start.9 = (bf16[48,1280]{1,0:T(8,128)(2,1)S(1)}, bf16[48,1280]{1,0:T(8,128)(2,1)S(1)}, u32[]{:S(2)}, u32[]{:S(2)}) collective-permute-start(bf16[48,1280]{1,0:T(8,128)(2,1)S(1)} %collective-permute-done.5.refs_6_.refs_12_), channel_id=1, source_target_pairs={{0,8},{8,0},{1,9},{9,1},{2,10},{10,2},{3,11},{11,3},{4,12},{12,4},... | collective-permute-start | bytes 368648 | tf_op jit(solution)/shard_map/ppermute | solution.py:420
  35.8 0.0 collective-permute-done
  35.8 0.6 pad_bitcast_fusion.refs_1_.refs_6_
  36.4 0.4 collective-permute-done.9.refs_11_.refs_17_
  36.7 0.0 collective-permute-done.7.refs_9_.refs_15_
  36.8 0.7 copy-done.15
  37.5 0.1 copy-done.16
  37.6 0.0 copy-done.19
  37.6 0.6 copy-done.17
  38.2 7.4 %shard_map.84 = (f32[768,768]{1,0:T(8,128)}, f32[24,128]{1,0:T(8,128)}, f32[16,48,128]{2,1,0:T(8,128)}) custom-call(f32[1]{0:T(128)} %bitcast.refs_0_, f32[8,128]{1,0:T(8,128)} %pad_bitcast_fusion.refs_1_.refs_6_, bf16[768,1280]{1,0:T(8,128)(2,1)} %bitcast.2.refs_2_.refs_8_, bf16[96,1280]{1,0:T(8,128)(2,1)} %copy-done.13, bf16[96,1280]{1,0:T(8,128)(2,1)} %copy-done.7, ...), custom_call_target="tpu_custom_call" | custom-call | flops 1509949440 | bytes 3936260 | tf_op jit(solution)/shard_map/pallas_call | solution.py:111
  45.6 2.5 %collective-permute-start.10 = (f32[24,128]{1,0:T(8,128)}, f32[24,128]{1,0:T(8,128)S(1)}, u32[]{:S(2)}, u32[]{:S(2)}) collective-permute-start(f32[24,128]{1,0:T(8,128)} %get-tuple-element.26), channel_id=1, source_target_pairs={{0,8},{8,0},{1,9},{9,1},{2,10},{10,2},{3,11},{11,3},{4,12},{12,4},... | collective-permute-start | bytes 36872 | tf_op jit(solution)/shard_map/ppermute | solution.py:420
  48.1 4.8 %all-to-all-start.1 = ((f32[16,48,128]{2,1,0:T(8,128)}), f32[16,48,128]{2,1,0:T(8,128)S(1)}, u32[]{:S(2)}, u32[]{:S(2)}) async-start(f32[16,48,128]{2,1,0:T(8,128)} %get-tuple-element.25), calls=%async_computation.1 | async-start | bytes 786432 | tf_op jit(solution)/shard_map/all_to_all | solution.py:468
  53.0 0.7 log_add_fusion.1
  53.7 0.8 collective-permute-start.14
  54.5 2.6 %collective-permute-start.13 = (f32[24,128]{1,0:T(8,128)S(1)}, f32[24,128]{1,0:T(8,128)S(1)}, u32[]{:S(2)}, u32[]{:S(2)}) collective-permute-start(f32[24,128]{1,0:T(8,128)S(1)} %pad_maximum_fusion.refs_2_), channel_id=1, source_target_pairs={{2,0},{3,1},{4,2},{5,3},{6,4},{7,5},{0,6},{1,7},{8,10},{9,11},{10,... | collective-permute-start | bytes 36872 | tf_op jit(solution)/shard_map/ppermute | solution.py:424
  57.2 3.7 %collective-permute-start.12 = (f32[24,128]{1,0:T(8,128)S(1)}, f32[24,128]{1,0:T(8,128)S(1)}, u32[]{:S(2)}, u32[]{:S(2)}) collective-permute-start(f32[24,128]{1,0:T(8,128)S(1)} %pad_maximum_fusion.refs_2_), channel_id=1, source_target_pairs={{3,0},{4,1},{5,2},{6,3},{7,4},{0,5},{1,6},{2,7},{8,11},{9,12},{10,... | collective-permute-start | bytes 36872 | tf_op jit(solution)/shard_map/ppermute | solution.py:424
  60.9 0.5 collective-permute-start.11
  61.4 1.6 %collective-permute-done.12 = f32[24,128]{1,0:T(8,128)S(1)} collective-permute-done((f32[24,128]{1,0:T(8,128)S(1)}, f32[24,128]{1,0:T(8,128)S(1)}, u32[]{:S(2)}, u32[]{:S(2)}) %collective-permute-start.12) | collective-permute-done | bytes 12320 | tf_op jit(solution)/shard_map/ppermute | solution.py:424
  63.1 2.5 %collective-permute-start.15 = (f32[24,128]{1,0:T(8,128)S(1)}, f32[24,128]{1,0:T(8,128)S(1)}, u32[]{:S(2)}, u32[]{:S(2)}) collective-permute-start(f32[24,128]{1,0:T(8,128)S(1)} %pad_maximum_fusion.1.refs_4_), channel_id=1, source_target_pairs={{0,8},{8,0},{1,9},{9,1},{2,10},{10,2},{3,11},{11,3},{4,12},{12,4},... | collective-permute-start | bytes 36872 | tf_op jit(solution)/shard_map/ppermute | solution.py:420
  65.6 1.7 %collective-permute-done.11.refs_3_ = f32[24,128]{1,0:T(8,128)S(1)} collective-permute-done((f32[24,128]{1,0:T(8,128)S(1)}, f32[24,128]{1,0:T(8,128)S(1)}, u32[]{:S(2)}, u32[]{:S(2)}) %collective-permute-start.11) | collective-permute-done | bytes 12320 | tf_op jit(solution)/shard_map/ppermute | solution.py:424
  67.3 0.6 copy-done.20
  67.9 0.0 copy-done.21
  67.9 0.2 copy-done.4
  68.1 9.5 %shard_map.85 = (bf16[16,496,128]{2,1,0:T(8,128)(2,1)}, bf16[384,768]{1,0:T(8,128)(2,1)}, f32[8,128]{1,0:T(8,128)}, f32[8,128]{1,0:T(8,128)}, f32[8,128]{1,0:T(8,128)}, /*index=5*/bf16[384,1408]{1,0:T(8,128)(2,1)}) custom-call(f32[1]{0:T(128)} %bitcast.refs_0_, f32[16,48,128]{2,1,0:T(8,128)} %copy-done.4, f32[24,128]{1,0:T(8,128)} %copy-done.8, ...), custom_call_target="tpu_custom_call" | custom-call | flops 3019898880 | bytes 6737924 | tf_op jit(solution)/shard_map/pallas_call | solution.py:111
  77.6 0.9 collective-permute-start.17
  78.5 7.1 %all-to-all-start.2 = ((bf16[16,496,128]{2,1,0:T(8,128)(2,1)}), bf16[16,496,128]{2,1,0:T(8,128)(2,1)S(1)}, u32[]{:S(2)}, u32[]{:S(2)}) async-start(bf16[16,496,128]{2,1,0:T(8,128)(2,1)} %get-tuple-element.40), calls=%async_computation.2 | async-start | bytes 4063232 | tf_op jit(solution)/shard_map/all_to_all | solution.py:497
  85.6 1.1 copy-done
  86.7 4.3 %shard_map.86 = (bf16[96,1408]{1,0:T(8,128)(2,1)}, f32[96,1408]{1,0:T(8,128)S(1)}, bf16[96,1408]{1,0:T(8,128)(2,1)S(1)}, bf16[48,1408]{1,0:T(8,128)(2,1)S(1)}, f32[48,1408]{1,0:T(8,128)S(1)}) custom-call(f32[8,128]{1,0:T(8,128)S(1)} %copy-done.3, bf16[384,768]{1,0:T(8,128)(2,1)S(1)} %copy-done, bf16[768,1280]{1,0:T(8,128)(2,1)} %bitcast.2.refs_2_.refs_8_, ...), custom_call_target="tpu_custom_call" | custom-call | flops 754974720 | bytes 3641344 | tf_op jit(solution)/shard_map/pallas_call | solution.py:111
  91.0 0.8 collective-permute-start.19
  91.8 3.8 %collective-permute-start.20 = (bf16[48,1408]{1,0:T(8,128)(2,1)S(1)}, bf16[48,1408]{1,0:T(8,128)(2,1)S(1)}, u32[]{:S(2)}, u32[]{:S(2)}) collective-permute-start(bf16[48,1408]{1,0:T(8,128)(2,1)S(1)} %get-tuple-element.37), channel_id=1, source_target_pairs={{0,2},{1,3},{2,4},{3,5},{4,6},{5,7},{6,0},{7,1},{10,8},{11,9},{12,... | collective-permute-start | bytes 405512 | tf_op jit(solution)/shard_map/ppermute | solution.py:428
  95.6 0.7 collective-permute-start.18
  96.3 4.6 %collective-permute-done.20.refs_2_ = bf16[48,1408]{1,0:T(8,128)(2,1)S(1)} collective-permute-done((bf16[48,1408]{1,0:T(8,128)(2,1)S(1)}, bf16[48,1408]{1,0:T(8,128)(2,1)S(1)}, u32[]{:S(2)}, u32[]{:S(2)}) %collective-permute-start.20) | collective-permute-done | bytes 135200 | tf_op jit(solution)/shard_map/ppermute | solution.py:428
  100.9 0.6 shard_map.87
  101.4 2.2 %collective-permute-start.21 = (bf16[96,1408]{1,0:T(8,128)(2,1)S(1)}, bf16[96,1408]{1,0:T(8,128)(2,1)S(1)}, u32[]{:S(2)}, u32[]{:S(2)}) collective-permute-start(bf16[96,1408]{1,0:T(8,128)(2,1)S(1)} %shard_map.87), channel_id=1, source_target_pairs={{0,2},{1,3},{2,4},{3,5},{4,6},{5,7},{6,0},{7,1},{10,8},{11,9},{12,... | collective-permute-start | bytes 811016 | tf_op jit(solution)/shard_map/ppermute | solution.py:428
  103.6 0.1 reshape.33
  103.7 0.1 collective-permute-start.16
  103.8 0.0 copy-start.2
  103.8 1.1 collective-permute-done.16
  105.0 0.1 select_n.80.refs_1_
  105.1 0.0 collective-permute-done.18.one
  105.1 5.5 %collective-permute-done.21.two = bf16[96,1408]{1,0:T(8,128)(2,1)S(1)} collective-permute-done((bf16[96,1408]{1,0:T(8,128)(2,1)S(1)}, bf16[96,1408]{1,0:T(8,128)(2,1)S(1)}, u32[]{:S(2)}, u32[]{:S(2)}) %collective-permute-start.21) | collective-permute-done | bytes 270368 | tf_op jit(solution)/shard_map/ppermute | solution.py:428
  110.6 0.1 shard_map.88
  110.7 0.8 collective-permute-start.22
  111.5 2.7 %all-to-all-done.2.got = bf16[16,496,128]{2,1,0:T(8,128)(2,1)S(1)} async-done(((bf16[16,496,128]{2,1,0:T(8,128)(2,1)}), bf16[16,496,128]{2,1,0:T(8,128)(2,1)S(1)}, u32[]{:S(2)}, u32[]{:S(2)}) %all-to-all-start.2) | async-done | bytes 2031648 | tf_op jit(solution)/shard_map/all_to_all | solution.py:497
  114.2 1.0 shard_map.89
  115.2 0.7 shard_map.90
  (57 shorter events, 0.2 us)
Async XLA Ops:
  3.0 7.8 %copy-start.5 = (bf16[48,1280]{1,0:T(8,128)(2,1)S(1)}, bf16[48,1280]{1,0:T(8,128)(2,1)}, u32[]{:S(2)}) copy-start(bf16[48,1280]{1,0:T(8,128)(2,1)} %refs_13_.1) | copy-start | bytes 368644
  3.0 23.3 %copy-start.10 = (s32[384]{0:T(512)S(1)}, s32[384]{0:T(512)}, u32[]{:S(2)}) copy-start(s32[384]{0:T(512)} %param.6) | copy-start | bytes 4612
  3.0 34.5 %all-to-all-start = ((bf16[16,48,1280]{2,1,0:T(8,128)(2,1)}), bf16[16,48,1280]{2,1,0:T(8,128)(2,1)}, u32[]{:S(2)}, u32[]{:S(2)}) async-start(bf16[16,48,1280]{2,1,0:T(8,128)(2,1)} %shard_map.83), calls=%async_computation | async-start | bytes 3932160 | tf_op jit(solution)/shard_map/all_to_all | solution.py:431
  10.8 2.0 %collective-permute-start.1 = (bf16[48,1280]{1,0:T(8,128)(2,1)S(1)}, bf16[48,1280]{1,0:T(8,128)(2,1)S(1)}, u32[]{:S(2)}, u32[]{:S(2)}) collective-permute-start(bf16[48,1280]{1,0:T(8,128)(2,1)S(1)} %copy-done.5), channel_id=1, source_target_pairs={{0,8},{8,0},{1,9},{9,1},{2,10},{10,2},{3,11},{11,3},{4,12},{12,4},... | collective-permute-start | bytes 368648 | tf_op jit(solution)/shard_map/ppermute | solution.py:420
  12.8 25.3 %copy-start.6 = (bf16[48,1280]{1,0:T(8,128)(2,1)}, bf16[48,1280]{1,0:T(8,128)(2,1)S(1)}, u32[]{:S(2)}) copy-start(bf16[48,1280]{1,0:T(8,128)(2,1)S(1)} %collective-permute-done.1.refs_12_.refs_18_) | copy-start | bytes 368644
  12.8 10.7 %collective-permute-start.3 = (bf16[96,1280]{1,0:T(8,128)(2,1)S(1)}, bf16[96,1280]{1,0:T(8,128)(2,1)S(1)}, u32[]{:S(2)}, u32[]{:S(2)}) collective-permute-start(bf16[96,1280]{1,0:T(8,128)(2,1)S(1)} %constant_dynamic-update-slice_fusion), channel_id=1, source_target_pairs={{2,0},{3,1},{4,2},{5,3},{6,4},{7,5},{0,6},{1,7},{8,10},{9,11},{10,... | collective-permute-start | bytes 737288 | tf_op jit(solution)/shard_map/ppermute | solution.py:424
  15.9 14.9 %collective-permute-start.2 = (bf16[96,1280]{1,0:T(8,128)(2,1)S(1)}, bf16[96,1280]{1,0:T(8,128)(2,1)S(1)}, u32[]{:S(2)}, u32[]{:S(2)}) collective-permute-start(bf16[96,1280]{1,0:T(8,128)(2,1)S(1)} %constant_dynamic-update-slice_fusion), channel_id=1, source_target_pairs={{1,0},{2,1},{3,2},{4,3},{5,4},{6,5},{7,6},{0,7},{8,9},{9,10},{10,1... | collective-permute-start | bytes 737288 | tf_op jit(solution)/shard_map/ppermute | solution.py:424
  23.5 14.6 %copy-start.7 = (bf16[96,1280]{1,0:T(8,128)(2,1)}, bf16[96,1280]{1,0:T(8,128)(2,1)S(1)}, u32[]{:S(2)}) copy-start(bf16[96,1280]{1,0:T(8,128)(2,1)S(1)} %collective-permute-done.3.refs_4_.refs_10_) | copy-start | bytes 737284
  23.5 7.4 %collective-permute-start.4 = (bf16[96,1280]{1,0:T(8,128)(2,1)S(1)}, bf16[96,1280]{1,0:T(8,128)(2,1)S(1)}, u32[]{:S(2)}, u32[]{:S(2)}) collective-permute-start(bf16[96,1280]{1,0:T(8,128)(2,1)S(1)} %collective-permute-done.3.refs_4_.refs_10_), channel_id=1, source_target_pairs={{1,0},{2,1},{3,2},{4,3},{5,4},{6,5},{7,6},{0,7},{8,9},{9,10},{10,1... | collective-permute-start | bytes 737288 | tf_op jit(solution)/shard_map/ppermute | solution.py:424
  26.4 8.1 %collective-permute-start.5 = (bf16[48,1280]{1,0:T(8,128)(2,1)S(1)}, bf16[48,1280]{1,0:T(8,128)(2,1)S(1)}, u32[]{:S(2)}, u32[]{:S(2)}) collective-permute-start(bf16[48,1280]{1,0:T(8,128)(2,1)S(1)} %slice.68), channel_id=1, source_target_pairs={{2,0},{3,1},{4,2},{5,3},{6,4},{7,5},{0,6},{1,7},{8,10},{9,11},{10,... | collective-permute-start | bytes 368648 | tf_op jit(solution)/shard_map/ppermute | solution.py:424
  26.5 10.3 %collective-permute-start.7 = (bf16[96,1280]{1,0:T(8,128)(2,1)S(1)}, bf16[96,1280]{1,0:T(8,128)(2,1)S(1)}, u32[]{:S(2)}, u32[]{:S(2)}) collective-permute-start(bf16[96,1280]{1,0:T(8,128)(2,1)S(1)} %collective-permute-done.3.refs_4_.refs_10_), channel_id=1, source_target_pairs={{0,8},{8,0},{1,9},{9,1},{2,10},{10,2},{3,11},{11,3},{4,12},{12,4},... | collective-permute-start | bytes 737288 | tf_op jit(solution)/shard_map/ppermute | solution.py:420
  30.8 7.4 %copy-start.13 = (bf16[96,1280]{1,0:T(8,128)(2,1)}, bf16[96,1280]{1,0:T(8,128)(2,1)S(1)}, u32[]{:S(2)}) copy-start(bf16[96,1280]{1,0:T(8,128)(2,1)S(1)} %collective-permute-done.2.refs_3_.refs_9_) | copy-start | bytes 737284
  30.8 6.0 %collective-permute-start.6 = (bf16[96,1280]{1,0:T(8,128)(2,1)S(1)}, bf16[96,1280]{1,0:T(8,128)(2,1)S(1)}, u32[]{:S(2)}, u32[]{:S(2)}) collective-permute-start(bf16[96,1280]{1,0:T(8,128)(2,1)S(1)} %collective-permute-done.2.refs_3_.refs_9_), channel_id=1, source_target_pairs={{0,8},{8,0},{1,9},{9,1},{2,10},{10,2},{3,11},{11,3},{4,12},{12,4},... | collective-permute-start | bytes 737288 | tf_op jit(solution)/shard_map/ppermute | solution.py:420
  30.9 7.3 %copy-start.14 = (bf16[96,1280]{1,0:T(8,128)(2,1)}, bf16[96,1280]{1,0:T(8,128)(2,1)S(1)}, u32[]{:S(2)}) copy-start(bf16[96,1280]{1,0:T(8,128)(2,1)S(1)} %collective-permute-done.4.refs_5_.refs_11_) | copy-start | bytes 737284
  30.9 5.9 %collective-permute-start.8 = (bf16[96,1280]{1,0:T(8,128)(2,1)S(1)}, bf16[96,1280]{1,0:T(8,128)(2,1)S(1)}, u32[]{:S(2)}, u32[]{:S(2)}) collective-permute-start(bf16[96,1280]{1,0:T(8,128)(2,1)S(1)} %collective-permute-done.4.refs_5_.refs_11_), channel_id=1, source_target_pairs={{0,8},{8,0},{1,9},{9,1},{2,10},{10,2},{3,11},{11,3},{4,12},{12,4},... | collective-permute-start | bytes 737288 | tf_op jit(solution)/shard_map/ppermute | solution.py:420
  32.5 3.3 %collective-permute-start = (f32[384]{0:T(512)S(1)}, f32[384]{0:T(512)S(1)}, u32[]{:S(2)}, u32[]{:S(2)}) collective-permute-start(f32[384]{0:T(512)S(1)} %and_select_fusion), channel_id=1, source_target_pairs={{0,8},{8,0},{1,9},{9,1},{2,10},{10,2},{3,11},{11,3},{4,12},{12,4},... | collective-permute-start | bytes 4616 | tf_op jit(solution)/shard_map/ppermute | solution.py:420
  34.5 3.1 %copy-start.18 = (bf16[48,1280]{1,0:T(8,128)(2,1)}, bf16[48,1280]{1,0:T(8,128)(2,1)S(1)}, u32[]{:S(2)}) copy-start(bf16[48,1280]{1,0:T(8,128)(2,1)S(1)} %collective-permute-done.5.refs_6_.refs_12_) | copy-start | bytes 368644
  34.5 2.3 %collective-permute-start.9 = (bf16[48,1280]{1,0:T(8,128)(2,1)S(1)}, bf16[48,1280]{1,0:T(8,128)(2,1)S(1)}, u32[]{:S(2)}, u32[]{:S(2)}) collective-permute-start(bf16[48,1280]{1,0:T(8,128)(2,1)S(1)} %collective-permute-done.5.refs_6_.refs_12_), channel_id=1, source_target_pairs={{0,8},{8,0},{1,9},{9,1},{2,10},{10,2},{3,11},{11,3},{4,12},{12,4},... | collective-permute-start | bytes 368648 | tf_op jit(solution)/shard_map/ppermute | solution.py:420
  36.7 0.8 copy-start.19
  36.7 0.7 copy-start.15
  36.7 0.8 copy-start.16
  37.5 0.7 copy-start.17
  45.6 7.3 %collective-permute-start.10 = (f32[24,128]{1,0:T(8,128)}, f32[24,128]{1,0:T(8,128)S(1)}, u32[]{:S(2)}, u32[]{:S(2)}) collective-permute-start(f32[24,128]{1,0:T(8,128)} %get-tuple-element.26), channel_id=1, source_target_pairs={{0,8},{8,0},{1,9},{9,1},{2,10},{10,2},{3,11},{11,3},{4,12},{12,4},... | collective-permute-start | bytes 36872 | tf_op jit(solution)/shard_map/ppermute | solution.py:420
  48.1 19.2 %all-to-all-start.1 = ((f32[16,48,128]{2,1,0:T(8,128)}), f32[16,48,128]{2,1,0:T(8,128)S(1)}, u32[]{:S(2)}, u32[]{:S(2)}) async-start(f32[16,48,128]{2,1,0:T(8,128)} %get-tuple-element.25), calls=%async_computation.1 | async-start | bytes 786432 | tf_op jit(solution)/shard_map/all_to_all | solution.py:468
  53.7 13.6 %copy-start.8 = (f32[24,128]{1,0:T(8,128)}, f32[24,128]{1,0:T(8,128)S(1)}, u32[]{:S(2)}) copy-start(f32[24,128]{1,0:T(8,128)S(1)} %pad_maximum_fusion.refs_2_) | copy-start | bytes 36868
  53.7 7.7 %collective-permute-start.14 = (f32[24,128]{1,0:T(8,128)S(1)}, f32[24,128]{1,0:T(8,128)S(1)}, u32[]{:S(2)}, u32[]{:S(2)}) collective-permute-start(f32[24,128]{1,0:T(8,128)S(1)} %pad_maximum_fusion.refs_2_), channel_id=1, source_target_pairs={{1,0},{2,1},{3,2},{4,3},{5,4},{6,5},{7,6},{0,7},{8,9},{9,10},{10,1... | collective-permute-start | bytes 36872 | tf_op jit(solution)/shard_map/ppermute | solution.py:424
  54.5 6.9 %collective-permute-start.13 = (f32[24,128]{1,0:T(8,128)S(1)}, f32[24,128]{1,0:T(8,128)S(1)}, u32[]{:S(2)}, u32[]{:S(2)}) collective-permute-start(f32[24,128]{1,0:T(8,128)S(1)} %pad_maximum_fusion.refs_2_), channel_id=1, source_target_pairs={{2,0},{3,1},{4,2},{5,3},{6,4},{7,5},{0,6},{1,7},{8,10},{9,11},{10,... | collective-permute-start | bytes 36872 | tf_op jit(solution)/shard_map/ppermute | solution.py:424
  57.2 5.8 %collective-permute-start.12 = (f32[24,128]{1,0:T(8,128)S(1)}, f32[24,128]{1,0:T(8,128)S(1)}, u32[]{:S(2)}, u32[]{:S(2)}) collective-permute-start(f32[24,128]{1,0:T(8,128)S(1)} %pad_maximum_fusion.refs_2_), channel_id=1, source_target_pairs={{3,0},{4,1},{5,2},{6,3},{7,4},{0,5},{1,6},{2,7},{8,11},{9,12},{10,... | collective-permute-start | bytes 36872 | tf_op jit(solution)/shard_map/ppermute | solution.py:424
  60.9 6.5 %collective-permute-start.11 = (f32[24,128]{1,0:T(8,128)S(1)}, f32[24,128]{1,0:T(8,128)S(1)}, u32[]{:S(2)}, u32[]{:S(2)}) collective-permute-start(f32[24,128]{1,0:T(8,128)S(1)} %pad_maximum_fusion.refs_2_), channel_id=1, source_target_pairs={{4,0},{5,1},{6,2},{7,3},{0,4},{1,5},{2,6},{3,7},{8,12},{9,13},{10,... | collective-permute-start | bytes 36872 | tf_op jit(solution)/shard_map/ppermute | solution.py:424
  63.0 4.3 %copy-start.9 = (f32[24,128]{1,0:T(8,128)}, f32[24,128]{1,0:T(8,128)S(1)}, u32[]{:S(2)}) copy-start(f32[24,128]{1,0:T(8,128)S(1)} %pad_maximum_fusion.1.refs_4_) | copy-start | bytes 36868
  63.1 4.3 %collective-permute-start.15 = (f32[24,128]{1,0:T(8,128)S(1)}, f32[24,128]{1,0:T(8,128)S(1)}, u32[]{:S(2)}, u32[]{:S(2)}) collective-permute-start(f32[24,128]{1,0:T(8,128)S(1)} %pad_maximum_fusion.1.refs_4_), channel_id=1, source_target_pairs={{0,8},{8,0},{1,9},{9,1},{2,10},{10,2},{3,11},{11,3},{4,12},{12,4},... | collective-permute-start | bytes 36872 | tf_op jit(solution)/shard_map/ppermute | solution.py:420
  67.3 0.6 copy-start.20
  67.3 0.6 copy-start.21
  67.3 0.8 copy-start.4
  77.6 8.0 %collective-permute-start.17 = (bf16[384,1408]{1,0:T(8,128)(2,1)}, bf16[384,1408]{1,0:T(8,128)(2,1)S(1)}, u32[]{:S(2)}, u32[]{:S(2)}) collective-permute-start(bf16[384,1408]{1,0:T(8,128)(2,1)} %get-tuple-element.32), channel_id=1, source_target_pairs={{0,8},{8,0},{1,9},{9,1},{2,10},{10,2},{3,11},{11,3},{4,12},{12,4},... | collective-permute-start | bytes 3244040 | tf_op jit(solution)/shard_map/ppermute | solution.py:420
  78.5 7.1 %copy-start.3 = (f32[8,128]{1,0:T(8,128)S(1)}, f32[8,128]{1,0:T(8,128)}, u32[]{:S(2)}) copy-start(f32[8,128]{1,0:T(8,128)} %get-tuple-element.30.refs_0_) | copy-start | bytes 12292
  78.5 35.6 %all-to-all-start.2 = ((bf16[16,496,128]{2,1,0:T(8,128)(2,1)}), bf16[16,496,128]{2,1,0:T(8,128)(2,1)S(1)}, u32[]{:S(2)}, u32[]{:S(2)}) async-start(bf16[16,496,128]{2,1,0:T(8,128)(2,1)} %get-tuple-element.40), calls=%async_computation.2 | async-start | bytes 4063232 | tf_op jit(solution)/shard_map/all_to_all | solution.py:497
  85.6 1.1 copy-start
  86.7 16.9 %copy-start.11 = (f32[8,128]{1,0:T(8,128)S(1)}, f32[8,128]{1,0:T(8,128)}, u32[]{:S(2)}) copy-start(f32[8,128]{1,0:T(8,128)} %get-tuple-element.29) | copy-start | bytes 12292
  86.7 17.1 %copy-start.12 = (f32[8,128]{1,0:T(8,128)S(1)}, f32[8,128]{1,0:T(8,128)}, u32[]{:S(2)}) copy-start(f32[8,128]{1,0:T(8,128)} %get-tuple-element.28) | copy-start | bytes 12292
  91.0 9.8 %collective-permute-start.19 = (bf16[96,1408]{1,0:T(8,128)(2,1)S(1)}, bf16[96,1408]{1,0:T(8,128)(2,1)S(1)}, u32[]{:S(2)}, u32[]{:S(2)}) collective-permute-start(bf16[96,1408]{1,0:T(8,128)(2,1)S(1)} %get-tuple-element.36), channel_id=1, source_target_pairs={{0,1},{1,2},{2,3},{3,4},{4,5},{5,6},{6,7},{7,0},{9,8},{10,9},{11,1... | collective-permute-start | bytes 811016 | tf_op jit(solution)/shard_map/ppermute | solution.py:428
  91.8 9.0 %collective-permute-start.20 = (bf16[48,1408]{1,0:T(8,128)(2,1)S(1)}, bf16[48,1408]{1,0:T(8,128)(2,1)S(1)}, u32[]{:S(2)}, u32[]{:S(2)}) collective-permute-start(bf16[48,1408]{1,0:T(8,128)(2,1)S(1)} %get-tuple-element.37), channel_id=1, source_target_pairs={{0,2},{1,3},{2,4},{3,5},{4,6},{5,7},{6,0},{7,1},{10,8},{11,9},{12,... | collective-permute-start | bytes 405512 | tf_op jit(solution)/shard_map/ppermute | solution.py:428
  95.6 9.5 %collective-permute-start.18 = (bf16[96,1408]{1,0:T(8,128)(2,1)}, bf16[96,1408]{1,0:T(8,128)(2,1)S(1)}, u32[]{:S(2)}, u32[]{:S(2)}) collective-permute-start(bf16[96,1408]{1,0:T(8,128)(2,1)} %get-tuple-element.34), channel_id=1, source_target_pairs={{0,1},{1,2},{2,3},{3,4},{4,5},{5,6},{6,7},{7,0},{9,8},{10,9},{11,1... | collective-permute-start | bytes 811016 | tf_op jit(solution)/shard_map/ppermute | solution.py:428
  101.4 9.1 %collective-permute-start.21 = (bf16[96,1408]{1,0:T(8,128)(2,1)S(1)}, bf16[96,1408]{1,0:T(8,128)(2,1)S(1)}, u32[]{:S(2)}, u32[]{:S(2)}) collective-permute-start(bf16[96,1408]{1,0:T(8,128)(2,1)S(1)} %shard_map.87), channel_id=1, source_target_pairs={{0,2},{1,3},{2,4},{3,5},{4,6},{5,7},{6,0},{7,1},{10,8},{11,9},{12,... | collective-permute-start | bytes 811016 | tf_op jit(solution)/shard_map/ppermute | solution.py:428
  103.7 1.3 %collective-permute-start.16 = (f32[16,1,48]{2,0,1:T(8,128)S(1)}, f32[16,1,48]{2,0,1:T(8,128)S(1)}, u32[]{:S(2)}, u32[]{:S(2)}) collective-permute-start(f32[16,1,48]{2,0,1:T(8,128)S(1)} %bitcast.11), channel_id=1, source_target_pairs={{0,8},{8,0},{1,9},{9,1},{2,10},{10,2},{3,11},{11,3},{4,12},{12,4},... | collective-permute-start | bytes 9224 | tf_op jit(solution)/shard_map/ppermute | solution.py:420
  103.8 12.1 %copy-start.2 = (f32[384]{0:T(512)}, f32[384]{0:T(512)S(1)}, u32[]{:S(2)}) copy-start(f32[384]{0:T(512)S(1)} %dynamic-slice_bitcast_fusion.refs_0_) | copy-start | bytes 4612
  105.1 10.9 %copy-start.1 = (f32[1536]{0:T(1024)}, f32[1536]{0:T(1024)S(1)}, u32[]{:S(2)}) copy-start(f32[1536]{0:T(1024)S(1)} %select_n.80.refs_1_) | copy-start | bytes 18436
  110.7 4.5 %collective-permute-start.22 = (f32[48,1408]{1,0:T(8,128)S(1)}, f32[48,1408]{1,0:T(8,128)S(1)}, u32[]{:S(2)}, u32[]{:S(2)}) collective-permute-start(f32[48,1408]{1,0:T(8,128)S(1)} %get-tuple-element.39.unread), channel_id=1, source_target_pairs={{0,8},{8,0},{1,9},{9,1},{2,10},{10,2},{3,11},{11,3},{4,12},{12,4},... | collective-permute-start | bytes 811016 | tf_op jit(solution)/shard_map/ppermute | solution.py:420

commit v6 on v5

--- a/solution.py
+++ b/solution.py
@@ -8,7 +8,8 @@
 from jax.sharding import Mesh, PartitionSpec as P
 
 NY, NX, NC = 4, 4, 2
-XY = ("x", "y")
+CHIP = ("y1", "y0", "x1", "x0")
+XY = ("y0", "y1", "x0", "x1")
 CZ = ("c", "z")
 SWAP = [(0, 1), (1, 0)]
 LANES = 128
@@ -70,7 +71,7 @@
             copy.wait()
 
 
-def call(body, out_shape, *args, flops=0, smem=(), scratch=(), cuts=(), joined=None, held=None, sends=16, spare=0, later=()):
+def call(body, out_shape, *args, flops=0, smem=(), scratch=(), cuts=(), joined=None, held=None, sends=16, spare=0, later=(), fixed=()):
     many = isinstance(out_shape, tuple)
     shapes = out_shape if many else (out_shape,)
     held = [x if held is None or held[i] is None else held[i] for i, x in enumerate(shapes)]
@@ -111,7 +112,10 @@
     return pl.pallas_call(
         kernel,
         out_shape=out_shape,
-        in_specs=[scalars if i in smem else far for i in range(len(args))],
+        in_specs=[
+            scalars if i in smem else pl.BlockSpec(memory_space=pltpu.HBM) if i in fixed else far
+            for i in range(len(args))
+        ],
         out_specs=tuple(far for _ in shapes) if many else far,
         scratch_shapes=[
             *buffers_of,
@@ -313,8 +317,7 @@
         hit = lax.broadcasted_iota(jnp.int32, x.shape, 1) == column[at, 1:2].astype(jnp.int32)
         value = 0.5 * (jnp.exp(x - column[at, 0:1]) + jnp.exp(x - flat)) - jnp.where(hit, 1.0, 0.0)
         grad[i * part : (i + 1) * part, :] = (s * value).astype(BF16)
-    first[...] = grad[:half, :]
-    sender.send(first, outs[1])
+    sender.send(grad.at[:half, :], outs[1])
 
     for i, n in enumerate(range(0, embed, 256)):
         txt.part(i)
@@ -439,7 +442,9 @@
     block = rem // part
     ours = pair_col // (cols * NC) == z
     chip = block // NC
-    place = ((chip % NX * NY + chip // NX) * part + rem % part).astype(F32)
+    bits = len(CHIP) - 1
+    spot = sum((chip >> (bits - CHIP.index(a)) & 1) << (bits - i) for i, a in enumerate(XY))
+    place = (spot * part + rem % part).astype(F32)
     mine = jnp.where(ours & (block % NC == c), place, -1.0)
     theirs = swap(jnp.where(ours & (block % NC == 1 - c), place, -1.0))
     pairs = jnp.where(c == 0, jnp.concatenate([mine, theirs]), jnp.concatenate([theirs, mine]))
@@ -461,7 +466,7 @@
         joined=3,
         later=(2, 3),
         held=(None, None, message),
-        spare=SPARE,
+        spare=1 << 20,
         sends=1 + cols // 256 + peers,
         scratch=[vmem((rows, 8), F32), vmem((rows, LANES), F32)],
     )
@@ -490,7 +495,7 @@
         cuts={7: (0, part), 8: (1, 256)},
         joined=9,
         later=(8, 9),
-        spare=SPARE,
+        spare=1 << 20,
         scratch=[vmem((rows, 8), F32), vmem((rows, cols), BF16), vmem((cols, rows), BF16)],
     )
     received = swap(send)
@@ -505,11 +510,13 @@
         received,
         flops=work // 2,
         cuts={2: (1, 256), 3: (1, 256)},
+        fixed=(1, 2, 3),
         spare=VMEM_BYTES // 2,
     )
     two = call(forward_kernel, chip_rows, two, onward(three, 1), onward(four, 2), spare=VMEM_BYTES // 2)
     row_loss = lax.dynamic_slice(row_loss, (c * (count // NC), 0), (count // NC, LANES)).reshape(-1)
-    col_loss = jnp.swapaxes(col_loss[:count].reshape(NX, NY, part), 0, 1).reshape(peers, 1, part)
+    col_loss = col_loss[:count].reshape(2, 2, 2, 2, part)
+    col_loss = col_loss.transpose([XY.index(a) for a in CHIP] + [4]).reshape(peers, 1, part)
     other = swap(col_loss)
     col_loss = jnp.where(
         c == 0, jnp.concatenate([col_loss, other], 1), jnp.concatenate([other, col_loss], 1)
@@ -539,8 +546,8 @@
 
 def solution(mesh):
     nz = mesh.shape["txt"]
-    grid = Mesh(mesh.devices.reshape(NY, NX, NC, nz), ("y", "x", "c", "z"))
-    images, texts = ("y", "x", "c", "z"), ("z", "y", "x", "c")
-    in_specs = (P(images, None), P(texts, None), P(("y", "x", "c")), P())
-    out_specs = (P(("y", "x", "c")), P("z"), P(images, None), P(texts, None), P())
+    grid = Mesh(mesh.devices.reshape(2, 2, 2, 2, NC, nz), (*CHIP, "c", "z"))
+    images, texts = (*CHIP, "c", "z"), ("z", *CHIP, "c")
+    in_specs = (P(images, None), P(texts, None), P((*CHIP, "c")), P())
+    out_specs = (P((*CHIP, "c")), P("z"), P(images, None), P(texts, None), P())
     return jax.shard_map(local, mesh=grid, in_specs=in_specs, out_specs=out_specs, check_vma=False)

time: 116 us -> 116 us (level)
  waiting for transfers between devices: 25.8 us -> 24 us
  starting transfers between devices: 57.6 us -> 59.4 us
    all_to_all x1, waiting for transfers between devices: 2.68 us -> 0.01 us  [local(): text_got = lax.all_to_all(text_term, XY, 0, 0)]
    ppermute x11, starting transfers between devices: 15.3 us -> 17.2 us  [swap(): return lax.ppermute(x, 'c', SWAP)]
    all_to_all x1, starting transfers between devices: 4.84 us -> 6.2 us  [local(): col_got = lax.all_to_all(msg, XY, 0, 0)]
  transfers between devices with their start and end apart: 26 -> 26, of which waited for: 10 -> 11; matrix products, arithmetic and copies ran while one was open for 1% -> 1% of each run, Pallas kernels for 5% -> 5%
where the time goes in v6:
time: 116 us
  starting transfers between devices  59.4 us (51%)
  Pallas kernels  26 us (22%)
  waiting for transfers between devices  24 us (21%)
  local copies, waits for them, and re-layouts  4.1 us (4%)
  between operations  1.65 us (1%)
    pallas_call x5, Pallas kernels, call(): pl.pallas_call(kernel, out_shape=out_shape, in_specs=[scalars if i in sme...  24.2 us
    ppermute x11, starting transfers between devices, swap(): return lax.ppermute(x, 'c', SWAP)  17.2 us
    ppermute x8, starting transfers between devices, ahead(): lax.ppermute(x, CZ, pairs + [(nz + i, nz + (i + k) % nz) for i in range(n...  14.5 us
    ppermute x8, waiting for transfers between devices, ahead(): lax.ppermute(x, CZ, pairs + [(nz + i, nz + (i + k) % nz) for i in range(n...  11.1 us
    ppermute x4, waiting for transfers between devices, onward(): lax.ppermute(x, CZ, pairs + [(nz + (i + k) % nz, nz + i) for i in range(n...  10.3 us
    all_to_all x1, starting transfers between devices, local(): txt = lax.all_to_all(spread, XY, 0, 0).reshape(cols, embed)  7.77 us
    all_to_all x1, starting transfers between devices, local(): text_got = lax.all_to_all(text_term, XY, 0, 0)  7.06 us
    ppermute x4, starting transfers between devices, onward(): lax.ppermute(x, CZ, pairs + [(nz + (i + k) % nz, nz + i) for i in range(n...  6.64 us
  transfers between devices with their start and end apart: 26, of which 11 were waited for; matrix products, arithmetic and copies ran while one was open for 1% of the time, Pallas kernels for 5%

profile of v6, /device:TPU:1, one launch (start us, length us, event | category | flops | bytes accessed | tf_op | source)
XLA Modules:
  0.0 116.0 jit_solution(12198668359043860274)
XLA Ops:
  0.6 2.4 %shard_map.83 = bf16[16,48,1280]{2,1,0:T(8,128)(2,1)} custom-call(bf16[48,1280]{1,0:T(8,128)(2,1)} %refs_0_.1), custom_call_target="tpu_custom_call" | custom-call | flops 17179869184 | bytes 122880 | tf_op jit(solution)/shard_map/pallas_call | solution.py:112
  3.0 0.0 copy-start.5
  3.0 0.0 copy-start.10
  3.0 7.8 %all-to-all-start = ((bf16[16,48,1280]{2,1,0:T(8,128)(2,1)}), bf16[16,48,1280]{2,1,0:T(8,128)(2,1)}, u32[]{:S(2)}, u32[]{:S(2)}) async-start(bf16[16,48,1280]{2,1,0:T(8,128)(2,1)} %shard_map.83), calls=%async_computation | async-start | bytes 3932160 | tf_op jit(solution)/shard_map/all_to_all | solution.py:434
  10.8 1.0 collective-permute-start.1
  11.9 1.0 collective-permute-done.1.refs_12_.refs_18_
  12.8 3.1 %collective-permute-start.3 = (bf16[96,1280]{1,0:T(8,128)(2,1)S(1)}, bf16[96,1280]{1,0:T(8,128)(2,1)S(1)}, u32[]{:S(2)}, u32[]{:S(2)}) collective-permute-start(bf16[96,1280]{1,0:T(8,128)(2,1)S(1)} %constant_dynamic-update-slice_fusion), channel_id=1, source_target_pairs={{2,0},{3,1},{4,2},{5,3},{6,4},{7,5},{0,6},{1,7},{8,10},{9,11},{10,... | collective-permute-start | bytes 737288 | tf_op jit(solution)/shard_map/ppermute | solution.py:427
  15.9 1.6 %collective-permute-start.2 = (bf16[96,1280]{1,0:T(8,128)(2,1)S(1)}, bf16[96,1280]{1,0:T(8,128)(2,1)S(1)}, u32[]{:S(2)}, u32[]{:S(2)}) collective-permute-start(bf16[96,1280]{1,0:T(8,128)(2,1)S(1)} %constant_dynamic-update-slice_fusion), channel_id=1, source_target_pairs={{1,0},{2,1},{3,2},{4,3},{5,4},{6,5},{7,6},{0,7},{8,9},{9,10},{10,1... | collective-permute-start | bytes 737288 | tf_op jit(solution)/shard_map/ppermute | solution.py:427
  17.5 5.8 %collective-permute-done.3.refs_4_.refs_10_ = bf16[96,1280]{1,0:T(8,128)(2,1)S(1)} collective-permute-done((bf16[96,1280]{1,0:T(8,128)(2,1)S(1)}, bf16[96,1280]{1,0:T(8,128)(2,1)S(1)}, u32[]{:S(2)}, u32[]{:S(2)}) %collective-permute-start.3) | collective-permute-done | bytes 245792 | tf_op jit(solution)/shard_map/ppermute | solution.py:427
  23.4 2.6 %collective-permute-start.4 = (bf16[96,1280]{1,0:T(8,128)(2,1)S(1)}, bf16[96,1280]{1,0:T(8,128)(2,1)S(1)}, u32[]{:S(2)}, u32[]{:S(2)}) collective-permute-start(bf16[96,1280]{1,0:T(8,128)(2,1)S(1)} %collective-permute-done.3.refs_4_.refs_10_), channel_id=1, source_target_pairs={{1,0},{2,1},{3,2},{4,3},{5,4},{6,5},{7,6},{0,7},{8,9},{9,10},{10,1... | collective-permute-start | bytes 737288 | tf_op jit(solution)/shard_map/ppermute | solution.py:427
  26.1 0.1 collective-permute-start.5
  26.2 4.6 %collective-permute-start.7 = (bf16[96,1280]{1,0:T(8,128)(2,1)S(1)}, bf16[96,1280]{1,0:T(8,128)(2,1)S(1)}, u32[]{:S(2)}, u32[]{:S(2)}) collective-permute-start(bf16[96,1280]{1,0:T(8,128)(2,1)S(1)} %collective-permute-done.3.refs_4_.refs_10_), channel_id=1, source_target_pairs={{0,8},{8,0},{1,9},{9,1},{2,10},{10,2},{3,11},{11,3},{4,12},{12,4},... | collective-permute-start | bytes 737288 | tf_op jit(solution)/shard_map/ppermute | solution.py:423
  30.8 0.0 collective-permute-done.2.refs_3_.refs_9_
  30.8 0.1 collective-permute-start.6
  30.9 0.2 collective-permute-done.4.refs_5_.refs_11_
  31.0 1.4 %collective-permute-start.8 = (bf16[96,1280]{1,0:T(8,128)(2,1)S(1)}, bf16[96,1280]{1,0:T(8,128)(2,1)S(1)}, u32[]{:S(2)}, u32[]{:S(2)}) collective-permute-start(bf16[96,1280]{1,0:T(8,128)(2,1)S(1)} %collective-permute-done.4.refs_5_.refs_11_), channel_id=1, source_target_pairs={{0,8},{8,0},{1,9},{9,1},{2,10},{10,2},{3,11},{11,3},{4,12},{12,4},... | collective-permute-start | bytes 737288 | tf_op jit(solution)/shard_map/ppermute | solution.py:423
  32.5 0.1 collective-permute-start
  33.2 1.2 %collective-permute-done.5.refs_6_.refs_12_ = bf16[48,1280]{1,0:T(8,128)(2,1)S(1)} collective-permute-done((bf16[48,1280]{1,0:T(8,128)(2,1)S(1)}, bf16[48,1280]{1,0:T(8,128)(2,1)S(1)}, u32[]{:S(2)}, u32[]{:S(2)}) %collective-permute-start.5) | collective-permute-done | bytes 122912 | tf_op jit(solution)/shard_map/ppermute | solution.py:427
  34.5 1.3 %collective-permute-start.9 = (bf16[48,1280]{1,0:T(8,128)(2,1)S(1)}, bf16[48,1280]{1,0:T(8,128)(2,1)S(1)}, u32[]{:S(2)}, u32[]{:S(2)}) collective-permute-start(bf16[48,1280]{1,0:T(8,128)(2,1)S(1)} %collective-permute-done.5.refs_6_.refs_12_), channel_id=1, source_target_pairs={{0,8},{8,0},{1,9},{9,1},{2,10},{10,2},{3,11},{11,3},{4,12},{12,4},... | collective-permute-start | bytes 368648 | tf_op jit(solution)/shard_map/ppermute | solution.py:423
  35.7 0.0 collective-permute-done
  35.8 0.6 pad_bitcast_fusion.refs_1_.refs_6_
  36.4 0.4 collective-permute-done.9.refs_11_.refs_17_
  36.7 0.0 collective-permute-done.7.refs_9_.refs_15_
  36.8 0.7 copy-done.15
  37.5 0.1 copy-done.16
  37.6 0.0 copy-done.19
  37.6 0.6 copy-done.17
  38.2 7.4 %shard_map.84 = (f32[768,768]{1,0:T(8,128)}, f32[24,128]{1,0:T(8,128)}, f32[16,48,128]{2,1,0:T(8,128)}) custom-call(f32[1]{0:T(128)} %bitcast.refs_0_, f32[8,128]{1,0:T(8,128)} %pad_bitcast_fusion.refs_1_.refs_6_, bf16[768,1280]{1,0:T(8,128)(2,1)} %bitcast.2.refs_2_.refs_8_, bf16[96,1280]{1,0:T(8,128)(2,1)} %copy-done.13, bf16[96,1280]{1,0:T(8,128)(2,1)} %copy-done.7, ...), custom_call_target="tpu_custom_call" | custom-call | flops 1509949440 | bytes 3936260 | tf_op jit(solution)/shard_map/pallas_call | solution.py:112
  45.6 1.1 collective-permute-start.10
  46.7 6.2 %all-to-all-start.1 = ((f32[16,48,128]{2,1,0:T(8,128)}), f32[16,48,128]{2,1,0:T(8,128)S(1)}, u32[]{:S(2)}, u32[]{:S(2)}) async-start(f32[16,48,128]{2,1,0:T(8,128)} %get-tuple-element.25), calls=%async_computation.1 | async-start | bytes 786432 | tf_op jit(solution)/shard_map/all_to_all | solution.py:473
  53.0 0.7 log_add_fusion.1
  53.7 0.8 collective-permute-start.14
  54.5 2.6 %collective-permute-start.13 = (f32[24,128]{1,0:T(8,128)S(1)}, f32[24,128]{1,0:T(8,128)S(1)}, u32[]{:S(2)}, u32[]{:S(2)}) collective-permute-start(f32[24,128]{1,0:T(8,128)S(1)} %pad_maximum_fusion.refs_2_), channel_id=1, source_target_pairs={{2,0},{3,1},{4,2},{5,3},{6,4},{7,5},{0,6},{1,7},{8,10},{9,11},{10,... | collective-permute-start | bytes 36872 | tf_op jit(solution)/shard_map/ppermute | solution.py:427
  57.1 3.0 %collective-permute-start.12 = (f32[24,128]{1,0:T(8,128)S(1)}, f32[24,128]{1,0:T(8,128)S(1)}, u32[]{:S(2)}, u32[]{:S(2)}) collective-permute-start(f32[24,128]{1,0:T(8,128)S(1)} %pad_maximum_fusion.refs_2_), channel_id=1, source_target_pairs={{3,0},{4,1},{5,2},{6,3},{7,4},{0,5},{1,6},{2,7},{8,11},{9,12},{10,... | collective-permute-start | bytes 36872 | tf_op jit(solution)/shard_map/ppermute | solution.py:427
  60.1 0.5 collective-permute-start.11
  60.7 2.3 %collective-permute-done.12 = f32[24,128]{1,0:T(8,128)S(1)} collective-permute-done((f32[24,128]{1,0:T(8,128)S(1)}, f32[24,128]{1,0:T(8,128)S(1)}, u32[]{:S(2)}, u32[]{:S(2)}) %collective-permute-start.12) | collective-permute-done | bytes 12320 | tf_op jit(solution)/shard_map/ppermute | solution.py:427
  63.0 2.0 %collective-permute-start.15 = (f32[24,128]{1,0:T(8,128)S(1)}, f32[24,128]{1,0:T(8,128)S(1)}, u32[]{:S(2)}, u32[]{:S(2)}) collective-permute-start(f32[24,128]{1,0:T(8,128)S(1)} %pad_maximum_fusion.1.refs_4_), channel_id=1, source_target_pairs={{0,8},{8,0},{1,9},{9,1},{2,10},{10,2},{3,11},{11,3},{4,12},{12,4},... | collective-permute-start | bytes 36872 | tf_op jit(solution)/shard_map/ppermute | solution.py:423
  65.0 1.6 %collective-permute-done.11.refs_3_ = f32[24,128]{1,0:T(8,128)S(1)} collective-permute-done((f32[24,128]{1,0:T(8,128)S(1)}, f32[24,128]{1,0:T(8,128)S(1)}, u32[]{:S(2)}, u32[]{:S(2)}) %collective-permute-start.11) | collective-permute-done | bytes 12320 | tf_op jit(solution)/shard_map/ppermute | solution.py:427
  66.6 0.6 copy-done.20
  67.2 0.0 copy-done.21
  67.2 0.2 copy-done.4
  67.4 9.5 %shard_map.85 = (bf16[16,496,128]{2,1,0:T(8,128)(2,1)}, bf16[384,768]{1,0:T(8,128)(2,1)}, f32[8,128]{1,0:T(8,128)}, f32[8,128]{1,0:T(8,128)}, f32[8,128]{1,0:T(8,128)}, /*index=5*/bf16[384,1408]{1,0:T(8,128)(2,1)}) custom-call(f32[1]{0:T(128)} %bitcast.refs_0_, f32[16,48,128]{2,1,0:T(8,128)} %copy-done.4, f32[24,128]{1,0:T(8,128)} %copy-done.8, ...), custom_call_target="tpu_custom_call" | custom-call | flops 3019898880 | bytes 6737924 | tf_op jit(solution)/shard_map/pallas_call | solution.py:112
  76.9 1.6 %collective-permute-start.17 = (bf16[384,1408]{1,0:T(8,128)(2,1)}, bf16[384,1408]{1,0:T(8,128)(2,1)S(1)}, u32[]{:S(2)}, u32[]{:S(2)}) collective-permute-start(bf16[384,1408]{1,0:T(8,128)(2,1)} %get-tuple-element.32), channel_id=1, source_target_pairs={{0,8},{8,0},{1,9},{9,1},{2,10},{10,2},{3,11},{11,3},{4,12},{12,4},... | collective-permute-start | bytes 3244040 | tf_op jit(solution)/shard_map/ppermute | solution.py:423
  78.5 7.1 %all-to-all-start.2 = ((bf16[16,496,128]{2,1,0:T(8,128)(2,1)}), bf16[16,496,128]{2,1,0:T(8,128)(2,1)S(1)}, u32[]{:S(2)}, u32[]{:S(2)}) async-start(bf16[16,496,128]{2,1,0:T(8,128)(2,1)} %get-tuple-element.40), calls=%async_computation.2 | async-start | bytes 4063232 | tf_op jit(solution)/shard_map/all_to_all | solution.py:502
  85.6 1.1 copy-done
  86.7 4.3 %shard_map.86 = (bf16[96,1408]{1,0:T(8,128)(2,1)}, f32[96,1408]{1,0:T(8,128)S(1)}, bf16[96,1408]{1,0:T(8,128)(2,1)S(1)}, bf16[48,1408]{1,0:T(8,128)(2,1)S(1)}, f32[48,1408]{1,0:T(8,128)S(1)}) custom-call(f32[8,128]{1,0:T(8,128)S(1)} %copy-done.3, bf16[384,768]{1,0:T(8,128)(2,1)S(1)} %copy-done, bf16[768,1280]{1,0:T(8,128)(2,1)} %bitcast.2.refs_2_.refs_8_, ...), custom_call_target="tpu_custom_call" | custom-call | flops 754974720 | bytes 3641344 | tf_op jit(solution)/shard_map/pallas_call | solution.py:112
  91.0 0.2 collective-permute-start.19
  91.2 3.8 %collective-permute-start.20 = (bf16[48,1408]{1,0:T(8,128)(2,1)S(1)}, bf16[48,1408]{1,0:T(8,128)(2,1)S(1)}, u32[]{:S(2)}, u32[]{:S(2)}) collective-permute-start(bf16[48,1408]{1,0:T(8,128)(2,1)S(1)} %get-tuple-element.37), channel_id=1, source_target_pairs={{0,2},{1,3},{2,4},{3,5},{4,6},{5,7},{6,0},{7,1},{10,8},{11,9},{12,... | collective-permute-start | bytes 405512 | tf_op jit(solution)/shard_map/ppermute | solution.py:431
  95.0 0.7 collective-permute-start.18
  95.7 5.1 %collective-permute-done.20.refs_2_ = bf16[48,1408]{1,0:T(8,128)(2,1)S(1)} collective-permute-done((bf16[48,1408]{1,0:T(8,128)(2,1)S(1)}, bf16[48,1408]{1,0:T(8,128)(2,1)S(1)}, u32[]{:S(2)}, u32[]{:S(2)}) %collective-permute-start.20) | collective-permute-done | bytes 135200 | tf_op jit(solution)/shard_map/ppermute | solution.py:431
  100.8 0.6 shard_map.87
  101.4 2.0 %collective-permute-start.21 = (bf16[96,1408]{1,0:T(8,128)(2,1)S(1)}, bf16[96,1408]{1,0:T(8,128)(2,1)S(1)}, u32[]{:S(2)}, u32[]{:S(2)}) collective-permute-start(bf16[96,1408]{1,0:T(8,128)(2,1)S(1)} %shard_map.87), channel_id=1, source_target_pairs={{0,2},{1,3},{2,4},{3,5},{4,6},{5,7},{6,0},{7,1},{10,8},{11,9},{12,... | collective-permute-start | bytes 811016 | tf_op jit(solution)/shard_map/ppermute | solution.py:431
  103.4 0.1 reshape.33
  103.5 0.1 collective-permute-start.16
  103.6 0.0 copy-start.2
  103.6 1.1 collective-permute-done.16
  104.8 0.1 select_n.71.refs_1_
  104.8 0.0 collective-permute-done.18.one
  104.9 5.2 %collective-permute-done.21.two = bf16[96,1408]{1,0:T(8,128)(2,1)S(1)} collective-permute-done((bf16[96,1408]{1,0:T(8,128)(2,1)S(1)}, bf16[96,1408]{1,0:T(8,128)(2,1)S(1)}, u32[]{:S(2)}, u32[]{:S(2)}) %collective-permute-start.21) | collective-permute-done | bytes 270368 | tf_op jit(solution)/shard_map/ppermute | solution.py:431
  110.0 0.1 shard_map.88
  110.1 3.9 %collective-permute-start.22 = (f32[48,1408]{1,0:T(8,128)S(1)}, f32[48,1408]{1,0:T(8,128)S(1)}, u32[]{:S(2)}, u32[]{:S(2)}) collective-permute-start(f32[48,1408]{1,0:T(8,128)S(1)} %get-tuple-element.39.unread), channel_id=1, source_target_pairs={{0,8},{8,0},{1,9},{9,1},{2,10},{10,2},{3,11},{11,3},{4,12},{12,4},... | collective-permute-start | bytes 811016 | tf_op jit(solution)/shard_map/ppermute | solution.py:423
  114.1 1.0 shard_map.89
  115.1 0.1 collective-permute-done.22.received
  115.2 0.7 shard_map.90
  (57 shorter events, 0.2 us)
Async XLA Ops:
  3.0 7.8 %copy-start.5 = (bf16[48,1280]{1,0:T(8,128)(2,1)S(1)}, bf16[48,1280]{1,0:T(8,128)(2,1)}, u32[]{:S(2)}) copy-start(bf16[48,1280]{1,0:T(8,128)(2,1)} %refs_13_.1) | copy-start | bytes 368644
  3.0 23.0 %copy-start.10 = (s32[384]{0:T(512)S(1)}, s32[384]{0:T(512)}, u32[]{:S(2)}) copy-start(s32[384]{0:T(512)} %param.6) | copy-start | bytes 4612
  3.0 34.5 %all-to-all-start = ((bf16[16,48,1280]{2,1,0:T(8,128)(2,1)}), bf16[16,48,1280]{2,1,0:T(8,128)(2,1)}, u32[]{:S(2)}, u32[]{:S(2)}) async-start(bf16[16,48,1280]{2,1,0:T(8,128)(2,1)} %shard_map.83), calls=%async_computation | async-start | bytes 3932160 | tf_op jit(solution)/shard_map/all_to_all | solution.py:434
  10.8 2.0 %collective-permute-start.1 = (bf16[48,1280]{1,0:T(8,128)(2,1)S(1)}, bf16[48,1280]{1,0:T(8,128)(2,1)S(1)}, u32[]{:S(2)}, u32[]{:S(2)}) collective-permute-start(bf16[48,1280]{1,0:T(8,128)(2,1)S(1)} %copy-done.5), channel_id=1, source_target_pairs={{0,8},{8,0},{1,9},{9,1},{2,10},{10,2},{3,11},{11,3},{4,12},{12,4},... | collective-permute-start | bytes 368648 | tf_op jit(solution)/shard_map/ppermute | solution.py:423
  12.8 25.3 %copy-start.6 = (bf16[48,1280]{1,0:T(8,128)(2,1)}, bf16[48,1280]{1,0:T(8,128)(2,1)S(1)}, u32[]{:S(2)}) copy-start(bf16[48,1280]{1,0:T(8,128)(2,1)S(1)} %collective-permute-done.1.refs_12_.refs_18_) | copy-start | bytes 368644
  12.8 10.5 %collective-permute-start.3 = (bf16[96,1280]{1,0:T(8,128)(2,1)S(1)}, bf16[96,1280]{1,0:T(8,128)(2,1)S(1)}, u32[]{:S(2)}, u32[]{:S(2)}) collective-permute-start(bf16[96,1280]{1,0:T(8,128)(2,1)S(1)} %constant_dynamic-update-slice_fusion), channel_id=1, source_target_pairs={{2,0},{3,1},{4,2},{5,3},{6,4},{7,5},{0,6},{1,7},{8,10},{9,11},{10,... | collective-permute-start | bytes 737288 | tf_op jit(solution)/shard_map/ppermute | solution.py:427
  15.9 14.9 %collective-permute-start.2 = (bf16[96,1280]{1,0:T(8,128)(2,1)S(1)}, bf16[96,1280]{1,0:T(8,128)(2,1)S(1)}, u32[]{:S(2)}, u32[]{:S(2)}) collective-permute-start(bf16[96,1280]{1,0:T(8,128)(2,1)S(1)} %constant_dynamic-update-slice_fusion), channel_id=1, source_target_pairs={{1,0},{2,1},{3,2},{4,3},{5,4},{6,5},{7,6},{0,7},{8,9},{9,10},{10,1... | collective-permute-start | bytes 737288 | tf_op jit(solution)/shard_map/ppermute | solution.py:427
  23.4 14.8 %copy-start.7 = (bf16[96,1280]{1,0:T(8,128)(2,1)}, bf16[96,1280]{1,0:T(8,128)(2,1)S(1)}, u32[]{:S(2)}) copy-start(bf16[96,1280]{1,0:T(8,128)(2,1)S(1)} %collective-permute-done.3.refs_4_.refs_10_) | copy-start | bytes 737284
  23.4 7.7 %collective-permute-start.4 = (bf16[96,1280]{1,0:T(8,128)(2,1)S(1)}, bf16[96,1280]{1,0:T(8,128)(2,1)S(1)}, u32[]{:S(2)}, u32[]{:S(2)}) collective-permute-start(bf16[96,1280]{1,0:T(8,128)(2,1)S(1)} %collective-permute-done.3.refs_4_.refs_10_), channel_id=1, source_target_pairs={{1,0},{2,1},{3,2},{4,3},{5,4},{6,5},{7,6},{0,7},{8,9},{9,10},{10,1... | collective-permute-start | bytes 737288 | tf_op jit(solution)/shard_map/ppermute | solution.py:427
  26.1 8.4 %collective-permute-start.5 = (bf16[48,1280]{1,0:T(8,128)(2,1)S(1)}, bf16[48,1280]{1,0:T(8,128)(2,1)S(1)}, u32[]{:S(2)}, u32[]{:S(2)}) collective-permute-start(bf16[48,1280]{1,0:T(8,128)(2,1)S(1)} %slice.68), channel_id=1, source_target_pairs={{2,0},{3,1},{4,2},{5,3},{6,4},{7,5},{0,6},{1,7},{8,10},{9,11},{10,... | collective-permute-start | bytes 368648 | tf_op jit(solution)/shard_map/ppermute | solution.py:427
  26.2 10.5 %collective-permute-start.7 = (bf16[96,1280]{1,0:T(8,128)(2,1)S(1)}, bf16[96,1280]{1,0:T(8,128)(2,1)S(1)}, u32[]{:S(2)}, u32[]{:S(2)}) collective-permute-start(bf16[96,1280]{1,0:T(8,128)(2,1)S(1)} %collective-permute-done.3.refs_4_.refs_10_), channel_id=1, source_target_pairs={{0,8},{8,0},{1,9},{9,1},{2,10},{10,2},{3,11},{11,3},{4,12},{12,4},... | collective-permute-start | bytes 737288 | tf_op jit(solution)/shard_map/ppermute | solution.py:423
  30.8 7.4 %copy-start.13 = (bf16[96,1280]{1,0:T(8,128)(2,1)}, bf16[96,1280]{1,0:T(8,128)(2,1)S(1)}, u32[]{:S(2)}) copy-start(bf16[96,1280]{1,0:T(8,128)(2,1)S(1)} %collective-permute-done.2.refs_3_.refs_9_) | copy-start | bytes 737284
  30.8 6.0 %collective-permute-start.6 = (bf16[96,1280]{1,0:T(8,128)(2,1)S(1)}, bf16[96,1280]{1,0:T(8,128)(2,1)S(1)}, u32[]{:S(2)}, u32[]{:S(2)}) collective-permute-start(bf16[96,1280]{1,0:T(8,128)(2,1)S(1)} %collective-permute-done.2.refs_3_.refs_9_), channel_id=1, source_target_pairs={{0,8},{8,0},{1,9},{9,1},{2,10},{10,2},{3,11},{11,3},{4,12},{12,4},... | collective-permute-start | bytes 737288 | tf_op jit(solution)/shard_map/ppermute | solution.py:423
  31.0 7.1 %copy-start.14 = (bf16[96,1280]{1,0:T(8,128)(2,1)}, bf16[96,1280]{1,0:T(8,128)(2,1)S(1)}, u32[]{:S(2)}) copy-start(bf16[96,1280]{1,0:T(8,128)(2,1)S(1)} %collective-permute-done.4.refs_5_.refs_11_) | copy-start | bytes 737284
  31.0 5.7 %collective-permute-start.8 = (bf16[96,1280]{1,0:T(8,128)(2,1)S(1)}, bf16[96,1280]{1,0:T(8,128)(2,1)S(1)}, u32[]{:S(2)}, u32[]{:S(2)}) collective-permute-start(bf16[96,1280]{1,0:T(8,128)(2,1)S(1)} %collective-permute-done.4.refs_5_.refs_11_), channel_id=1, source_target_pairs={{0,8},{8,0},{1,9},{9,1},{2,10},{10,2},{3,11},{11,3},{4,12},{12,4},... | collective-permute-start | bytes 737288 | tf_op jit(solution)/shard_map/ppermute | solution.py:423
  32.5 3.3 %collective-permute-start = (f32[384]{0:T(512)S(1)}, f32[384]{0:T(512)S(1)}, u32[]{:S(2)}, u32[]{:S(2)}) collective-permute-start(f32[384]{0:T(512)S(1)} %and_select_fusion), channel_id=1, source_target_pairs={{0,8},{8,0},{1,9},{9,1},{2,10},{10,2},{3,11},{11,3},{4,12},{12,4},... | collective-permute-start | bytes 4616 | tf_op jit(solution)/shard_map/ppermute | solution.py:423
  34.5 3.1 %copy-start.18 = (bf16[48,1280]{1,0:T(8,128)(2,1)}, bf16[48,1280]{1,0:T(8,128)(2,1)S(1)}, u32[]{:S(2)}) copy-start(bf16[48,1280]{1,0:T(8,128)(2,1)S(1)} %collective-permute-done.5.refs_6_.refs_12_) | copy-start | bytes 368644
  34.5 2.3 %collective-permute-start.9 = (bf16[48,1280]{1,0:T(8,128)(2,1)S(1)}, bf16[48,1280]{1,0:T(8,128)(2,1)S(1)}, u32[]{:S(2)}, u32[]{:S(2)}) collective-permute-start(bf16[48,1280]{1,0:T(8,128)(2,1)S(1)} %collective-permute-done.5.refs_6_.refs_12_), channel_id=1, source_target_pairs={{0,8},{8,0},{1,9},{9,1},{2,10},{10,2},{3,11},{11,3},{4,12},{12,4},... | collective-permute-start | bytes 368648 | tf_op jit(solution)/shard_map/ppermute | solution.py:423
  36.7 0.8 copy-start.19
  36.7 0.7 copy-start.15
  36.7 0.8 copy-start.16
  37.5 0.7 copy-start.17
  45.6 7.4 %collective-permute-start.10 = (f32[24,128]{1,0:T(8,128)}, f32[24,128]{1,0:T(8,128)S(1)}, u32[]{:S(2)}, u32[]{:S(2)}) collective-permute-start(f32[24,128]{1,0:T(8,128)} %get-tuple-element.26), channel_id=1, source_target_pairs={{0,8},{8,0},{1,9},{9,1},{2,10},{10,2},{3,11},{11,3},{4,12},{12,4},... | collective-permute-start | bytes 36872 | tf_op jit(solution)/shard_map/ppermute | solution.py:423
  46.7 19.8 %all-to-all-start.1 = ((f32[16,48,128]{2,1,0:T(8,128)}), f32[16,48,128]{2,1,0:T(8,128)S(1)}, u32[]{:S(2)}, u32[]{:S(2)}) async-start(f32[16,48,128]{2,1,0:T(8,128)} %get-tuple-element.25), calls=%async_computation.1 | async-start | bytes 786432 | tf_op jit(solution)/shard_map/all_to_all | solution.py:473
  53.7 12.9 %copy-start.8 = (f32[24,128]{1,0:T(8,128)}, f32[24,128]{1,0:T(8,128)S(1)}, u32[]{:S(2)}) copy-start(f32[24,128]{1,0:T(8,128)S(1)} %pad_maximum_fusion.refs_2_) | copy-start | bytes 36868
  53.7 7.0 %collective-permute-start.14 = (f32[24,128]{1,0:T(8,128)S(1)}, f32[24,128]{1,0:T(8,128)S(1)}, u32[]{:S(2)}, u32[]{:S(2)}) collective-permute-start(f32[24,128]{1,0:T(8,128)S(1)} %pad_maximum_fusion.refs_2_), channel_id=1, source_target_pairs={{1,0},{2,1},{3,2},{4,3},{5,4},{6,5},{7,6},{0,7},{8,9},{9,10},{10,1... | collective-permute-start | bytes 36872 | tf_op jit(solution)/shard_map/ppermute | solution.py:427
  54.5 6.1 %collective-permute-start.13 = (f32[24,128]{1,0:T(8,128)S(1)}, f32[24,128]{1,0:T(8,128)S(1)}, u32[]{:S(2)}, u32[]{:S(2)}) collective-permute-start(f32[24,128]{1,0:T(8,128)S(1)} %pad_maximum_fusion.refs_2_), channel_id=1, source_target_pairs={{2,0},{3,1},{4,2},{5,3},{6,4},{7,5},{0,6},{1,7},{8,10},{9,11},{10,... | collective-permute-start | bytes 36872 | tf_op jit(solution)/shard_map/ppermute | solution.py:427
  57.1 5.8 %collective-permute-start.12 = (f32[24,128]{1,0:T(8,128)S(1)}, f32[24,128]{1,0:T(8,128)S(1)}, u32[]{:S(2)}, u32[]{:S(2)}) collective-permute-start(f32[24,128]{1,0:T(8,128)S(1)} %pad_maximum_fusion.refs_2_), channel_id=1, source_target_pairs={{3,0},{4,1},{5,2},{6,3},{7,4},{0,5},{1,6},{2,7},{8,11},{9,12},{10,... | collective-permute-start | bytes 36872 | tf_op jit(solution)/shard_map/ppermute | solution.py:427
  60.1 6.5 %collective-permute-start.11 = (f32[24,128]{1,0:T(8,128)S(1)}, f32[24,128]{1,0:T(8,128)S(1)}, u32[]{:S(2)}, u32[]{:S(2)}) collective-permute-start(f32[24,128]{1,0:T(8,128)S(1)} %pad_maximum_fusion.refs_2_), channel_id=1, source_target_pairs={{4,0},{5,1},{6,2},{7,3},{0,4},{1,5},{2,6},{3,7},{8,12},{9,13},{10,... | collective-permute-start | bytes 36872 | tf_op jit(solution)/shard_map/ppermute | solution.py:427
  63.0 3.6 %copy-start.9 = (f32[24,128]{1,0:T(8,128)}, f32[24,128]{1,0:T(8,128)S(1)}, u32[]{:S(2)}) copy-start(f32[24,128]{1,0:T(8,128)S(1)} %pad_maximum_fusion.1.refs_4_) | copy-start | bytes 36868
  63.0 3.5 %collective-permute-start.15 = (f32[24,128]{1,0:T(8,128)S(1)}, f32[24,128]{1,0:T(8,128)S(1)}, u32[]{:S(2)}, u32[]{:S(2)}) collective-permute-start(f32[24,128]{1,0:T(8,128)S(1)} %pad_maximum_fusion.1.refs_4_), channel_id=1, source_target_pairs={{0,8},{8,0},{1,9},{9,1},{2,10},{10,2},{3,11},{11,3},{4,12},{12,4},... | collective-permute-start | bytes 36872 | tf_op jit(solution)/shard_map/ppermute | solution.py:423
  66.6 0.6 copy-start.20
  66.6 0.6 copy-start.21
  66.6 0.8 copy-start.4
  76.9 8.7 %collective-permute-start.17 = (bf16[384,1408]{1,0:T(8,128)(2,1)}, bf16[384,1408]{1,0:T(8,128)(2,1)S(1)}, u32[]{:S(2)}, u32[]{:S(2)}) collective-permute-start(bf16[384,1408]{1,0:T(8,128)(2,1)} %get-tuple-element.32), channel_id=1, source_target_pairs={{0,8},{8,0},{1,9},{9,1},{2,10},{10,2},{3,11},{11,3},{4,12},{12,4},... | collective-permute-start | bytes 3244040 | tf_op jit(solution)/shard_map/ppermute | solution.py:423
  78.5 7.1 %copy-start.3 = (f32[8,128]{1,0:T(8,128)S(1)}, f32[8,128]{1,0:T(8,128)}, u32[]{:S(2)}) copy-start(f32[8,128]{1,0:T(8,128)} %get-tuple-element.30.refs_0_) | copy-start | bytes 12292
  78.5 35.5 %all-to-all-start.2 = ((bf16[16,496,128]{2,1,0:T(8,128)(2,1)}), bf16[16,496,128]{2,1,0:T(8,128)(2,1)S(1)}, u32[]{:S(2)}, u32[]{:S(2)}) async-start(bf16[16,496,128]{2,1,0:T(8,128)(2,1)} %get-tuple-element.40), calls=%async_computation.2 | async-start | bytes 4063232 | tf_op jit(solution)/shard_map/all_to_all | solution.py:502
  85.6 1.1 copy-start
  86.7 16.7 %copy-start.11 = (f32[8,128]{1,0:T(8,128)S(1)}, f32[8,128]{1,0:T(8,128)}, u32[]{:S(2)}) copy-start(f32[8,128]{1,0:T(8,128)} %get-tuple-element.29) | copy-start | bytes 12292
  86.7 16.9 %copy-start.12 = (f32[8,128]{1,0:T(8,128)S(1)}, f32[8,128]{1,0:T(8,128)}, u32[]{:S(2)}) copy-start(f32[8,128]{1,0:T(8,128)} %get-tuple-element.28) | copy-start | bytes 12292
  91.0 9.8 %collective-permute-start.19 = (bf16[96,1408]{1,0:T(8,128)(2,1)S(1)}, bf16[96,1408]{1,0:T(8,128)(2,1)S(1)}, u32[]{:S(2)}, u32[]{:S(2)}) collective-permute-start(bf16[96,1408]{1,0:T(8,128)(2,1)S(1)} %get-tuple-element.36), channel_id=1, source_target_pairs={{0,1},{1,2},{2,3},{3,4},{4,5},{5,6},{6,7},{7,0},{9,8},{10,9},{11,1... | collective-permute-start | bytes 811016 | tf_op jit(solution)/shard_map/ppermute | solution.py:431
  91.2 9.6 %collective-permute-start.20 = (bf16[48,1408]{1,0:T(8,128)(2,1)S(1)}, bf16[48,1408]{1,0:T(8,128)(2,1)S(1)}, u32[]{:S(2)}, u32[]{:S(2)}) collective-permute-start(bf16[48,1408]{1,0:T(8,128)(2,1)S(1)} %get-tuple-element.37), channel_id=1, source_target_pairs={{0,2},{1,3},{2,4},{3,5},{4,6},{5,7},{6,0},{7,1},{10,8},{11,9},{12,... | collective-permute-start | bytes 405512 | tf_op jit(solution)/shard_map/ppermute | solution.py:431
  95.0 9.8 %collective-permute-start.18 = (bf16[96,1408]{1,0:T(8,128)(2,1)}, bf16[96,1408]{1,0:T(8,128)(2,1)S(1)}, u32[]{:S(2)}, u32[]{:S(2)}) collective-permute-start(bf16[96,1408]{1,0:T(8,128)(2,1)} %get-tuple-element.34), channel_id=1, source_target_pairs={{0,1},{1,2},{2,3},{3,4},{4,5},{5,6},{6,7},{7,0},{9,8},{10,9},{11,1... | collective-permute-start | bytes 811016 | tf_op jit(solution)/shard_map/ppermute | solution.py:431
  101.4 8.6 %collective-permute-start.21 = (bf16[96,1408]{1,0:T(8,128)(2,1)S(1)}, bf16[96,1408]{1,0:T(8,128)(2,1)S(1)}, u32[]{:S(2)}, u32[]{:S(2)}) collective-permute-start(bf16[96,1408]{1,0:T(8,128)(2,1)S(1)} %shard_map.87), channel_id=1, source_target_pairs={{0,2},{1,3},{2,4},{3,5},{4,6},{5,7},{6,0},{7,1},{10,8},{11,9},{12,... | collective-permute-start | bytes 811016 | tf_op jit(solution)/shard_map/ppermute | solution.py:431
  103.5 1.3 %collective-permute-start.16 = (f32[16,1,48]{2,0,1:T(8,128)S(1)}, f32[16,1,48]{2,0,1:T(8,128)S(1)}, u32[]{:S(2)}, u32[]{:S(2)}) collective-permute-start(f32[16,1,48]{2,0,1:T(8,128)S(1)} %bitcast.11), channel_id=1, source_target_pairs={{0,8},{8,0},{1,9},{9,1},{2,10},{10,2},{3,11},{11,3},{4,12},{12,4},... | collective-permute-start | bytes 9224 | tf_op jit(solution)/shard_map/ppermute | solution.py:423
  103.6 12.4 %copy-start.2 = (f32[384]{0:T(512)}, f32[384]{0:T(512)S(1)}, u32[]{:S(2)}) copy-start(f32[384]{0:T(512)S(1)} %dynamic-slice_bitcast_fusion.refs_0_) | copy-start | bytes 4612
  104.8 11.1 %copy-start.1 = (f32[1536]{0:T(1024)}, f32[1536]{0:T(1024)S(1)}, u32[]{:S(2)}) copy-start(f32[1536]{0:T(1024)S(1)} %select_n.71.refs_1_) | copy-start | bytes 18436
  110.1 5.1 %collective-permute-start.22 = (f32[48,1408]{1,0:T(8,128)S(1)}, f32[48,1408]{1,0:T(8,128)S(1)}, u32[]{:S(2)}, u32[]{:S(2)}) collective-permute-start(f32[48,1408]{1,0:T(8,128)S(1)} %get-tuple-element.39.unread), channel_id=1, source_target_pairs={{0,8},{8,0},{1,9},{9,1},{2,10},{10,2},{3,11},{11,3},{4,12},{12,4},... | collective-permute-start | bytes 811016 | tf_op jit(solution)/shard_map/ppermute | solution.py:423
